TPU v7x, 32 devices: a whole 2x2x4 slice. The times are simulated.
32 devices in a mesh: dp: 8 (over z, y), tensor: 4 (over x, core).
Axes of the slice: x: 2, y: 2, z: 4, core: 2. Of those that a mesh axis runs over, the one named last changes fastest.
Arguments:
- text_in: bfloat16 [32, 512, 768], P('dp', 'tensor'), may hold values from -20 to 20, as said below
- layout_in: bfloat16 [32, 98304], P('dp', 'tensor'), may hold values from -20 to 20, as said below
- segment_ids: int32 [32, 512], P('dp', 'tensor'), may hold values from 0 to 3, never falling along the last dimension, each value on 1 to 256 neighbouring positions
- box_bins: int32 [32, 1024], P('dp', 'tensor'), may hold values from 0 to 1023
- text_cot: bfloat16 [32, 512, 768], P('dp', 'tensor'), may hold values from -20 to 20, as said below
- layout_cot: bfloat16 [32, 98304], P('dp', 'tensor'), may hold values from -20 to 20, as said below
- attend_text: float32 [768, 4, 768], P('dp', None, 'tensor'), as said below
- attend_text_mean: float32 [768, 4, 768], P('dp', None, 'tensor'), may hold values from -0.00024414062 to 0.00024414062
- attend_text_square: float32 [768, 4, 768], P('dp', None, 'tensor'), may hold values from 1.2939316e-10 to 5.1757265e-10
- feed_text: float32 [768, 2, 3072], P('dp', None, 'tensor'), as said below
- feed_text_mean: float32 [768, 2, 3072], P('dp', None, 'tensor'), may hold values from -0.00024414062 to 0.00024414062
- feed_text_square: float32 [768, 2, 3072], P('dp', None, 'tensor'), may hold values from 1.2939316e-10 to 5.1757265e-10
- attend_layout: float32 [192, 4, 192], P('dp', None, 'tensor'), as said below
- attend_layout_mean: float32 [192, 4, 192], P('dp', None, 'tensor'), may hold values from -0.00024414062 to 0.00024414062
- attend_layout_square: float32 [192, 4, 192], P('dp', None, 'tensor'), may hold values from 1.2939316e-10 to 5.1757265e-10
- feed_layout: float32 [192, 2, 768], P('dp', None, 'tensor'), as said below
- feed_layout_mean: float32 [192, 2, 768], P('dp', None, 'tensor'), may hold values from -0.00024414062 to 0.00024414062
- feed_layout_square: float32 [192, 2, 768], P('dp', None, 'tensor'), may hold values from 1.2939316e-10 to 5.1757265e-10
- vectors: float32 [11520], replicated, as said below
- vectors_mean: float32 [11520], replicated, may hold values from -0.00024414062 to 0.00024414062
- vectors_square: float32 [11520], replicated, may hold values from 1.2939316e-10 to 5.1757265e-10
- tables: float32 [196608], replicated, may hold values from -3 to 3
- tables_mean: float32 [196608], replicated, may hold values from -7.6293945e-06 to 7.6293945e-06
- tables_square: float32 [196608], replicated, may hold values from 1.2636051e-13 to 5.0544204e-13
Outputs:
- out_text: bfloat16 [32, 512, 768], P('dp', 'tensor')
- out_layout: bfloat16 [32, 98304], P('dp', 'tensor')
- grad_text: float32 [32, 512, 768], P('dp', 'tensor')
- grad_layout: float32 [32, 98304], P('dp', 'tensor')
- new_attend_text: float32 [768, 4, 768], P('dp', None, 'tensor')
- new_attend_text_mean: float32 [768, 4, 768], P('dp', None, 'tensor')
- new_attend_text_square: float32 [768, 4, 768], P('dp', None, 'tensor')
- new_feed_text: float32 [768, 2, 3072], P('dp', None, 'tensor')
- new_feed_text_mean: float32 [768, 2, 3072], P('dp', None, 'tensor')
- new_feed_text_square: float32 [768, 2, 3072], P('dp', None, 'tensor')
- new_attend_layout: float32 [192, 4, 192], P('dp', None, 'tensor')
- new_attend_layout_mean: float32 [192, 4, 192], P('dp', None, 'tensor')
- new_attend_layout_square: float32 [192, 4, 192], P('dp', None, 'tensor')
- new_feed_layout: float32 [192, 2, 768], P('dp', None, 'tensor')
- new_feed_layout_mean: float32 [192, 2, 768], P('dp', None, 'tensor')
- new_feed_layout_square: float32 [192, 2, 768], P('dp', None, 'tensor')
- new_vectors: float32 [11520], replicated
- new_vectors_mean: float32 [11520], replicated
- new_vectors_square: float32 [11520], replicated
- new_tables: float32 [196608], replicated
- new_tables_mean: float32 [196608], replicated
- new_tables_square: float32 [196608], replicated
- clip_norm: float32 [], replicated
Inputs may be any that keep to these rules, and one draw needn't show every extreme that they name: `text_in`: entries are independent and of order one. `layout_in`: entries are independent and of order one. `text_cot`: entries are independent and of order one. `layout_cot`: entries are independent and of order one. `attend_text`: entries are independent; the query, key, value slots have spread of order 1 / sqrt of the width, the output projection slot a larger one. `attend_layout`: entries are independent; the query, key, value slots have spread of order 1 / sqrt of the width, the output projection slot a larger one. `feed_text`: entries are independent with spread of order 1 / sqrt of the fan-in. `feed_layout`: entries are independent with spread of order 1 / sqrt of the fan-in. `vectors`: gains near one, biases of both signs.
All inputs are finite; a program needn't handle non-finite values.
Results may differ from a plain program's by a relative error of at most 0.017.
The roundings to bfloat16 on the way count: a program that leaves them out, or rounds other values in their place, can miss the bound.
Values may be sent and summed in bfloat16 or wider, within the bound.
No kernel may reach another device: no remote copies, remote signals or barrier semaphores. Data moves between devices by JAX's collectives and lax.ppermute only.
A program may use at most 128 MiB of HBM per device.

v0:
```python
import math

import jax
import jax.numpy as jnp
from jax import lax
from jax.sharding import PartitionSpec as P

HD = 64
LHD = 16
STEP = 10


NORM_EPS = 1e-05
NEG_FILL = -1000000000.0
CLIP_NORM = 1.0
LEARN_RATES = (0.3, 0.05, 0.3, 0.05, 0.3, 0.3)
BETA_ONE = 0.9
BETA_TWO = 0.999
ADAM_EPS = 1e-08
WEIGHT_DECAY = 0.01


def to_low(values):
    return values.astype(jnp.bfloat16)


def split_vectors(packed, widths, hidden):
    result = []
    offset = 0
    for stream in range(2):
        width_now = widths[stream]
        pieces = [
            packed[offset + slot_index * width_now : offset + (slot_index + 1) * width_now]
            for slot_index in range(8)
        ]
        offset = offset + 8 * width_now
        result.append((pieces, packed[offset : offset + hidden[stream]]))
        offset = offset + hidden[stream]
    return result


def norm_forward(residual, gain_vec, shift_vec):
    centered = residual - jnp.mean(residual, axis=-1, keepdims=True)
    inv_std = lax.rsqrt(jnp.mean(centered * centered, axis=-1, keepdims=True) + NORM_EPS)
    normed = centered * inv_std
    return (normed * gain_vec + shift_vec, normed, inv_std)


def norm_backward(gradient, normed, inv_std, gain_vec):
    scaled = gradient * gain_vec
    d_resid = inv_std * (
        scaled
        - jnp.mean(scaled, axis=-1, keepdims=True)
        - normed * jnp.mean(scaled * normed, axis=-1, keepdims=True)
    )
    return (d_resid, jnp.sum(gradient * normed, axis=(0, 1)), jnp.sum(gradient, axis=(0, 1)))


def gelu_exact(values):
    return jax.nn.gelu(values, approximate=False)


def gelu_backward(gate_in, gradient):
    return jax.vjp(gelu_exact, gate_in)[1](gradient)[0]


def place_slice(local_part, start, length):
    return lax.dynamic_update_slice_in_dim(jnp.zeros((length,), jnp.float32), local_part, start, 0)


def page_logits(q_text, k_text, q_lay, k_lay, segments):
    s_text = jnp.einsum("qhd,khd->hqk", q_text, k_text, preferred_element_type=jnp.float32) * (
        1.0 / math.sqrt(HD)
    )
    s_lay = jnp.einsum("qhd,khd->hqk", q_lay, k_lay, preferred_element_type=jnp.float32) * (
        1.0 / math.sqrt(LHD)
    )
    same_doc = (segments[:, None] == segments[None, :])[None]
    return jnp.where(same_doc, s_text + s_lay, NEG_FILL)


def page_forward(page_args):
    q_text, k_text, v_text, q_lay, k_lay, v_lay, segments = page_args
    logits = page_logits(q_text, k_text, q_lay, k_lay, segments)
    top_score = jnp.max(logits, axis=-1, keepdims=True)
    exponent = jnp.exp(logits - top_score)
    row_total = jnp.sum(exponent, axis=-1, keepdims=True)
    probs_low = to_low(exponent / row_total)
    ctx_text = to_low(
        jnp.einsum("hqk,khd->qhd", probs_low, v_text, preferred_element_type=jnp.float32)
    )
    ctx_lay = to_low(
        jnp.einsum("hqk,khd->qhd", probs_low, v_lay, preferred_element_type=jnp.float32)
    )
    return (ctx_text, ctx_lay, top_score + jnp.log(row_total))


def page_backward(page_args):
    q_text, k_text, v_text, q_lay, k_lay, v_lay, segments, log_total, d_ctx_text, d_ctx_lay = (
        page_args
    )
    probs_full = jnp.exp(page_logits(q_text, k_text, q_lay, k_lay, segments) - log_total)
    probs_low = to_low(probs_full)

    def softmax_back(d_context, values):
        d_probs = jnp.einsum("qhd,khd->hqk", d_context, values, preferred_element_type=jnp.float32)
        d_values = jnp.einsum(
            "hqk,qhd->khd", probs_low, d_context, preferred_element_type=jnp.float32
        )
        d_logits = probs_full * (d_probs - jnp.sum(probs_full * d_probs, axis=-1, keepdims=True))
        return (d_logits, d_values)

    dz_text, dv_text = softmax_back(d_ctx_text, v_text)
    dz_lay, dv_lay = softmax_back(d_ctx_lay, v_lay)
    ds_text = to_low(dz_text + dz_lay)
    ds_lay = to_low(dz_lay)
    scale_text = 1.0 / math.sqrt(HD)
    scale_lay = 1.0 / math.sqrt(LHD)
    dq_text = (
        jnp.einsum("hqk,khd->qhd", ds_text, k_text, preferred_element_type=jnp.float32) * scale_text
    )
    dk_text = (
        jnp.einsum("hqk,qhd->khd", ds_text, q_text, preferred_element_type=jnp.float32) * scale_text
    )
    dq_lay = (
        jnp.einsum("hqk,khd->qhd", ds_lay, k_lay, preferred_element_type=jnp.float32) * scale_lay
    )
    dk_lay = (
        jnp.einsum("hqk,qhd->khd", ds_lay, q_lay, preferred_element_type=jnp.float32) * scale_lay
    )
    return (dq_text, dk_text, dv_text, dq_lay, dk_lay, dv_lay)


def adamw_step(weight, moment, square, gradient, decay_rate, rate_now):
    new_moment = BETA_ONE * moment + (1.0 - BETA_ONE) * gradient
    new_square = BETA_TWO * square + (1.0 - BETA_TWO) * gradient * gradient
    moment_hat = new_moment / (1.0 - BETA_ONE**STEP)
    square_hat = new_square / (1.0 - BETA_TWO**STEP)
    new_weight = weight - rate_now * (
        moment_hat / (jnp.sqrt(square_hat) + ADAM_EPS) + decay_rate * weight
    )
    return (new_weight, new_moment, new_square)


def on_device(
    text_in,
    layout_in,
    segment_ids,
    box_bins,
    text_cot,
    layout_cot,
    attend_text,
    attend_text_mean,
    attend_text_square,
    feed_text,
    feed_text_mean,
    feed_text_square,
    attend_layout,
    attend_layout_mean,
    attend_layout_square,
    feed_layout,
    feed_layout_mean,
    feed_layout_square,
    vectors,
    vectors_mean,
    vectors_square,
    tables,
    tables_mean,
    tables_square,
):
    n_tensor = lax.axis_size("tensor")
    tensor_pos = lax.axis_index("tensor")
    page_count, quarter, width_text = text_in.shape
    width_lay = layout_in.shape[1] // quarter
    layout_rows_in = layout_in.reshape(page_count, quarter, width_lay)
    full_page = quarter * n_tensor
    n_rows = page_count * full_page
    own_count = page_count * quarter
    widths = [width_text, width_lay]
    head_dims = [HD, LHD]
    weights_low = (
        lax.all_gather(to_low(attend_text), "dp", axis=0, tiled=True),
        lax.all_gather(to_low(feed_text), "dp", axis=0, tiled=True),
        lax.all_gather(to_low(attend_layout), "dp", axis=0, tiled=True),
        lax.all_gather(to_low(feed_layout), "dp", axis=0, tiled=True),
    )
    attend = [weights_low[0], weights_low[2]]
    feed_mats = [weights_low[1], weights_low[3]]
    head_cols = [attend[0].shape[2], attend[1].shape[2]]
    feed_cols = [feed_mats[0].shape[2], feed_mats[1].shape[2]]
    vector_parts = split_vectors(
        vectors, widths, [feed_cols[0] * n_tensor, feed_cols[1] * n_tensor]
    )
    half_width = width_lay // 2
    table_rows = tables.reshape(-1, width_lay)
    levels = jnp.arange(table_rows.shape[0], dtype=jnp.int32)[None, :]
    flat_bins = box_bins.reshape(own_count, 2)
    hot_x = flat_bins[:, 0:1] == levels
    hot_y = flat_bins[:, 1:2] == levels
    tables_low = to_low(table_rows)
    embedded = jnp.concatenate(
        [
            jnp.dot(
                hot_x.astype(jnp.bfloat16),
                tables_low[:, :half_width],
                preferred_element_type=jnp.float32,
            ),
            jnp.dot(
                hot_y.astype(jnp.bfloat16),
                tables_low[:, half_width:],
                preferred_element_type=jnp.float32,
            ),
        ],
        axis=1,
    )
    own_rows = [
        text_in.astype(jnp.float32),
        layout_rows_in.astype(jnp.float32) + embedded.reshape(page_count, quarter, width_lay),
    ]
    gathered = (
        lax.all_gather(text_in, "tensor", axis=1, tiled=True),
        lax.all_gather(to_low(own_rows[1]), "tensor", axis=1, tiled=True),
        lax.all_gather(segment_ids, "tensor", axis=1, tiled=True),
    )
    flat_in = [gathered[0].reshape(n_rows, width_text), gathered[1].reshape(n_rows, width_lay)]
    projected = []
    for stream in range(2):
        columns = head_cols[stream]
        bias_q = lax.dynamic_slice_in_dim(vector_parts[stream][0][0], tensor_pos * columns, columns)
        bias_v = lax.dynamic_slice_in_dim(vector_parts[stream][0][1], tensor_pos * columns, columns)
        raw_proj = jnp.einsum(
            "rd,dcn->rcn",
            flat_in[stream],
            attend[stream][:, :3],
            preferred_element_type=jnp.float32,
        )
        projected.append(
            [
                to_low(raw_proj[:, 0] + bias_q),
                to_low(raw_proj[:, 1]),
                to_low(raw_proj[:, 2] + bias_v),
            ]
        )
    paged_heads = [
        [
            member.reshape(page_count, full_page, -1, head_dims[stream])
            for member in projected[stream]
        ]
        for stream in range(2)
    ]
    ctx_text, ctx_lay, log_total = lax.map(
        page_forward, tuple(paged_heads[0]) + tuple(paged_heads[1]) + (gathered[2],)
    )
    contexts = [ctx_text.reshape(n_rows, head_cols[0]), ctx_lay.reshape(n_rows, head_cols[1])]
    partials = [
        jnp.einsum(
            "rn,dn->rd", contexts[stream], attend[stream][:, 3], preferred_element_type=jnp.float32
        ).reshape(page_count, full_page, widths[stream])
        for stream in range(2)
    ]
    attended = (
        lax.psum_scatter(partials[0], "tensor", scatter_dimension=1, tiled=True),
        lax.psum_scatter(partials[1], "tensor", scatter_dimension=1, tiled=True),
    )
    first_norm = []
    for stream in range(2):
        parts_now = vector_parts[stream][0]
        first_norm.append(
            norm_forward(
                own_rows[stream] + attended[stream] + parts_now[2], parts_now[3], parts_now[4]
            )
        )
    rows_back = (
        lax.all_gather(to_low(first_norm[0][0]), "tensor", axis=1, tiled=True),
        lax.all_gather(to_low(first_norm[1][0]), "tensor", axis=1, tiled=True),
    )
    feed_rows = [rows_back[stream].reshape(n_rows, widths[stream]) for stream in range(2)]
    bias_in = [
        lax.dynamic_slice_in_dim(
            vector_parts[stream][1], tensor_pos * feed_cols[stream], feed_cols[stream]
        )
        for stream in range(2)
    ]
    gate_in = [
        jnp.einsum(
            "rd,df->rf",
            feed_rows[stream],
            feed_mats[stream][:, 0],
            preferred_element_type=jnp.float32,
        )
        + bias_in[stream]
        for stream in range(2)
    ]
    activated = [to_low(gelu_exact(gate_in[stream])) for stream in range(2)]
    feed_part = [
        jnp.einsum(
            "rf,df->rd",
            activated[stream],
            feed_mats[stream][:, 1],
            preferred_element_type=jnp.float32,
        )
        for stream in range(2)
    ]
    feed_out = (
        lax.psum_scatter(
            feed_part[0].reshape(page_count, full_page, width_text),
            "tensor",
            scatter_dimension=1,
            tiled=True,
        ),
        lax.psum_scatter(
            feed_part[1].reshape(page_count, full_page, width_lay),
            "tensor",
            scatter_dimension=1,
            tiled=True,
        ),
    )
    second_norm = []
    for stream in range(2):
        parts_now = vector_parts[stream][0]
        second_norm.append(
            norm_forward(
                first_norm[stream][0] + feed_out[stream] + parts_now[5], parts_now[6], parts_now[7]
            )
        )
    cotangents = [
        text_cot.astype(jnp.float32),
        layout_cot.reshape(page_count, quarter, width_lay).astype(jnp.float32),
    ]
    back_second = [
        norm_backward(
            cotangents[stream],
            second_norm[stream][1],
            second_norm[stream][2],
            vector_parts[stream][0][6],
        )
        for stream in range(2)
    ]
    grads_back = (
        lax.all_gather(to_low(back_second[0][0]), "tensor", axis=1, tiled=True),
        lax.all_gather(to_low(back_second[1][0]), "tensor", axis=1, tiled=True),
    )
    feed_grad_rows = [grads_back[stream].reshape(n_rows, widths[stream]) for stream in range(2)]
    feed_grads = []
    hidden_parts = []
    bias_in_grads = []
    for stream in range(2):
        down_grad = jnp.einsum(
            "rd,rf->df",
            feed_grad_rows[stream],
            activated[stream],
            preferred_element_type=jnp.float32,
        )
        d_activated = jnp.einsum(
            "rd,df->rf",
            feed_grad_rows[stream],
            feed_mats[stream][:, 1],
            preferred_element_type=jnp.float32,
        )
        d_gate = gelu_backward(gate_in[stream], d_activated)
        bias_in_grads.append(jnp.sum(d_gate, axis=0))
        d_gate_low = to_low(d_gate)
        up_grad = jnp.einsum(
            "rd,rf->df", feed_rows[stream], d_gate_low, preferred_element_type=jnp.float32
        )
        feed_grads.append(jnp.stack([up_grad, down_grad], axis=1))
        hidden_parts.append(
            jnp.einsum(
                "rf,df->rd", d_gate_low, feed_mats[stream][:, 0], preferred_element_type=jnp.float32
            )
        )
    hidden_back = (
        lax.psum_scatter(
            hidden_parts[0].reshape(page_count, full_page, width_text),
            "tensor",
            scatter_dimension=1,
            tiled=True,
        ),
        lax.psum_scatter(
            hidden_parts[1].reshape(page_count, full_page, width_lay),
            "tensor",
            scatter_dimension=1,
            tiled=True,
        ),
    )
    bias_in_full = [
        place_slice(
            bias_in_grads[stream], tensor_pos * feed_cols[stream], feed_cols[stream] * n_tensor
        )
        for stream in range(2)
    ]
    back_first = [
        norm_backward(
            hidden_back[stream] + back_second[stream][0],
            first_norm[stream][1],
            first_norm[stream][2],
            vector_parts[stream][0][3],
        )
        for stream in range(2)
    ]
    attn_grads = (
        lax.all_gather(to_low(back_first[0][0]), "tensor", axis=1, tiled=True),
        lax.all_gather(to_low(back_first[1][0]), "tensor", axis=1, tiled=True),
    )
    grad_rows = [attn_grads[stream].reshape(n_rows, widths[stream]) for stream in range(2)]
    out_proj_grads = [
        jnp.einsum(
            "rd,rn->dn", grad_rows[stream], contexts[stream], preferred_element_type=jnp.float32
        )
        for stream in range(2)
    ]
    d_context = [
        to_low(
            jnp.einsum(
                "rd,dn->rn",
                grad_rows[stream],
                attend[stream][:, 3],
                preferred_element_type=jnp.float32,
            )
        ).reshape(page_count, full_page, -1, head_dims[stream])
        for stream in range(2)
    ]
    head_grads = lax.map(
        page_backward,
        tuple(paged_heads[0])
        + tuple(paged_heads[1])
        + (gathered[2], log_total, d_context[0], d_context[1]),
    )
    attend_grads = []
    input_parts = []
    qv_bias = []
    for stream in range(2):
        pieces = [
            head_grads[3 * stream + member].reshape(n_rows, head_cols[stream])
            for member in range(3)
        ]
        qv_bias.append((jnp.sum(pieces[0], axis=0), jnp.sum(pieces[2], axis=0)))
        d_proj = jnp.stack([to_low(piece_now) for piece_now in pieces], axis=1)
        qkv_grad = jnp.einsum(
            "rd,rcn->dcn", flat_in[stream], d_proj, preferred_element_type=jnp.float32
        )
        attend_grads.append(jnp.concatenate([qkv_grad, out_proj_grads[stream][:, None]], axis=1))
        input_parts.append(
            jnp.einsum(
                "rcn,dcn->rd", d_proj, attend[stream][:, :3], preferred_element_type=jnp.float32
            ).reshape(page_count, full_page, widths[stream])
        )
    input_back = (
        lax.psum_scatter(
            input_parts[0].astype(jnp.bfloat16), "tensor", scatter_dimension=1, tiled=True
        ).astype(jnp.float32),
        lax.psum_scatter(
            input_parts[1].astype(jnp.bfloat16), "tensor", scatter_dimension=1, tiled=True
        ).astype(jnp.float32),
    )
    grad_text = input_back[0] + back_first[0][0]
    grad_layout = input_back[1] + back_first[1][0]
    flat_grad_layout = grad_layout.reshape(own_count, width_lay)
    table_grad = jnp.concatenate(
        [
            jnp.einsum(
                "rb,rl->bl",
                hot_x.astype(jnp.float32),
                flat_grad_layout[:, :half_width],
                precision=lax.Precision.HIGHEST,
            ),
            jnp.einsum(
                "rb,rl->bl",
                hot_y.astype(jnp.float32),
                flat_grad_layout[:, half_width:],
                precision=lax.Precision.HIGHEST,
            ),
        ],
        axis=1,
    ).reshape(-1)
    vector_grads = []
    for stream in range(2):
        width_now = widths[stream]
        columns = head_cols[stream]
        vector_grads.extend(
            [
                place_slice(qv_bias[stream][0], tensor_pos * columns, width_now),
                place_slice(qv_bias[stream][1], tensor_pos * columns, width_now),
                jnp.sum(back_first[stream][0], axis=(0, 1)),
                back_first[stream][1],
                back_first[stream][2],
                jnp.sum(back_second[stream][0], axis=(0, 1)),
                back_second[stream][1],
                back_second[stream][2],
                bias_in_full[stream],
            ]
        )
    vector_grad = jnp.concatenate(vector_grads)
    weight_grads = (
        lax.psum_scatter(attend_grads[0], "dp", scatter_dimension=0, tiled=True),
        lax.psum_scatter(feed_grads[0], "dp", scatter_dimension=0, tiled=True),
        lax.psum_scatter(attend_grads[1], "dp", scatter_dimension=0, tiled=True),
        lax.psum_scatter(feed_grads[1], "dp", scatter_dimension=0, tiled=True),
    )
    small_grads = lax.psum((vector_grad, table_grad), ("dp", "tensor"))
    local_sq = sum((jnp.sum(member_grad * member_grad) for member_grad in weight_grads))
    shared_sq = lax.psum(local_sq, ("dp", "tensor"))
    clip_norm = jnp.sqrt(
        shared_sq
        + jnp.sum(small_grads[0] * small_grads[0])
        + jnp.sum(small_grads[1] * small_grads[1])
    )
    factor = jnp.minimum(1.0, CLIP_NORM / (clip_norm + 1e-06))
    states = [
        (attend_text, attend_text_mean, attend_text_square, weight_grads[0], WEIGHT_DECAY),
        (feed_text, feed_text_mean, feed_text_square, weight_grads[1], WEIGHT_DECAY),
        (attend_layout, attend_layout_mean, attend_layout_square, weight_grads[2], WEIGHT_DECAY),
        (feed_layout, feed_layout_mean, feed_layout_square, weight_grads[3], WEIGHT_DECAY),
        (vectors, vectors_mean, vectors_square, small_grads[0], 0.0),
        (tables, tables_mean, tables_square, small_grads[1], 0.0),
    ]
    updated = [
        adamw_step(
            states[which_param][0],
            states[which_param][1],
            states[which_param][2],
            states[which_param][3] * factor,
            states[which_param][4],
            LEARN_RATES[which_param],
        )
        for which_param in range(6)
    ]
    return (
        second_norm[0][0].astype(jnp.bfloat16),
        second_norm[1][0].astype(jnp.bfloat16).reshape(page_count, quarter * width_lay),
        grad_text,
        grad_layout.reshape(page_count, quarter * width_lay),
        updated[0][0],
        updated[0][1],
        updated[0][2],
        updated[1][0],
        updated[1][1],
        updated[1][2],
        updated[2][0],
        updated[2][1],
        updated[2][2],
        updated[3][0],
        updated[3][1],
        updated[3][2],
        updated[4][0],
        updated[4][1],
        updated[4][2],
        updated[5][0],
        updated[5][1],
        updated[5][2],
        clip_norm,
    )


def solution(mesh):
    in_specs = (
        P("dp", "tensor", None),
        P("dp", "tensor"),
        P("dp", "tensor"),
        P("dp", "tensor"),
        P("dp", "tensor", None),
        P("dp", "tensor"),
        P("dp", None, "tensor"),
        P("dp", None, "tensor"),
        P("dp", None, "tensor"),
        P("dp", None, "tensor"),
        P("dp", None, "tensor"),
        P("dp", None, "tensor"),
        P("dp", None, "tensor"),
        P("dp", None, "tensor"),
        P("dp", None, "tensor"),
        P("dp", None, "tensor"),
        P("dp", None, "tensor"),
        P("dp", None, "tensor"),
        P(),
        P(),
        P(),
        P(),
        P(),
        P(),
    )
    out_specs = (
        P("dp", "tensor", None),
        P("dp", "tensor"),
        P("dp", "tensor", None),
        P("dp", "tensor"),
        P("dp", None, "tensor"),
        P("dp", None, "tensor"),
        P("dp", None, "tensor"),
        P("dp", None, "tensor"),
        P("dp", None, "tensor"),
        P("dp", None, "tensor"),
        P("dp", None, "tensor"),
        P("dp", None, "tensor"),
        P("dp", None, "tensor"),
        P("dp", None, "tensor"),
        P("dp", None, "tensor"),
        P("dp", None, "tensor"),
        P(),
        P(),
        P(),
        P(),
        P(),
        P(),
        P(),
    )
    return jax.shard_map(
        on_device, mesh=mesh, in_specs=in_specs, out_specs=out_specs, check_vma=False
    )
```

profile of v0, /device:TPU:0, one launch (start us, length us, event | category | flops | bytes accessed | tf_op | source)
XLA Modules:
  0.0 1118.3 jit_solution(15312431527509082593)
XLA Ops:
  15.6 32.8 %all_gather.43 = bf16[192,4,48]{2,1,0:T(4,128)(2,1)S(1)} all-gather(bf16[24,4,48]{2,1,0:T(4,128)(2,1)S(1)} %convert_element_type.244), channel_id=1, replica_groups=mesh['dp'=8,'tensor'=4] {'dp'}, dimensions={0}, use_global_device_ids=true | all-gather | bytes 82944 | tf_op jit(solution)/shard_map/all_gather | solution.py:184
  52.0 8.6 all_gather.42
  73.9 13.2 %all-gather.7.cloned.1.call-done = bf16[4,512,768]{2,1,0:T(8,128)(2,1)} async-done(((bf16[4,128,768]{2,1,0:T(8,128)(2,1)}), bf16[4,512,768]{2,1,0:T(8,128)(2,1)}) %all-gather.7.cloned.1.call-update) | async-done | bytes 3145744 | tf_op jit(solution)/shard_map/all_gather | solution.py:221
  102.1 22.8 %while.34 = (s32[]{:T(128)}, bf16[4,512,3,64]{1,3,2,0:T(8,128)(2,1)}, bf16[4,512,3,16]{1,3,2,0:T(8,128)(2,1)S(1)}, f32[4,3,512,1]{2,1,3,0:T(4,128)}, bf16[4,512,...) while((s32[]{:T(128)}, ...), condition=%wide.region_3.4_spmd, body=%wide.region_0.3_spmd.sunk | while | flops 259906048 | bytes 22016132 | solution.py:251
  132.3 56.7 %reduce-scatter.16.cloned.1.call-done = f32[4,128,768]{2,1,0:T(8,128)} async-done(((f32[4,512,768]{2,1,0:T(8,128)}), f32[4,128,768]{2,1,0:T(8,128)}) %reduce-scatter.16.cloned.1.call-update) | async-done | bytes 1572880 | tf_op jit(solution)/shard_map/reduce_scatter | solution.py:262
  192.4 51.6 %all-gather.13.cloned.1.call-done = bf16[768,2,768]{2,0,1:T(8,128)(2,1)} async-done(((bf16[96,2,768]{2,0,1:T(8,128)(2,1)}), bf16[768,2,768]{2,0,1:T(8,128)(2,1)}) %all-gather.13.cloned.1.call-update) | async-done | bytes 2359312 | tf_op jit(solution)/shard_map/all_gather | solution.py:183
  243.9 29.2 %all-gather.11.cloned.1.call-done = bf16[4,512,768]{2,1,0:T(8,128)(2,1)} async-done(((bf16[4,128,768]{2,1,0:T(8,128)(2,1)}), bf16[4,512,768]{2,1,0:T(8,128)(2,1)}) %all-gather.11.cloned.1.call-update) | async-done | bytes 3145744 | tf_op jit(solution)/shard_map/all_gather | solution.py:274
  273.1 19.1 %multiply_convert_fusion = (bf16[2048,768]{1,0:T(8,128)(2,1)S(1)}, f32[2048,768]{1,0:T(8,128)}, f32[2048,768]{1,0:T(8,128)}) fusion(f32[768]{0:T(1024)S(1)} %dynamic_slice.77, bf16[2048,768]{1,0:T(8,128)(2,1)} %bitcast.434, bf16[768,2,768]{2,0,1:T(8,128)(2,1)} %all-gather.13.cloned.1.call-done), kind=kOutput, calls=%fused_computation.110 | convolution fusion | flops 2519728128 | bytes 20057088 | tf_op jit(solution)/shard_map/rd,df->rf/dot_general | solution.py:285
  301.1 55.7 %reduce-scatter.18.cloned.1.call-done = f32[4,128,768]{2,1,0:T(8,128)} async-done(((f32[4,512,768]{2,1,0:T(8,128)}), f32[4,128,768]{2,1,0:T(8,128)}) %reduce-scatter.18.cloned.1.call-update) | async-done | bytes 1572880 | tf_op jit(solution)/shard_map/reduce_scatter | solution.py:305
  363.4 32.7 %all_gather.47 = bf16[192,2,192]{2,0,1:T(8,128)(2,1)} all-gather(bf16[24,2,192]{2,0,1:T(8,128)(2,1)S(1)} %copy.321), channel_id=1, replica_groups=mesh['dp'=8,'tensor'=4] {'dp'}, dimensions={0}, use_global_device_ids=true | all-gather | bytes 165888 | tf_op jit(solution)/shard_map/all_gather | solution.py:185
  398.5 12.8 %all_gather.46 = bf16[4,512,192]{1,2,0:T(8,128)(2,1)S(1)} all-gather(bf16[4,128,192]{1,2,0:T(8,128)(2,1)S(1)} %fusion.161), channel_id=1, replica_groups=mesh['dp'=8,'tensor'=4] {'tensor'}, dimensions={1}, use_global_device_ids=true | all-gather | bytes 983040 | tf_op jit(solution)/shard_map/all_gather | solution.py:275
  423.2 11.1 fusion.210
  444.5 9.6 reduce-scatter.22.cloned.1.call-done
  459.9 8.2 all_gather.50
  472.4 42.6 %reduce-scatter.24.cloned.1.call-done = f32[4,128,768]{2,1,0:T(8,128)} async-done(((f32[4,512,768]{2,1,0:T(8,128)}), f32[4,128,768]{2,1,0:T(8,128)}) %reduce-scatter.24.cloned.1.call-update) | async-done | bytes 1572880 | tf_op jit(solution)/shard_map/reduce_scatter | solution.py:373
  526.1 19.7 %reduce-scatter.26.cloned.1.call-done = f32[4,128,192]{1,2,0:T(8,128)} async-done(((f32[4,512,192]{1,2,0:T(8,128)}), f32[4,128,192]{1,2,0:T(8,128)}) %reduce-scatter.26.cloned.1.call-update) | async-done | bytes 393232 | tf_op jit(solution)/shard_map/reduce_scatter | solution.py:379
  548.5 8.7 all_gather.51
  569.6 6.3 all-gather.17.cloned.1.call-done
  580.0 119.8 %while.35 = (s32[]{:T(128)}, f32[4,512,3,64]{1,3,2,0:T(8,128)}, bf16[4,512,3,64]{1,3,2,0:T(8,128)(2,1)}, f32[4,512,3,64]{1,3,2,0:T(8,128)}, f32[4,512,3,16]{1,3,...) while((s32[]{:T(128)}, f32[4,512,3,64]{1,3,2,0:T(8,128)}, ...), condition=%wide.region_29.30_spmd, body=%wide.region_26.29_spmd.sunk | while | flops 650103296 | bytes 93438352 | solution.py:423
  746.6 18.0 %reduce-scatter.34.cloned.1.call-done = bf16[128,768]{1,0:T(8,128)(2,1)} async-done(((bf16[512,768]{1,0:T(8,128)(2,1)}), bf16[128,768]{1,0:T(8,128)(2,1)}) %reduce-scatter.34.cloned.1.call-update) | async-done | bytes 196624
  777.0 63.1 %all-reduce.7.cloned.1.call-done = f32[192,4,48]{2,1,0:T(4,128)} async-done(((f32[192,4,48]{2,1,0:T(4,128)}), f32[192,4,48]{2,1,0:T(4,128)}) %all-reduce.7.cloned.1.call-update) | async-done | bytes 147472
  842.8 68.7 %reduce-scatter.36.cloned.1.call-done = f32[96,768]{1,0:T(8,128)} async-done(((f32[768,768]{1,0:T(8,128)}), f32[96,768]{1,0:T(8,128)}) %reduce-scatter.36.cloned.1.call-update) | async-done | bytes 294928
  915.9 129.2 %all-reduce.5.cloned.1.call-done = f32[196608]{0:T(1024)} async-done(((f32[196608]{0:T(1024)}), f32[196608]{0:T(1024)}) %all-reduce.5.cloned.1.call-update) | async-done | bytes 786448 | tf_op jit(solution)/shard_map/psum | solution.py:500
  1047.1 40.1 %all-reduce.1 = (f32[]{:T(128)}, f32[11520]{0:T(1024)S(1)}) all-reduce(f32[]{:T(128)S(6)} %add.419, f32[11520]{0:T(1024)S(1)} %concatenate.18), channel_id=1, replica_groups=mesh['dp'=8,'tensor'=4] {'dp','tensor'}, use_global_device_ids=true, to_apply=%region_40.41 | all-reduce | flops 11521 | bytes 92168 | tf_op jit(solution)/shard_map/psum | solution.py:502
  (663 shorter events, 357.3 us)
Async XLA Ops:
  7.2 61.2 %all-gather.9.cloned.1.call-start = ((), (), s32[]{:S(2)}) async-start(), calls=%async_computation.12 | async-start | bytes 1769472 | tf_op jit(solution)/shard_map/all_gather | solution.py:182
  9.1 78.0 %all-gather.7.cloned.1.call-start = ((), (), s32[]{:S(2)}) async-start(), calls=%async_computation.11 | async-start | bytes 3932160 | tf_op jit(solution)/shard_map/all_gather | solution.py:221
  9.9 179.1 %reduce-scatter.16.cloned.1.call-start = ((), (), s32[]{:S(2)}) async-start(), calls=%async_computation.13 | async-start | bytes 7864320 | tf_op jit(solution)/shard_map/reduce_scatter | solution.py:262
  124.9 174.5 %copy-start.57 = (bf16[4,512,3,16]{1,3,2,0:T(8,128)(2,1)}, bf16[4,512,3,16]{1,3,2,0:T(8,128)(2,1)S(1)}, u32[]{:S(2)}) copy-start(bf16[4,512,3,16]{1,3,2,0:T(8,128)(2,1)S(1)} %get-tuple-element.175) | copy-start | bytes 589828
  130.4 113.5 %all-gather.13.cloned.1.call-start = ((), (), s32[]{:S(2)}) async-start(), calls=%async_computation.15 | async-start | bytes 2654208 | tf_op jit(solution)/shard_map/all_gather | solution.py:183
  132.2 140.9 %all-gather.11.cloned.1.call-start = ((), (), s32[]{:S(2)}) async-start(), calls=%async_computation.14 | async-start | bytes 3932160 | tf_op jit(solution)/shard_map/all_gather | solution.py:274
  190.7 166.2 %copy-start.79 = (f32[4,128]{1,0:T(4,128)}, f32[4,128]{1,0:T(4,128)S(1)}, u32[]{:S(2)}) copy-start(f32[4,128]{1,0:T(4,128)S(1)} %broadcast_multiply_fusion.11) | copy-start | bytes 6148
  191.0 165.9 %copy-start.84 = (f32[4,128]{1,0:T(4,128)}, f32[4,128]{1,0:T(4,128)S(1)}, u32[]{:S(2)}) copy-start(f32[4,128]{1,0:T(4,128)S(1)} %add_rsqrt_fusion.3) | copy-start | bytes 6148
  192.2 164.6 %reduce-scatter.18.cloned.1.call-start = ((), (), s32[]{:S(2)}) async-start(), calls=%async_computation.16 | async-start | bytes 7864320 | tf_op jit(solution)/shard_map/reduce_scatter | solution.py:305
  298.3 97.8 %reduce-scatter.20.cloned.1.call-start = ((), (), s32[]{:S(2)}) async-start(), calls=%async_computation.17 | async-start | bytes 1966080 | tf_op jit(solution)/shard_map/reduce_scatter | solution.py:263
  301.1 122.1 %all-gather.15.cloned.1.call-start = ((), (), s32[]{:S(2)}) async-start(), calls=%async_computation.19 | async-start | bytes 3932160 | tf_op jit(solution)/shard_map/all_gather | solution.py:340
  362.0 92.1 %reduce-scatter.22.cloned.1.call-start = ((), (), s32[]{:S(2)}) async-start(), calls=%async_computation.18 | async-start | bytes 1966080 | tf_op jit(solution)/shard_map/reduce_scatter | solution.py:311
  418.8 96.1 %reduce-scatter.24.cloned.1.call-start = ((), (), s32[]{:S(2)}) async-start(), calls=%async_computation.20 | async-start | bytes 7864320 | tf_op jit(solution)/shard_map/reduce_scatter | solution.py:373
  440.5 105.3 %reduce-scatter.26.cloned.1.call-start = ((), (), s32[]{:S(2)}) async-start(), calls=%async_computation.22 | async-start | bytes 1966080 | tf_op jit(solution)/shard_map/reduce_scatter | solution.py:379
  472.3 103.5 %all-gather.17.cloned.1.call-start = ((), (), s32[]{:S(2)}) async-start(), calls=%async_computation.21 | async-start | bytes 3932160 | tf_op jit(solution)/shard_map/all_gather | solution.py:402
  522.5 219.5 %reduce-scatter.32.cloned.1.call-start = ((), (), s32[]{:S(2)}) async-start(), calls=%async_computation.25 | async-start | bytes 442368 | tf_op jit(solution)/shard_map/reduce_scatter | solution.py:498
  526.1 217.6 %reduce-scatter.30.cloned.1.call-start = ((), (), s32[]{:S(2)}) async-start(), calls=%async_computation.24 | async-start | bytes 5308416 | tf_op jit(solution)/shard_map/reduce_scatter | solution.py:496
  569.5 195.1 %reduce-scatter.34.cloned.1.call-start = ((), (), s32[]{:S(2)}) async-start(), calls=%async_computation.27 | async-start | bytes 983040
  706.4 133.7 %all-reduce.7.cloned.1.call-start = ((), (), s32[]{:S(2)}) async-start(), calls=%async_computation.29 | async-start | bytes 786432
  727.3 184.2 %reduce-scatter.36.cloned.1.call-start = ((), (), s32[]{:S(2)}) async-start(), calls=%async_computation.28 | async-start | bytes 2654208
  737.4 307.8 %all-reduce.5.cloned.1.call-start = ((), (), s32[]{:S(2)}) async-start(), calls=%async_computation.26 | async-start | bytes 1572864 | tf_op jit(solution)/shard_map/psum | solution.py:500
  769.9 337.8 %reduce-scatter.28.cloned.1.call-start = ((), (), s32[]{:S(2)}) async-start(), calls=%async_computation.23 | async-start | bytes 3932160 | tf_op jit(solution)/shard_map/reduce_scatter | solution.py:449
  915.9 175.1 %copy-start.43 = (f32[96,2,768]{2,1,0:T(2,128)S(1)}, f32[96,2,768]{2,1,0:T(2,128)}, u32[]{:S(2)}) copy-start(f32[96,2,768]{2,1,0:T(2,128)} %param.37) | copy-start | bytes 1769476
  915.9 175.1 %copy-start.44 = (f32[96,2,768]{2,0,1:T(8,128)S(1)}, f32[96,2,768]{2,0,1:T(8,128)}, u32[]{:S(2)}) copy-start(f32[96,2,768]{2,0,1:T(8,128)} %reduce-scatter.30.cloned.1.call-done) | copy-start | bytes 1769476
  (149 other events, 1102.2 us)
Sparse Core Ops, SparseCore 0:
  10.8 47.1 all-gather.8
  59.5 27.5 all-gather.6
  130.5 58.3 reduce-scatter.15
  191.8 52.0 all-gather.12
  246.0 27.0 all-gather.10
  298.5 58.3 reduce-scatter.17
  359.9 28.1 reduce-scatter.19
  390.4 32.7 all-gather.14
  425.9 28.1 reduce-scatter.21
  456.5 58.4 reduce-scatter.23
  517.7 28.1 reduce-scatter.25
  547.3 28.5 all-gather.16
  579.7 61.3 reduce-scatter.31
  644.6 94.5 reduce-scatter.29
  741.5 23.0 reduce-scatter.33
  768.8 71.2 all-reduce.6
  843.4 68.0 reduce-scatter.35
  917.1 128.0 all-reduce.4
  1047.9 37.0 reduce-scatter.27
where the time goes:
time: 1130 us; the launch traced here: 1120 us
  waiting for transfers between devices  569 us (50%)
  matrix products  212 us (19%)
  blocking collectives  149 us (13%)
  local copies, waits for them, and re-layouts  90.4 us (8%)
  other arithmetic  73.9 us (7%)
  between operations  22.7 us (2%)
    unnamed x22, waiting for transfers between devices  151 us
    psum x1, waiting for transfers between devices, on_device(): small_grads = lax.psum((vector_grad, table_grad), ('dp', 'tensor'))  129 us
    reduce_scatter x1, waiting for transfers between devices, on_device(): lax.psum_scatter(partials[0], 'tensor', scatter_dimension=1, tiled=True)  56.7 us
    reduce_scatter x1, waiting for transfers between devices, on_device(): lax.psum_scatter(feed_part[0].reshape(page_count, full_page, width_text),...  55.7 us
    all_gather x1, waiting for transfers between devices, on_device(): lax.all_gather(to_low(feed_text), 'dp', axis=0, tiled=True)  51.6 us
    unnamed x281, local copies, waits for them, and re-layouts  43.4 us
    reduce_scatter x1, waiting for transfers between devices, on_device(): lax.psum_scatter(hidden_parts[0].reshape(page_count, full_page, width_tex...  42.6 us
    psum x1, blocking collectives, on_device(): shared_sq = lax.psum(local_sq, ('dp', 'tensor'))  40.1 us
  transfers between devices with their start and end apart: 19, of which 14 were waited for; matrix products, arithmetic and copies ran while one was open for 26% of the time, Pallas kernels for 0%

commit v1 on v0

v1 whole, which is shorter than its diff:
```python
import functools
import math

import jax
import jax.numpy as jnp
from jax import lax
from jax.experimental import pallas as pl
from jax.experimental.pallas import tpu as pltpu
from jax.sharding import PartitionSpec as P

HD = 64
LHD = 16
STEP = 10

NORM_EPS = 1e-05
NEG_FILL = -1000000000.0
CLIP_NORM = 1.0
LEARN_RATES = (0.3, 0.05, 0.3, 0.05, 0.3, 0.3)
BETA_ONE = 0.9
BETA_TWO = 0.999
ADAM_EPS = 1e-08
WEIGHT_DECAY = 0.01
AXES = ("dp", "tensor")
LAY_ROWS = 32
F32 = jnp.float32
BF16 = jnp.bfloat16


def to_low(values):
    return values.astype(BF16)


def xor_send(values, total, distance):
    return lax.ppermute(values, AXES, [(i, i ^ distance) for i in range(total)])


def split_vectors(packed, widths, hidden):
    result = []
    offset = 0
    for stream in range(2):
        width_now = widths[stream]
        pieces = [packed[offset + k * width_now : offset + (k + 1) * width_now] for k in range(8)]
        offset = offset + 8 * width_now
        result.append((pieces, packed[offset : offset + hidden[stream]]))
        offset = offset + hidden[stream]
    return result


def norm_forward(residual, gain_vec, shift_vec):
    centered = residual - jnp.mean(residual, axis=-1, keepdims=True)
    inv_std = lax.rsqrt(jnp.mean(centered * centered, axis=-1, keepdims=True) + NORM_EPS)
    normed = centered * inv_std
    return (normed * gain_vec + shift_vec, normed, inv_std)


def norm_backward(gradient, normed, inv_std, gain_vec):
    scaled = gradient * gain_vec
    d_resid = inv_std * (
        scaled
        - jnp.mean(scaled, axis=-1, keepdims=True)
        - normed * jnp.mean(scaled * normed, axis=-1, keepdims=True)
    )
    return (d_resid, jnp.sum(gradient * normed, axis=0), jnp.sum(gradient, axis=0))


def gelu_exact(values):
    return jax.nn.gelu(values, approximate=False)


def gelu_backward(gate_in, gradient):
    return jax.vjp(gelu_exact, gate_in)[1](gradient)[0]


def page_logits(q_text, k_text, q_lay, k_lay, segments):
    s_text = jnp.einsum("qhd,khd->hqk", q_text, k_text, preferred_element_type=F32) * (
        1.0 / math.sqrt(HD)
    )
    s_lay = jnp.einsum("qhd,khd->hqk", q_lay, k_lay, preferred_element_type=F32) * (
        1.0 / math.sqrt(LHD)
    )
    same_doc = (segments[:, None] == segments[None, :])[None]
    return jnp.where(same_doc, s_text + s_lay, NEG_FILL)


def page_forward(q_text, k_text, v_text, q_lay, k_lay, v_lay, segments):
    logits = page_logits(q_text, k_text, q_lay, k_lay, segments)
    top_score = jnp.max(logits, axis=-1, keepdims=True)
    exponent = jnp.exp(logits - top_score)
    row_total = jnp.sum(exponent, axis=-1, keepdims=True)
    probs_low = to_low(exponent / row_total)
    ctx_text = to_low(jnp.einsum("hqk,khd->qhd", probs_low, v_text, preferred_element_type=F32))
    ctx_lay = to_low(jnp.einsum("hqk,khd->qhd", probs_low, v_lay, preferred_element_type=F32))
    return (ctx_text, ctx_lay, top_score + jnp.log(row_total))


def page_backward(
    q_text, k_text, v_text, q_lay, k_lay, v_lay, segments, log_total, d_ctx_text, d_ctx_lay
):
    probs_full = jnp.exp(page_logits(q_text, k_text, q_lay, k_lay, segments) - log_total)
    probs_low = to_low(probs_full)

    def softmax_back(d_context, values):
        d_probs = jnp.einsum("qhd,khd->hqk", d_context, values, preferred_element_type=F32)
        d_values = jnp.einsum("hqk,qhd->khd", probs_low, d_context, preferred_element_type=F32)
        d_logits = probs_full * (d_probs - jnp.sum(probs_full * d_probs, axis=-1, keepdims=True))
        return (d_logits, d_values)

    dz_text, dv_text = softmax_back(d_ctx_text, v_text)
    dz_lay, dv_lay = softmax_back(d_ctx_lay, v_lay)
    ds_text = to_low(dz_text + dz_lay)
    ds_lay = to_low(dz_lay)
    scale_text = 1.0 / math.sqrt(HD)
    scale_lay = 1.0 / math.sqrt(LHD)
    dq_text = jnp.einsum("hqk,khd->qhd", ds_text, k_text, preferred_element_type=F32) * scale_text
    dk_text = jnp.einsum("hqk,qhd->khd", ds_text, q_text, preferred_element_type=F32) * scale_text
    dq_lay = jnp.einsum("hqk,khd->qhd", ds_lay, k_lay, preferred_element_type=F32) * scale_lay
    dk_lay = jnp.einsum("hqk,qhd->khd", ds_lay, q_lay, preferred_element_type=F32) * scale_lay
    return (dq_text, dk_text, dv_text, dq_lay, dk_lay, dv_lay)


def adamw_step(weight, moment, square, gradient, decay_rate, rate_now):
    new_moment = BETA_ONE * moment + (1.0 - BETA_ONE) * gradient
    new_square = BETA_TWO * square + (1.0 - BETA_TWO) * gradient * gradient
    moment_hat = new_moment / (1.0 - BETA_ONE**STEP)
    square_hat = new_square / (1.0 - BETA_TWO**STEP)
    new_weight = weight - rate_now * (
        moment_hat / (jnp.sqrt(square_hat) + ADAM_EPS) + decay_rate * weight
    )
    return (new_weight, new_moment, new_square)


def reorder(blocks, own_index):
    def body(own_ref, in_ref, out_ref):
        out_ref[...] = in_ref[...]

    count, rows, cols = blocks.shape
    return pl.pallas_call(
        body,
        grid_spec=pltpu.PrefetchScalarGridSpec(
            num_scalar_prefetch=1,
            grid=(count,),
            in_specs=[pl.BlockSpec((1, rows, cols), lambda i, own: (i, 0, 0))],
            out_specs=pl.BlockSpec((1, rows, cols), lambda i, own: (i ^ own[0], 0, 0)),
        ),
        out_shape=jax.ShapeDtypeStruct(blocks.shape, blocks.dtype),
    )(own_index, blocks)


def gather_shards(shard, total):
    far = total // 8
    rows, cols = shard.shape
    half = rows // 2
    stacked = jnp.stack([shard] + [xor_send(shard, total, 8 * r) for r in range(1, far)])

    def two_more(part, first, second):
        part = jnp.stack([part, xor_send(part, total, first)])
        return jnp.stack([part, xor_send(part, total, second)])

    low_half = two_more(stacked[:, :half], 2, 4)
    high_half = two_more(stacked[:, half:], 4, 2)
    both = (low_half, xor_send(low_half, total, 1), high_half, xor_send(high_half, total, 1))
    low_all = jnp.stack([both[0], both[1]])
    high_all = jnp.stack([both[2], both[3]])
    low_all = low_all.transpose(3, 1, 2, 0, 4, 5).reshape(total, half, cols)
    high_all = high_all.transpose(3, 2, 1, 0, 4, 5).reshape(total, rows - half, cols)
    return jnp.concatenate([low_all, high_all], axis=1)


def reduce_shards(blocks, total):
    far = total // 8
    rows, cols = blocks.shape[1:]
    half = rows // 2
    parts = blocks.reshape(far, 2, 2, 2, rows, cols)

    def add(mine, theirs):
        return to_low(mine.astype(F32) + theirs.astype(F32))

    chip = add(parts[:, :, :, 0], xor_send(parts[:, :, :, 1], total, 1))
    low, high = chip[..., :half, :], chip[..., half:, :]
    low = add(low[:, :, 0], xor_send(low[:, :, 1], total, 2))
    high = add(high[:, 0], xor_send(high[:, 1], total, 4))
    low = add(low[:, 0], xor_send(low[:, 1], total, 4))
    high = add(high[:, 0], xor_send(high[:, 1], total, 2))
    line = jnp.concatenate([low, high], axis=1)
    out = line[0].astype(F32)
    for r in range(1, far):
        out = out + xor_send(line[r], total, 8 * r).astype(F32)
    return out


def sum_everywhere(values, total):
    distance = 1
    while distance < total:
        values = values + xor_send(values, total, distance)
        distance = distance * 2
    return values


def reduce_small(values, total):
    me = lax.axis_index("dp") * lax.axis_size("tensor") + lax.axis_index("tensor")
    distance = 1
    sizes = []
    while distance < total:
        half = values.shape[0] // 2
        bit = (me // distance) % 2
        mine = lax.dynamic_slice_in_dim(values, bit * half, half)
        other = lax.dynamic_slice_in_dim(values, (1 - bit) * half, half)
        values = mine + xor_send(to_low(other), total, distance).astype(F32)
        sizes.append(distance)
        distance = distance * 2
    square_sum = jnp.sum(values * values)
    for distance in reversed(sizes):
        bit = (me // distance) % 2
        other = xor_send(values, total, distance)
        values = jnp.where(
            bit == 0, jnp.concatenate([values, other]), jnp.concatenate([other, values])
        )
    return values, square_sum


def on_device(
    text_in,
    layout_in,
    segment_ids,
    box_bins,
    text_cot,
    layout_cot,
    attend_text,
    attend_text_mean,
    attend_text_square,
    feed_text,
    feed_text_mean,
    feed_text_square,
    attend_layout,
    attend_layout_mean,
    attend_layout_square,
    feed_layout,
    feed_layout_mean,
    feed_layout_square,
    vectors,
    vectors_mean,
    vectors_square,
    tables,
    tables_mean,
    tables_square,
):
    n_dp, n_t = lax.axis_size("dp"), lax.axis_size("tensor")
    total = n_dp * n_t
    t_pos = lax.axis_index("tensor")
    me = lax.axis_index("dp") * n_t + t_pos
    me_arr = me.astype(jnp.int32).reshape(1)
    pages, quarter, wt = text_in.shape
    wl = layout_in.shape[1] // quarter
    rows = quarter * n_t
    widths = [wt, wl]
    head_dims = [HD, LHD]
    d_own, dl_own = attend_text.shape[0], attend_layout.shape[0]
    ct, cl = attend_text.shape[2], attend_layout.shape[2]
    ht, hl = feed_text.shape[2], feed_layout.shape[2]

    def page_of(values):
        take = lambda r: lax.dynamic_index_in_dim(values, t_pos ^ r, 0, keepdims=False)
        return jnp.concatenate([take(0)] + [xor_send(take(r), total, r) for r in range(1, n_t)])

    def pages_of(page):
        blocks = page.reshape(n_t, quarter, page.shape[-1])
        parts = [blocks[0]] + [xor_send(blocks[r], total, r) for r in range(1, n_t)]
        out = jnp.zeros((n_t,) + parts[0].shape, parts[0].dtype)
        for r in range(n_t):
            out = lax.dynamic_update_slice(out, parts[r][None], (t_pos ^ r, 0, 0))
        return out

    lay_pack = jnp.concatenate(
        [
            to_low(attend_layout).reshape(dl_own, 4 * cl),
            to_low(feed_layout).reshape(dl_own, 2 * hl),
        ],
        axis=1,
    )
    lay_cols = lay_pack.shape[1]
    lay_pack = jnp.pad(lay_pack, ((0, LAY_ROWS - dl_own), (0, 4 * ct - lay_cols)))
    attend_pack = jnp.concatenate([to_low(attend_text).reshape(d_own, 4 * ct), lay_pack])
    feed_pack = to_low(feed_text).transpose(1, 0, 2).reshape(2 * d_own, ht)
    attend_all = reorder(gather_shards(attend_pack, total), me_arr)
    feed_all = reorder(gather_shards(feed_pack, total), me_arr)
    attend_all = attend_all.reshape(n_dp, n_t, d_own + LAY_ROWS, 4 * ct)
    w_text = attend_all[:, :, :d_own].reshape(n_dp, n_t, d_own, 4, ct)
    w_text = w_text.transpose(0, 2, 3, 1, 4).reshape(wt, 4, n_t * ct)
    w_lay = attend_all[:, :, d_own : d_own + dl_own, : 4 * cl].reshape(n_dp, n_t, dl_own, 4, cl)
    w_lay = w_lay.transpose(0, 2, 3, 1, 4).reshape(wl, 4, n_t * cl)
    f_lay = attend_all[:, :, d_own : d_own + dl_own, 4 * cl : lay_cols]
    f_lay = f_lay.reshape(n_dp, n_t, dl_own, 2, hl).transpose(0, 2, 3, 1, 4)
    f_lay = f_lay.reshape(wl, 2, n_t * hl)
    f_text = feed_all.reshape(n_dp, n_t, 2, d_own, ht).transpose(0, 3, 2, 1, 4)
    f_text = f_text.reshape(wt, 2, n_t * ht)
    attend = [w_text, w_lay]
    feeds = [f_text, f_lay]

    text_page = page_of(text_in)
    lay_page = page_of(layout_in.reshape(pages, quarter, wl))
    ints = page_of(
        jnp.concatenate([segment_ids[:, :, None], box_bins.reshape(pages, quarter, 2)], axis=2)
    )
    segments, bins = ints[:, 0], ints[:, 1:]
    cots = [page_of(text_cot), page_of(layout_cot.reshape(pages, quarter, wl))]

    parts = split_vectors(vectors, widths, [n_t * ht, n_t * hl])
    half_width = wl // 2
    table_rows = to_low(tables.reshape(-1, wl))
    levels = jnp.arange(table_rows.shape[0], dtype=jnp.int32)[None, :]
    hots = [(bins[:, k : k + 1] == levels).astype(BF16) for k in range(2)]
    embedded = jnp.concatenate(
        [
            jnp.dot(hots[0], table_rows[:, :half_width], preferred_element_type=F32),
            jnp.dot(hots[1], table_rows[:, half_width:], preferred_element_type=F32),
        ],
        axis=1,
    )
    own_rows = [text_page.astype(F32), lay_page.astype(F32) + embedded]
    rows_low = [text_page, to_low(own_rows[1])]
    qkv = []
    for s in range(2):
        raw = jnp.einsum("rd,dcn->rcn", rows_low[s], attend[s][:, :3], preferred_element_type=F32)
        qkv.append(
            [
                to_low(member).reshape(rows, -1, head_dims[s])
                for member in (raw[:, 0] + parts[s][0][0], raw[:, 1], raw[:, 2] + parts[s][0][1])
            ]
        )
    ctx_text, ctx_lay, log_total = page_forward(*qkv[0], *qkv[1], segments)
    contexts = [ctx_text.reshape(rows, -1), ctx_lay.reshape(rows, -1)]
    attend_grads, feed_grads, input_grads, vector_grads, outs = [], [], [], [], []
    first, d_first, d_ctx, out_proj = [], [], [], []
    for s in range(2):
        vec, bias_in = parts[s]
        attended = jnp.einsum(
            "rn,dn->rd", contexts[s], attend[s][:, 3], preferred_element_type=F32
        )
        h1, n1, inv1 = norm_forward(own_rows[s] + attended + vec[2], vec[3], vec[4])
        h1_low = to_low(h1)
        gate = jnp.dot(h1_low, feeds[s][:, 0], preferred_element_type=F32) + bias_in
        active = to_low(gelu_exact(gate))
        f_out = jnp.einsum("rf,df->rd", active, feeds[s][:, 1], preferred_element_type=F32)
        o, n2, inv2 = norm_forward(h1 + f_out + vec[5], vec[6], vec[7])
        outs.append(to_low(o))
        d_r2, g_gain2, g_shift2 = norm_backward(cots[s].astype(F32), n2, inv2, vec[6])
        df = to_low(d_r2)
        down = jnp.einsum("rd,rf->df", df, active, preferred_element_type=F32)
        d_active = jnp.dot(df, feeds[s][:, 1], preferred_element_type=F32)
        d_gate = gelu_backward(gate, d_active)
        d_gate_low = to_low(d_gate)
        up = jnp.einsum("rd,rf->df", h1_low, d_gate_low, preferred_element_type=F32)
        feed_grads.append(jnp.stack([to_low(up), to_low(down)], axis=1))
        d_h1 = d_r2 + jnp.einsum(
            "rf,df->rd", d_gate_low, feeds[s][:, 0], preferred_element_type=F32
        )
        d_r1, g_gain1, g_shift1 = norm_backward(d_h1, n1, inv1, vec[3])
        da = to_low(d_r1)
        out_proj.append(jnp.einsum("rd,rn->dn", da, contexts[s], preferred_element_type=F32))
        d_ctx.append(
            to_low(jnp.dot(da, attend[s][:, 3], preferred_element_type=F32)).reshape(
                rows, -1, head_dims[s]
            )
        )
        d_first.append(d_r1)
        vector_grads.append(
            [
                None,
                None,
                jnp.sum(d_r1, axis=0),
                g_gain1,
                g_shift1,
                jnp.sum(d_r2, axis=0),
                g_gain2,
                g_shift2,
                jnp.sum(d_gate, axis=0),
            ]
        )
    heads = page_backward(*qkv[0], *qkv[1], segments, log_total, d_ctx[0], d_ctx[1])
    for s in range(2):
        pieces = [heads[3 * s + k].reshape(rows, -1) for k in range(3)]
        vector_grads[s][0] = jnp.sum(pieces[0], axis=0)
        vector_grads[s][1] = jnp.sum(pieces[2], axis=0)
        d_proj = jnp.stack([to_low(piece) for piece in pieces], axis=1)
        qkv_grad = jnp.einsum("rd,rcn->dcn", rows_low[s], d_proj, preferred_element_type=F32)
        attend_grads.append(
            to_low(jnp.concatenate([qkv_grad, out_proj[s][:, None]], axis=1))
        )
        input_grads.append(
            d_first[s]
            + jnp.einsum("rcn,dcn->rd", d_proj, attend[s][:, :3], preferred_element_type=F32)
        )
    g_lay = input_grads[1]
    g_high = to_low(g_lay)
    g_rest = to_low(g_lay - g_high.astype(F32))

    def bin_sum(hot, high, rest):
        both = jnp.einsum(
            "rb,rl->bl", hot, jnp.concatenate([high, rest], axis=1), preferred_element_type=F32
        )
        return both[:, : high.shape[1]] + both[:, high.shape[1] :]

    table_grad = jnp.concatenate(
        [
            bin_sum(hots[0], g_high[:, :half_width], g_rest[:, :half_width]),
            bin_sum(hots[1], g_high[:, half_width:], g_rest[:, half_width:]),
        ],
        axis=1,
    )
    table_grad, _ = reduce_small(table_grad, total)
    vector_grad = sum_everywhere(
        jnp.concatenate([member for stream in vector_grads for member in stream]), total
    )

    def by_owner(grad, own, cols):
        return grad.reshape(n_dp, own, grad.shape[1], n_t, cols).transpose(0, 3, 1, 2, 4)

    g_feed = by_owner(feed_grads[0], d_own, ht).transpose(0, 1, 3, 2, 4)
    g_feed = g_feed.reshape(total, 2 * d_own, ht)
    g_at = by_owner(attend_grads[0], d_own, ct).reshape(total, d_own, 4 * ct)
    g_al = by_owner(attend_grads[1], dl_own, cl).reshape(total, dl_own, 4 * cl)
    g_fl = by_owner(feed_grads[1], dl_own, hl).reshape(total, dl_own, 2 * hl)
    g_lay_pack = jnp.pad(
        jnp.concatenate([g_al, g_fl], axis=2),
        ((0, 0), (0, LAY_ROWS - dl_own), (0, 4 * ct - lay_cols)),
    )
    g_attend = jnp.concatenate([g_at, g_lay_pack], axis=1)
    feed_sum = reduce_shards(reorder(g_feed, me_arr), total)
    attend_sum = reduce_shards(reorder(g_attend, me_arr), total)
    shared_sq = sum_everywhere(
        (jnp.sum(feed_sum * feed_sum) + jnp.sum(attend_sum * attend_sum)).reshape(1), total
    )[0]
    clip_norm = jnp.sqrt(
        shared_sq + jnp.sum(vector_grad * vector_grad) + jnp.sum(table_grad * table_grad)
    )
    factor = jnp.minimum(1.0, CLIP_NORM / (clip_norm + 1e-06))
    lay_sum = attend_sum[d_own : d_own + dl_own]
    states = [
        (
            attend_text,
            attend_text_mean,
            attend_text_square,
            attend_sum[:d_own].reshape(d_own, 4, ct),
            WEIGHT_DECAY,
        ),
        (
            feed_text,
            feed_text_mean,
            feed_text_square,
            feed_sum.reshape(2, d_own, ht).transpose(1, 0, 2),
            WEIGHT_DECAY,
        ),
        (
            attend_layout,
            attend_layout_mean,
            attend_layout_square,
            lay_sum[:, : 4 * cl].reshape(dl_own, 4, cl),
            WEIGHT_DECAY,
        ),
        (
            feed_layout,
            feed_layout_mean,
            feed_layout_square,
            lay_sum[:, 4 * cl : lay_cols].reshape(dl_own, 2, hl),
            WEIGHT_DECAY,
        ),
        (vectors, vectors_mean, vectors_square, vector_grad, 0.0),
        (tables, tables_mean, tables_square, table_grad.reshape(-1), 0.0),
    ]
    updated = []
    for k in range(6):
        updated.extend(
            adamw_step(
                states[k][0],
                states[k][1],
                states[k][2],
                states[k][3] * factor,
                states[k][4],
                LEARN_RATES[k],
            )
        )
    return (
        pages_of(outs[0]),
        pages_of(outs[1]).reshape(pages, quarter * wl),
        pages_of(to_low(input_grads[0])).astype(F32),
        pages_of(to_low(input_grads[1])).astype(F32).reshape(pages, quarter * wl),
        *updated,
        clip_norm,
    )


def solution(mesh):
    rows3, rows2, cols3 = P("dp", "tensor", None), P("dp", "tensor"), P("dp", None, "tensor")
    in_specs = (rows3, rows2, rows2, rows2, rows3, rows2) + (cols3,) * 12 + (P(),) * 6
    out_specs = (rows3, rows2, rows3, rows2) + (cols3,) * 12 + (P(),) * 7
    return jax.shard_map(
        on_device, mesh=mesh, in_specs=in_specs, out_specs=out_specs, check_vma=False
    )
```

time: 1130 us -> 851 us (0.75)
  waiting for transfers between devices: 569 us -> 173 us
  blocking collectives: 149 us -> 0 us
  local copies, waits for them, and re-layouts: 90.4 us -> 234 us
  starting transfers between devices: 1.46 us -> 82.1 us
  Pallas kernels: 0 us -> 76.7 us
  matrix products: 212 us -> 142 us
  other arithmetic: 73.9 us -> 119 us
  between operations: 22.7 us -> 10.5 us
    reduce_scatter x9 -> x0, waiting for transfers between devices: 184 us -> none  [the longest x1 56.7 us: on_device(): lax.psum_scatter(partials[0], 'tensor', scatter_dimension=1, tiled=True)]
    ppermute x0 -> x81, waiting for transfers between devices: none -> 173 us  [xor_send(): return lax.ppermute(values, AXES, [(i, i ^ distance) for i in range(total)])]
    unnamed x22 -> x0, waiting for transfers between devices: 151 us -> none
    psum x1 -> x0, waiting for transfers between devices: 129 us -> none  [on_device(): small_grads = lax.psum((vector_grad, table_grad), ('dp', 'tensor'))]
    all_gather x7 -> x0, blocking collectives: 109 us -> none  [the longest x1 32.8 us: on_device(): lax.all_gather(to_low(attend_layout), 'dp', axis=0, tiled=True)]
    all_gather x6 -> x0, waiting for transfers between devices: 104 us -> none  [the longest x1 51.6 us: on_device(): lax.all_gather(to_low(feed_text), 'dp', axis=0, tiled=True)]
    dot_general x81 -> x38, matrix products: 207 us -> 124 us  [the longest x2 23 us: on_device(): gate = jnp.dot(h1_low, feeds[s][:, 0], preferred_element_type=F32) + bias_in]
    ppermute x0 -> x81, starting transfers between devices: none -> 82.1 us  [xor_send(): return lax.ppermute(values, AXES, [(i, i ^ distance) for i in range(total)])]
  transfers between devices with their start and end apart: 19 -> 81, of which waited for: 14 -> 30; matrix products, arithmetic and copies ran while one was open for 26% -> 37% of each run, Pallas kernels for 0% -> 7%
where the time goes in v1:
time: 851 us; the launch traced here: 838 us
  local copies, waits for them, and re-layouts  234 us (27%)
  waiting for transfers between devices  173 us (20%)
  matrix products  142 us (17%)
  other arithmetic  119 us (14%)
  starting transfers between devices  82.1 us (10%)
  Pallas kernels  76.7 us (9%)
  between operations  10.5 us (1%)
    ppermute x81, waiting for transfers between devices, xor_send(): return lax.ppermute(values, AXES, [(i, i ^ distance) for i in range(total)])  173 us
    ppermute x81, starting transfers between devices, xor_send(): return lax.ppermute(values, AXES, [(i, i ^ distance) for i in range(total)])  82.1 us
    pallas_call x4, Pallas kernels, reorder(): pl.pallas_call(body, grid_spec=pltpu.PrefetchScalarGridSpec(num_scalar_pr...  76.7 us
    another operation x8, local copies, waits for them, and re-layouts, on_device(): feed_grads.append(jnp.stack([to_low(up), to_low(down)], axis=1))  33 us
    convert_element_type x17, other arithmetic, to_low(): return values.astype(BF16)  25.2 us
    reshape x2, local copies, waits for them, and re-layouts, on_device(): w_text = attend_all[:, :, :d_own].reshape(n_dp, n_t, d_own, 4, ct)  23.7 us
    dot_general x2, matrix products, on_device(): gate = jnp.dot(h1_low, feeds[s][:, 0], preferred_element_type=F32) + bias_in  23 us
    unnamed x347, local copies, waits for them, and re-layouts  21.5 us
  transfers between devices with their start and end apart: 81, of which 30 were waited for; matrix products, arithmetic and copies ran while one was open for 37% of the time, Pallas kernels for 7%

profile of v1, /device:TPU:0, one launch (start us, length us, event | category | flops | bytes accessed | tf_op | source)
XLA Modules:
  0.0 837.8 jit_solution(17537202842084759550)
XLA Ops:
  31.5 19.4 %collective-permute-done.19 = bf16[192,768]{1,0:T(8,128)(2,1)S(1)} collective-permute-done((bf16[192,768]{1,0:T(8,128)(2,1)S(1)}, bf16[192,768]{1,0:T(8,128)(2,1)S(1)}, u32[]{:S(2)}, u32[]{:S(2)}) %collective-permute-start.19) | collective-permute-done | bytes 294944 | tf_op jit(solution)/shard_map/ppermute | solution.py:34
  60.8 22.9 %collective-permute-done.24 = bf16[4,96,768]{2,1,0:T(8,128)(2,1)} collective-permute-done((bf16[4,96,768]{2,1,0:T(8,128)(2,1)}, bf16[4,96,768]{2,1,0:T(8,128)(2,1)}, u32[]{:S(2)}, u32[]{:S(2)}) %collective-permute-start.24) | collective-permute-done | bytes 589856 | tf_op jit(solution)/shard_map/ppermute | solution.py:34
  140.3 18.8 %shard_map.407 = bf16[32,128,768]{2,1,0:T(8,128)(2,1)} custom-call(s32[1]{0:T(128)} %bitcast.5.own_ref, bf16[32,128,768]{2,1,0:T(8,128)(2,1)} %pad_maximum_fusion.2.in_ref), custom_call_target="tpu_custom_call" | custom-call | tf_op jit(solution)/shard_map/pallas_call | solution.py:137
  172.8 12.9 %reshape.547 = bf16[8,4,96,4,192]{4,3,2,1,0:T(4,128)(2,1)} reshape(bf16[8,4,96,768]{3,2,1,0:T(8,128)(2,1)} %slice.478) | data formatting | bytes 9437184 | tf_op jit(solution)/shard_map/reshape | solution.py:287
  185.7 10.8 %copy.377 = bf16[8,4,96,4,192]{4,1,2,0,3:T(4,128)(2,1)} copy(bf16[8,4,96,4,192]{4,3,2,1,0:T(4,128)(2,1)} %reshape.547) | data formatting | bytes 9437184 | tf_op jit(solution)/shard_map/reshape | solution.py:287
  196.5 12.0 %reshape.548 = bf16[768,4,768]{2,0,1:T(8,128)(2,1)} reshape(bf16[8,96,4,4,192]{4,3,1,0,2:T(4,128)(2,1)} %bitcast.465) | data formatting | bytes 9437184 | tf_op jit(solution)/shard_map/reshape | solution.py:288
  372.0 19.6 %shard_map.408 = bf16[32,192,768]{2,1,0:T(8,128)(2,1)} custom-call(s32[1]{0:T(128)} %bitcast.5.own_ref, bf16[32,192,768]{2,1,0:T(8,128)(2,1)} %pad_maximum_fusion.in_ref), custom_call_target="tpu_custom_call" | custom-call | tf_op jit(solution)/shard_map/pallas_call | solution.py:137
  391.6 12.4 %copy.376 = bf16[8,4,2,96,768]{4,1,3,0,2:T(4,128)(2,1)} copy(bf16[8,4,2,96,768]{4,3,2,1,0:T(8,128)(2,1)} %bitcast.459) | data formatting | bytes 18874368 | tf_op jit(solution)/shard_map/reshape | solution.py:294
  404.0 17.1 %reshape.558 = bf16[768,2,3072]{2,0,1:T(8,128)(2,1)} reshape(bf16[8,96,2,4,768]{4,3,1,0,2:T(4,128)(2,1)} %bitcast.460) | data formatting | bytes 18874368 | tf_op jit(solution)/shard_map/reshape | solution.py:295
  421.1 19.3 %multiply_convert_fusion = (bf16[512,3072]{1,0:T(8,128)(2,1)S(1)}, f32[512,3072]{1,0:T(8,128)S(1)}, f32[512,3072]{1,0:T(8,128)}) fusion(f32[3072]{0:T(1024)S(1)} %copy-done.118, bf16[768,2,3072]{2,0,1:T(8,128)(2,1)} %reshape.558, f32[512,768]{1,0:T(8,128)S(1)} %copy-done.14, f32[768]{0:T(1024)S(1)} %copy-done.128, f32[768]{0:T(1024)S(1)} %copy-done.114, ...), kind=kOutput, calls=%fused_computation.28 | convolution fusion | flops 2521694208 | bytes 22042624 | tf_op jit(solution)/shard_map/dot_general | solution.py:341
  448.7 8.0 fusion.215
  472.8 17.8 %add_convert_fusion = bf16[12,512,512]{1,2,0:T(8,128)(2,1)} fusion(f32[12,512,512]{1,2,0:T(8,128)} %copy-done, f32[12,512,512]{1,2,0:T(8,128)} %get-tuple-element.259, f32[12,512]{1,0:T(8,128)S(1)} %copy-done.95, f32[12,512]{1,0:T(8,128)S(1)} %copy-done.49, bf16[512,12,64]{0,2,1:T(8,128)(2,1)S(1)} %bitcast.494, f32[512,12,64]{0,2,1:T(8,128)S(1)} %bitcast.483, ...), kind=kOutput, calls=%fused_computation.1 | convolution fusion | flops 835197440 | bytes 33868800 | tf_op jit(solution)/shard_map/sub | solution.py:105
  490.6 8.2 bitcast_convert_fusion
  508.1 9.8 %stack.215 = bf16[8,96,1,4,768]{4,3,1,0,2:T(4,128)(2,1)} reshape(bf16[768,3072]{1,0:T(8,128)(2,1)} %convolution_convert_fusion.1) | data formatting | bytes 9437184 | tf_op jit(solution)/shard_map/stack | solution.py:353
  548.1 8.4 %maximum_bitcast_fusion = bf16[8,4,96,4,192]{4,3,2,1,0:T(4,128)(2,1)} fusion(bf16[8,96,1,4,192]{4,2,1,3,0:T(2,128)(2,1)S(1)} %copy.302, bf16[8,96,3,4,192]{4,2,1,3,0:T(4,128)(2,1)S(1)} %copy.301), kind=kLoop, calls=%fused_computation.21 | loop fusion | flops 9437184 | bytes 9437184 | tf_op jit(solution)/shard_map/transpose | solution.py:416
  556.5 11.6 %reshape.569 = bf16[32,96,768]{2,1,0:T(8,128)(2,1)} reshape(bf16[8,4,96,4,192]{4,3,2,1,0:T(4,128)(2,1)} %maximum_bitcast_fusion) | data formatting | bytes 9437184 | tf_op jit(solution)/shard_map/reshape | solution.py:420
  568.1 9.7 %stack.216 = bf16[8,96,1,4,768]{4,3,1,0,2:T(4,128)(2,1)} reshape(bf16[768,3072]{1,0:T(8,128)(2,1)} %convolution_convert_fusion) | data formatting | bytes 9437184 | tf_op jit(solution)/shard_map/stack | solution.py:353
  583.2 8.2 pad_maximum_fusion.1
  591.4 19.6 %shard_map.410 = bf16[32,192,768]{2,1,0:T(8,128)(2,1)} custom-call(s32[1]{0:T(128)} %bitcast.5.own_ref, bf16[32,192,768]{2,1,0:T(8,128)(2,1)} %bitcast.458), custom_call_target="tpu_custom_call" | custom-call | tf_op jit(solution)/shard_map/pallas_call | solution.py:137
  626.7 18.8 %shard_map.409 = bf16[32,128,768]{2,1,0:T(8,128)(2,1)} custom-call(s32[1]{0:T(128)} %bitcast.5.own_ref, bf16[32,128,768]{2,1,0:T(8,128)(2,1)} %pad_maximum_fusion.3.in_ref), custom_call_target="tpu_custom_call" | custom-call | tf_op jit(solution)/shard_map/pallas_call | solution.py:137
  702.5 11.2 %collective-permute-done.48 = bf16[4,2,64,768]{3,2,1,0:T(8,128)(2,1)S(1)} collective-permute-done((bf16[4,2,64,768]{3,2,1,0:T(8,128)(2,1)S(1)}, bf16[4,2,64,768]{3,2,1,0:T(8,128)(2,1)S(1)}, u32[]{:S(2)}, u32[]{:S(2)}) %collective-permute-start.48) | collective-permute-done | bytes 786464 | tf_op jit(solution)/shard_map/ppermute | solution.py:34
  717.8 30.4 %collective-permute-done.49 = bf16[4,64,768]{2,1,0:T(8,128)(2,1)S(1)} collective-permute-done((bf16[4,64,768]{2,1,0:T(8,128)(2,1)S(1)}, bf16[4,64,768]{2,1,0:T(8,128)(2,1)S(1)}, u32[]{:S(2)}, u32[]{:S(2)}) %collective-permute-start.49) | collective-permute-done | bytes 393248 | tf_op jit(solution)/shard_map/ppermute | solution.py:34
  753.6 10.1 %collective-permute-done.57 = bf16[4,96,768]{2,1,0:T(8,128)(2,1)S(1)} collective-permute-done((bf16[4,96,768]{2,1,0:T(8,128)(2,1)S(1)}, bf16[4,96,768]{2,1,0:T(8,128)(2,1)S(1)}, u32[]{:S(2)}, u32[]{:S(2)}) %collective-permute-start.57) | collective-permute-done | bytes 589856 | tf_op jit(solution)/shard_map/ppermute | solution.py:34
  784.9 14.0 %collective-permute-done.59 = bf16[192,768]{1,0:T(8,128)(2,1)S(1)} collective-permute-done((bf16[192,768]{1,0:T(8,128)(2,1)S(1)}, bf16[192,768]{1,0:T(8,128)(2,1)S(1)}, u32[]{:S(2)}, u32[]{:S(2)}) %collective-permute-start.59) | collective-permute-done | bytes 294944 | tf_op jit(solution)/shard_map/ppermute | solution.py:34
  (775 shorter events, 476.5 us)
Async XLA Ops:
  18.9 78.3 %collective-permute-start.13 = (s32[128,3]{0,1:T(4,128)}, s32[128,3]{0,1:T(4,128)S(1)}, u32[]{:S(2)}, u32[]{:S(2)}) collective-permute-start(s32[128,3]{0,1:T(4,128)} %bitcast.450), channel_id=1, source_target_pairs={{0,2},{1,3},{2,0},{3,1},{4,6},{5,7},{6,4},{7,5},{8,10},{9,11},{10,... | collective-permute-start | bytes 4616 | tf_op jit(solution)/shard_map/ppermute | solution.py:34
  86.4 40.9 %collective-permute-start.25 = (bf16[2,4,96,768]{3,2,1,0:T(8,128)(2,1)}, bf16[2,4,96,768]{3,2,1,0:T(8,128)(2,1)}, u32[]{:S(2)}, u32[]{:S(2)}) collective-permute-start(bf16[2,4,96,768]{3,2,1,0:T(8,128)(2,1)} %get-tuple-element.173), channel_id=1, source_target_pairs={{0,2},{1,3},{2,0},{3,1},{4,6},{5,7},{6,4},{7,5},{8,10},{9,11},{10,... | collective-permute-start | bytes 3538952 | tf_op jit(solution)/shard_map/ppermute | solution.py:34
  90.1 41.0 %collective-permute-start.8 = (bf16[2,2,4,64,768]{4,3,2,1,0:T(8,128)(2,1)}, bf16[2,2,4,64,768]{4,3,2,1,0:T(8,128)(2,1)}, u32[]{:S(2)}, u32[]{:S(2)}) collective-permute-start(bf16[2,2,4,64,768]{4,3,2,1,0:T(8,128)(2,1)} %get-tuple-element.158), channel_id=1, source_target_pairs={{0,1},{1,0},{2,3},{3,2},{4,5},{5,4},{6,7},{7,6},{8,9},{9,8},{10,11... | collective-permute-start | bytes 4718600 | tf_op jit(solution)/shard_map/ppermute | solution.py:34
  115.8 52.9 %collective-permute-start.15 = (bf16[128,192]{0,1:T(8,128)(2,1)}, bf16[128,192]{0,1:T(8,128)(2,1)}, u32[]{:S(2)}, u32[]{:S(2)}) collective-permute-start(bf16[128,192]{0,1:T(8,128)(2,1)} %bitcast.534), channel_id=1, source_target_pairs={{0,1},{1,0},{2,3},{3,2},{4,5},{5,4},{6,7},{7,6},{8,9},{9,8},{10,11... | collective-permute-start | bytes 147464 | tf_op jit(solution)/shard_map/ppermute | solution.py:34
  121.9 46.9 %collective-permute-start.16 = (bf16[128,192]{0,1:T(8,128)(2,1)}, bf16[128,192]{0,1:T(8,128)(2,1)}, u32[]{:S(2)}, u32[]{:S(2)}) collective-permute-start(bf16[128,192]{0,1:T(8,128)(2,1)} %bitcast.39), channel_id=1, source_target_pairs={{0,2},{1,3},{2,0},{3,1},{4,6},{5,7},{6,4},{7,5},{8,10},{9,11},{10,... | collective-permute-start | bytes 147464 | tf_op jit(solution)/shard_map/ppermute | solution.py:34
  127.3 42.2 %collective-permute-start.17 = (bf16[128,192]{0,1:T(8,128)(2,1)}, bf16[128,192]{0,1:T(8,128)(2,1)}, u32[]{:S(2)}, u32[]{:S(2)}) collective-permute-start(bf16[128,192]{0,1:T(8,128)(2,1)} %bitcast.40), channel_id=1, source_target_pairs={{0,3},{1,2},{2,1},{3,0},{4,7},{5,6},{6,5},{7,4},{8,11},{9,10},{10,... | collective-permute-start | bytes 147464 | tf_op jit(solution)/shard_map/ppermute | solution.py:34
  131.1 120.8 %collective-permute-start.36 = (bf16[128,192]{0,1:T(8,128)(2,1)}, bf16[128,192]{0,1:T(8,128)(2,1)}, u32[]{:S(2)}, u32[]{:S(2)}) collective-permute-start(bf16[128,192]{0,1:T(8,128)(2,1)} %bitcast.99), channel_id=1, source_target_pairs={{0,1},{1,0},{2,3},{3,2},{4,5},{5,4},{6,7},{7,6},{8,9},{9,8},{10,11... | collective-permute-start | bytes 147464 | tf_op jit(solution)/shard_map/ppermute | solution.py:34
  133.7 118.2 %collective-permute-start.37 = (bf16[128,192]{0,1:T(8,128)(2,1)}, bf16[128,192]{0,1:T(8,128)(2,1)}, u32[]{:S(2)}, u32[]{:S(2)}) collective-permute-start(bf16[128,192]{0,1:T(8,128)(2,1)} %bitcast.100), channel_id=1, source_target_pairs={{0,2},{1,3},{2,0},{3,1},{4,6},{5,7},{6,4},{7,5},{8,10},{9,11},{10,... | collective-permute-start | bytes 147464 | tf_op jit(solution)/shard_map/ppermute | solution.py:34
  168.7 40.6 %collective-permute-start = (bf16[128,768]{1,0:T(8,128)(2,1)S(1)}, bf16[128,768]{1,0:T(8,128)(2,1)S(1)}, u32[]{:S(2)}, u32[]{:S(2)}) collective-permute-start(bf16[128,768]{1,0:T(8,128)(2,1)S(1)} %copy-done.79), channel_id=1, source_target_pairs={{0,1},{1,0},{2,3},{3,2},{4,5},{5,4},{6,7},{7,6},{8,9},{9,8},{10,11... | collective-permute-start | bytes 589832 | tf_op jit(solution)/shard_map/ppermute | solution.py:34
  168.8 40.5 %collective-permute-start.2 = (bf16[128,768]{1,0:T(8,128)(2,1)S(1)}, bf16[128,768]{1,0:T(8,128)(2,1)S(1)}, u32[]{:S(2)}, u32[]{:S(2)}) collective-permute-start(bf16[128,768]{1,0:T(8,128)(2,1)S(1)} %copy-done.78), channel_id=1, source_target_pairs={{0,3},{1,2},{2,1},{3,0},{4,7},{5,6},{6,5},{7,4},{8,11},{9,10},{10,... | collective-permute-start | bytes 589832 | tf_op jit(solution)/shard_map/ppermute | solution.py:34
  169.4 40.6 %collective-permute-start.1 = (bf16[128,768]{1,0:T(8,128)(2,1)S(1)}, bf16[128,768]{1,0:T(8,128)(2,1)S(1)}, u32[]{:S(2)}, u32[]{:S(2)}) collective-permute-start(bf16[128,768]{1,0:T(8,128)(2,1)S(1)} %copy-done.77), channel_id=1, source_target_pairs={{0,2},{1,3},{2,0},{3,1},{4,6},{5,7},{6,4},{7,5},{8,10},{9,11},{10,... | collective-permute-start | bytes 589832 | tf_op jit(solution)/shard_map/ppermute | solution.py:34
  209.3 42.6 %collective-permute-start.38 = (bf16[128,192]{0,1:T(8,128)(2,1)}, bf16[128,192]{0,1:T(8,128)(2,1)}, u32[]{:S(2)}, u32[]{:S(2)}) collective-permute-start(bf16[128,192]{0,1:T(8,128)(2,1)} %bitcast.101), channel_id=1, source_target_pairs={{0,3},{1,2},{2,1},{3,0},{4,7},{5,6},{6,5},{7,4},{8,11},{9,10},{10,... | collective-permute-start | bytes 147464 | tf_op jit(solution)/shard_map/ppermute | solution.py:34
  209.3 152.4 %collective-permute-start.26 = (bf16[2,2,4,96,768]{4,3,2,1,0:T(8,128)(2,1)}, bf16[2,2,4,96,768]{4,3,2,1,0:T(8,128)(2,1)}, u32[]{:S(2)}, u32[]{:S(2)}) collective-permute-start(bf16[2,2,4,96,768]{4,3,2,1,0:T(8,128)(2,1)} %get-tuple-element.155), channel_id=1, source_target_pairs={{0,1},{1,0},{2,3},{3,2},{4,5},{5,4},{6,7},{7,6},{8,9},{9,8},{10,11... | collective-permute-start | bytes 7077896 | tf_op jit(solution)/shard_map/ppermute | solution.py:34
  210.0 154.3 %collective-permute-start.23 = (bf16[2,2,4,96,768]{4,3,2,1,0:T(8,128)(2,1)}, bf16[2,2,4,96,768]{4,3,2,1,0:T(8,128)(2,1)}, u32[]{:S(2)}, u32[]{:S(2)}) collective-permute-start(bf16[2,2,4,96,768]{4,3,2,1,0:T(8,128)(2,1)} %get-tuple-element.153), channel_id=1, source_target_pairs={{0,1},{1,0},{2,3},{3,2},{4,5},{5,4},{6,7},{7,6},{8,9},{9,8},{10,11... | collective-permute-start | bytes 7077896 | tf_op jit(solution)/shard_map/ppermute | solution.py:34
  286.0 55.5 %collective-permute-start.31 = (bf16[128,192]{0,1:T(8,128)(2,1)}, bf16[128,192]{0,1:T(8,128)(2,1)}, u32[]{:S(2)}, u32[]{:S(2)}) collective-permute-start(bf16[128,192]{0,1:T(8,128)(2,1)} %get-tuple-element.223), channel_id=1, source_target_pairs={{0,2},{1,3},{2,0},{3,1},{4,6},{5,7},{6,4},{7,5},{8,10},{9,11},{10,... | collective-permute-start | bytes 147464 | tf_op jit(solution)/shard_map/ppermute | solution.py:34
  287.5 54.9 %collective-permute-start.30 = (bf16[128,192]{0,1:T(8,128)(2,1)}, bf16[128,192]{0,1:T(8,128)(2,1)}, u32[]{:S(2)}, u32[]{:S(2)}) collective-permute-start(bf16[128,192]{0,1:T(8,128)(2,1)} %get-tuple-element.224), channel_id=1, source_target_pairs={{0,1},{1,0},{2,3},{3,2},{4,5},{5,4},{6,7},{7,6},{8,9},{9,8},{10,11... | collective-permute-start | bytes 147464 | tf_op jit(solution)/shard_map/ppermute | solution.py:34
  351.1 92.5 %collective-permute-start.33 = (bf16[128,768]{1,0:T(8,128)(2,1)}, bf16[128,768]{1,0:T(8,128)(2,1)}, u32[]{:S(2)}, u32[]{:S(2)}) collective-permute-start(bf16[128,768]{1,0:T(8,128)(2,1)} %get-tuple-element.182), channel_id=1, source_target_pairs={{0,1},{1,0},{2,3},{3,2},{4,5},{5,4},{6,7},{7,6},{8,9},{9,8},{10,11... | collective-permute-start | bytes 589832 | tf_op jit(solution)/shard_map/ppermute | solution.py:34
  352.5 91.1 %collective-permute-start.35 = (bf16[128,768]{1,0:T(8,128)(2,1)}, bf16[128,768]{1,0:T(8,128)(2,1)}, u32[]{:S(2)}, u32[]{:S(2)}) collective-permute-start(bf16[128,768]{1,0:T(8,128)(2,1)} %get-tuple-element.183), channel_id=1, source_target_pairs={{0,3},{1,2},{2,1},{3,0},{4,7},{5,6},{6,5},{7,4},{8,11},{9,10},{10,... | collective-permute-start | bytes 589832 | tf_op jit(solution)/shard_map/ppermute | solution.py:34
  360.0 83.7 %collective-permute-start.34 = (bf16[128,768]{1,0:T(8,128)(2,1)}, bf16[128,768]{1,0:T(8,128)(2,1)S(1)}, u32[]{:S(2)}, u32[]{:S(2)}) collective-permute-start(bf16[128,768]{1,0:T(8,128)(2,1)} %get-tuple-element.184), channel_id=1, source_target_pairs={{0,2},{1,3},{2,0},{3,1},{4,6},{5,7},{6,4},{7,5},{8,10},{9,11},{10,... | collective-permute-start | bytes 589832 | tf_op jit(solution)/shard_map/ppermute | solution.py:34
  620.5 75.5 %collective-permute-start.53 = (bf16[4,2,2,192,768]{4,3,0,2,1:T(8,128)(2,1)}, bf16[4,2,2,192,768]{4,3,0,2,1:T(8,128)(2,1)}, u32[]{:S(2)}, u32[]{:S(2)}) collective-permute-start(bf16[4,2,2,192,768]{4,3,0,2,1:T(8,128)(2,1)} %bitcast.447), channel_id=1, source_target_pairs={{0,1},{1,0},{2,3},{3,2},{4,5},{5,4},{6,7},{7,6},{8,9},{9,8},{10,11... | collective-permute-start | bytes 14155784 | tf_op jit(solution)/shard_map/ppermute | solution.py:34
  649.6 40.4 %collective-permute-start.45 = (bf16[4,2,2,128,768]{4,3,2,1,0:T(8,128)(2,1)}, bf16[4,2,2,128,768]{4,3,2,1,0:T(8,128)(2,1)}, u32[]{:S(2)}, u32[]{:S(2)}) collective-permute-start(bf16[4,2,2,128,768]{4,3,2,1,0:T(8,128)(2,1)} %slice_bitcast_fusion.6), channel_id=1, source_target_pairs={{0,1},{1,0},{2,3},{3,2},{4,5},{5,4},{6,7},{7,6},{8,9},{9,8},{10,11... | collective-permute-start | bytes 9437192 | tf_op jit(solution)/shard_map/ppermute | solution.py:34
  685.3 79.8 %collective-permute-start.70 = (f32[11520]{0:T(1024)S(1)}, f32[11520]{0:T(1024)S(1)}, u32[]{:S(2)}, u32[]{:S(2)}) collective-permute-start(f32[11520]{0:T(1024)S(1)} %add.588), channel_id=1, source_target_pairs={{0,16},{1,17},{2,18},{3,19},{4,20},{5,21},{6,22},{7,23},{8,24},{9,... | collective-permute-start | bytes 138248 | tf_op jit(solution)/shard_map/ppermute | solution.py:34
  699.9 48.4 %collective-permute-start.54 = (bf16[4,2,96,768]{3,2,0,1:T(8,128)(2,1)S(1)}, bf16[4,2,96,768]{3,2,0,1:T(8,128)(2,1)S(1)}, u32[]{:S(2)}, u32[]{:S(2)}) collective-permute-start(bf16[4,2,96,768]{3,2,0,1:T(8,128)(2,1)S(1)} %slice_bitcast_fusion.16), channel_id=1, source_target_pairs={{0,2},{1,3},{2,0},{3,1},{4,6},{5,7},{6,4},{7,5},{8,10},{9,11},{10,... | collective-permute-start | bytes 3538952 | tf_op jit(solution)/shard_map/ppermute | solution.py:34
  701.2 47.2 %collective-permute-start.56 = (bf16[4,2,96,768]{3,2,0,1:T(8,128)(2,1)S(1)}, bf16[4,2,96,768]{3,2,0,1:T(8,128)(2,1)S(1)}, u32[]{:S(2)}, u32[]{:S(2)}) collective-permute-start(bf16[4,2,96,768]{3,2,0,1:T(8,128)(2,1)S(1)} %slice_bitcast_fusion.14), channel_id=1, source_target_pairs={{0,4},{1,5},{2,6},{3,7},{4,0},{5,1},{6,2},{7,3},{8,12},{9,13},{10,... | collective-permute-start | bytes 3538952 | tf_op jit(solution)/shard_map/ppermute | solution.py:34
  (224 other events, 2320.7 us)

commit v2 on v1

v2 whole, which is shorter than its diff:
```python
import functools
import math

import jax
import jax.numpy as jnp
from jax import lax
from jax.experimental import pallas as pl
from jax.experimental.pallas import tpu as pltpu
from jax.sharding import PartitionSpec as P

HD = 64
LHD = 16
STEP = 10

NORM_EPS = 1e-05
NEG_FILL = -1000000000.0
CLIP_NORM = 1.0
LEARN_RATES = (0.3, 0.05, 0.3, 0.05, 0.3, 0.3)
BETA_ONE = 0.9
BETA_TWO = 0.999
ADAM_EPS = 1e-08
WEIGHT_DECAY = 0.01
AXES = ("dp", "tensor")
LAY_ROWS = 32
F32 = jnp.float32
BF16 = jnp.bfloat16


def to_low(values):
    return values.astype(BF16)


def xor_send(values, total, distance):
    return lax.ppermute(values, AXES, [(i, i ^ distance) for i in range(total)])


def split_vectors(packed, widths, hidden):
    result = []
    offset = 0
    for stream in range(2):
        width_now = widths[stream]
        pieces = [packed[offset + k * width_now : offset + (k + 1) * width_now] for k in range(8)]
        offset = offset + 8 * width_now
        result.append((pieces, packed[offset : offset + hidden[stream]]))
        offset = offset + hidden[stream]
    return result


def adamw_step(weight, moment, square, gradient, decay_rate, rate_now):
    new_moment = BETA_ONE * moment + (1.0 - BETA_ONE) * gradient
    new_square = BETA_TWO * square + (1.0 - BETA_TWO) * gradient * gradient
    moment_hat = new_moment / (1.0 - BETA_ONE**STEP)
    square_hat = new_square / (1.0 - BETA_TWO**STEP)
    new_weight = weight - rate_now * (
        moment_hat / (jnp.sqrt(square_hat) + ADAM_EPS) + decay_rate * weight
    )
    return (new_weight, new_moment, new_square)


def lane_mean(values):
    return jnp.sum(values, axis=-1, keepdims=True) * (1.0 / values.shape[-1])


def norm_parts(residual):
    centered = residual - lane_mean(residual)
    inv_std = lax.rsqrt(lane_mean(centered * centered) + NORM_EPS)
    return centered * inv_std, inv_std


def norm_back(gradient, normed, inv_std, gain_vec):
    scaled = gradient * gain_vec
    d_resid = inv_std * (
        scaled - lane_mean(scaled) - normed * lane_mean(scaled * normed)
    )
    return d_resid


def col_sum(values):
    return jnp.sum(values, axis=0, keepdims=True)


def dot(a, b, da=1, db=0):
    return lax.dot_general(a, b, (((da,), (db,)), ((), ())), preferred_element_type=F32)


def round_up(count, step):
    return -(-count // step) * step


class Plan:
    def __init__(self, n_dp, n_t, quarter, wt, wl, ct, cl, ht, hl):
        self.n_dp, self.n_t, self.total = n_dp, n_t, n_dp * n_t
        self.far = self.total // 8
        self.quarter, self.rows = quarter, quarter * n_t
        self.wt, self.wl, self.ct, self.cl, self.ht, self.hl = wt, wl, ct, cl, ht, hl
        self.d_own, self.dl_own = wt // n_dp, wl // n_dp
        self.ra, self.rl = round_up(self.d_own, 16), round_up(self.dl_own, 16)
        self.cols = 4 * ct
        self.half_a = (self.ra + self.rl) // 2
        self.heads = ct // HD
        self.hw = HD + LHD
        self.lay_cols = 4 * cl + 2 * hl

    def spread(self, own, padded):
        out = jnp.arange(own * self.n_dp, dtype=jnp.int32)
        place = (out // own) * padded + out % own
        return (place[:, None] == jnp.arange(padded * self.n_dp, dtype=jnp.int32)[None]).astype(BF16)


VMEM_LIMIT = 60 * 2**20
COST = 10 * 10**9
ANY = pl.BlockSpec(memory_space=pl.ANY)
VM = pl.BlockSpec(memory_space=pltpu.VMEM)
SM = pl.BlockSpec(memory_space=pltpu.SMEM)


def kernel_call(body, outs, in_specs, out_specs, scratch, args):
    return pl.pallas_call(
        body,
        out_shape=outs,
        in_specs=in_specs,
        out_specs=out_specs,
        scratch_shapes=scratch,
        compiler_params=pltpu.CompilerParams(vmem_limit_bytes=VMEM_LIMIT),
        cost_estimate=pl.CostEstimate(flops=COST, bytes_accessed=2**20, transcendentals=0),
    )(*args)


def shape(dims, kind):
    return jax.ShapeDtypeStruct(tuple(dims), kind)


def wait_for(ref, sem):
    pltpu.make_async_copy(ref, ref, sem).wait()


def attend_forward(p, me2, core, rows_in, bias_t, bias_l, vec_t, vec_l, spread_t, spread_l, pieces):
    rows, hw, nh = p.rows, p.hw, p.heads
    padded_t, padded_l = p.n_dp * p.ra, p.n_dp * p.rl
    exact_t = p.ra == p.d_own
    first = core == 0
    nb = p.n_t // 2
    n_in = len(rows_in)

    def body(*refs):
        (me_ref, bt, bl, vt, vl, spt, spl), refs = refs[:7], refs[7:]
        in_refs, refs = refs[:n_in], refs[n_in:]
        piece_refs, refs = refs[:4], refs[4:]
        n_out = 12 if first else 11
        outs, scratch = refs[:n_out], refs[n_out:]
        wt_out, wl_out, qkv, ctx, lse_ref = outs[:5]
        wpad, lpad, acc_t, acc_l, ctx_rows, ctx_lay, sem_t, sem_l, sem_out = scratch
        my_dp, my_t = me_ref[0], me_ref[1]
        for k in range(nb):
            for y in range(2):
                low, high = piece_refs[y].at[k], piece_refs[2 + k].at[y]
                for z in range(p.far):
                    at = (z * 2 + y) ^ my_dp
                    row = pl.multiple_of(at * p.ra, 16)
                    lrow = pl.multiple_of(at * p.rl, 16)
                    pltpu.make_async_copy(
                        low.at[z], wpad.at[k, pl.ds(row, p.half_a)], sem_t.at[k]
                    ).start()
                    rest = p.ra - p.half_a
                    if rest:
                        pltpu.make_async_copy(
                            high.at[z, pl.ds(0, rest)],
                            wpad.at[k, pl.ds(pl.multiple_of(row + p.half_a, 16), rest)],
                            sem_t.at[k],
                        ).start()
                    pltpu.make_async_copy(
                        high.at[z, pl.ds(rest, p.rl)], lpad.at[k, pl.ds(lrow, p.rl)], sem_l
                    ).start()
        if first:
            x0, x1, x2, x3, tab = in_refs
            xt_ref, lay_low, lay_ref, ints_ref, intst_ref, acc_t_out, acc_l_out = outs[5:]
            for k, ref in enumerate((x0, x1, x2, x3)):
                xt_ref[pl.ds(k * p.quarter, p.quarter), :] = ref[:, : p.wt]
            x = xt_ref[...]
            side = jnp.concatenate([ref[:, p.wt :] for ref in (x0, x1, x2, x3)], axis=0).astype(F32)
            digits = side[:, p.wl : p.wl + 8]
            ints_ref[...] = digits
            intst_ref[...] = digits.T
            half = p.wl // 2
            levels = lax.broadcasted_iota(jnp.int32, (1, tab.shape[0]), 1).astype(F32)
            hot_x = (digits[:, 1:2] * 128.0 + digits[:, 2:3] == levels).astype(F32).astype(BF16)
            hot_y = (digits[:, 3:4] * 128.0 + digits[:, 4:5] == levels).astype(F32).astype(BF16)
            emb = jnp.concatenate([dot(hot_x, tab[:, :half]), dot(hot_y, tab[:, half:])], axis=1)
            lay = side[:, : p.wl] + emb
            low_rows = lay.astype(BF16)
            lay_low[...] = low_rows
            lay_ref[...] = lay
            acc_t[...] = jnp.zeros_like(acc_t)
            acc_l[...] = jnp.zeros_like(acc_l)
        else:
            xt_ref, lay_low, lay_ref, ints_ref, intst_ref, acc_t_in, acc_l_in = in_refs
            n1t, i1t, ht, n1l, i1l, hl = outs[5:]
            x, low_rows = xt_ref[...], lay_low[...]
            acc_t[...] = acc_t_in[...]
            acc_l[...] = acc_l_in[...]
        seg_col = ints_ref[:, 0:1]
        seg_row = intst_ref[0:1, :]
        wait_for(lpad, sem_l)
        for k in range(nb):
            wl_out[k] = dot(spl[...], lpad[k]).astype(BF16)

        def block(k, carry):
            wait_for(wpad.at[k], sem_t.at[k])
            if not exact_t:
                wpad[k, pl.ds(0, p.wt)] = dot(spt[...], wpad[k]).astype(BF16)
            out_copy = pltpu.make_async_copy(wpad.at[k, pl.ds(0, p.wt)], wt_out.at[k], sem_out)
            out_copy.start()
            own_t = (2 * k + core) ^ my_t
            w = wpad[k, pl.ds(0, p.wt)]
            wl = wl_out[k]
            raw = (dot(x, w[:, : 3 * p.ct]) + bt[own_t]).T
            raw_l = (dot(low_rows, wl[:, : 3 * p.cl]) + bl[own_t]).T
            for c in range(3):
                for h in range(nh):
                    top = raw[c * p.ct + h * HD : c * p.ct + (h + 1) * HD]
                    bot = raw_l[c * p.cl + h * LHD : c * p.cl + (h + 1) * LHD]
                    top, bot = top.astype(BF16), bot.astype(BF16)
                    if c == 0:
                        top = top * jnp.asarray(1.0 / math.sqrt(HD), BF16)
                        bot = bot * jnp.asarray(1.0 / math.sqrt(LHD), BF16)
                    qkv[k, c * nh + h, pl.ds(0, HD)] = top
                    qkv[k, c * nh + h, pl.ds(HD, LHD)] = bot
            for h in range(nh):
                scores = dot(qkv[k, nh + h], qkv[k, h], 0, 0)
                scores = jnp.where(seg_col == seg_row, scores, NEG_FILL)
                top_score = jnp.max(scores, axis=0, keepdims=True)
                expo = jnp.exp(scores - top_score)
                row_total = jnp.sum(expo, axis=0, keepdims=True)
                probs = (expo * (1.0 / row_total)).astype(BF16)
                mixed = dot(qkv[k, 2 * nh + h], probs).astype(BF16)
                ctx[k, h] = mixed
                ctx_rows[pl.ds(h * HD, HD)] = mixed[:HD]
                ctx_lay[pl.ds(h * LHD, LHD)] = mixed[HD:]
                lse_ref[k, pl.ds(h, 1), :] = top_score + jnp.log(row_total)
            acc_t[...] += dot(w[:, 3 * p.ct :], ctx_rows[...])
            acc_l[...] += dot(wl[:, 3 * p.cl : 4 * p.cl], ctx_lay[...])
            out_copy.wait()
            return carry

        lax.fori_loop(0, nb, block, 0)
        if first:
            acc_t_out[...] = acc_t[...]
            acc_l_out[...] = acc_l[...]
        else:
            for residual, acc, vec, n_ref, i_ref, h_ref in (
                (x.astype(F32), acc_t, vt, n1t, i1t, ht),
                (lay_ref[...], acc_l, vl, n1l, i1l, hl),
            ):
                normed, inv = norm_parts(residual + acc[...].T + vec[2:3])
                n_ref[...] = normed
                i_ref[...] = inv
                h_ref[...] = (normed * vec[3:4] + vec[4:5]).astype(BF16)

    outs = [
        shape((nb, p.wt, p.cols), BF16),
        shape((nb, p.wl, p.cols), BF16),
        shape((nb, 3 * nh, hw, rows), BF16),
        shape((nb, nh, hw, rows), BF16),
        shape((nb, 8, rows), F32),
    ]
    if first:
        outs += [
            shape((rows, p.wt), BF16),
            shape((rows, p.wl), BF16),
            shape((rows, p.wl), F32),
            shape((rows, 8), F32),
            shape((8, rows), F32),
            shape((p.wt, rows), F32),
            shape((p.wl, rows), F32),
        ]
    else:
        outs += [
            shape((rows, p.wt), F32),
            shape((rows, 1), F32),
            shape((rows, p.wt), BF16),
            shape((rows, p.wl), F32),
            shape((rows, 1), F32),
            shape((rows, p.wl), BF16),
        ]
    scratch = [
        pltpu.VMEM((nb, padded_t, p.cols), BF16),
        pltpu.VMEM((nb, padded_l, p.cols), BF16),
        pltpu.VMEM((p.wt, rows), F32),
        pltpu.VMEM((p.wl, rows), F32),
        pltpu.VMEM((p.ct, rows), BF16),
        pltpu.VMEM((p.cl, rows), BF16),
        pltpu.SemaphoreType.DMA((nb,)),
        pltpu.SemaphoreType.DMA,
        pltpu.SemaphoreType.DMA,
    ]
    args = (me2, bias_t, bias_l, vec_t, vec_l, spread_t, spread_l, *rows_in, *pieces)
    return kernel_call(
        body,
        outs,
        [SM] + [VM] * (6 + n_in) + [ANY] * 4,
        [ANY] + [VM] * (len(outs) - 1),
        scratch,
        args,
    )


def feed_forward(p, me2, core, pieces, w_lay, h_t, h_l, bin_t, bin_l, spread_t, rest_in):
    rows = p.rows
    padded_t = p.n_dp * p.ra
    exact_t = p.ra == p.d_own
    root = 1.0 / math.sqrt(2.0)
    first = core == 0
    nb = p.n_t // 2
    n_rest = len(rest_in)

    def body(*refs):
        (me_ref, wl, ht, hl, bt, bl, spt), refs = refs[:7], refs[7:]
        rest_refs, refs = refs[:n_rest], refs[n_rest:]
        piece_refs, refs = refs[:4], refs[4:]
        n_out = 7 if first else 13
        outs, scratch = refs[:n_out], refs[n_out:]
        f_out, g_t, gp_t, g_l, gp_l = outs[:5]
        fpad, acc_t, acc_l, sem_t, sem_out = scratch
        my_dp, my_t = me_ref[0], me_ref[1]
        for k in range(nb):
            for m in range(2):
                for y in range(2):
                    src = piece_refs[y].at[k] if m == 0 else piece_refs[2 + k].at[y]
                    for z in range(p.far):
                        row = pl.multiple_of(((z * 2 + y) ^ my_dp) * p.ra, 16)
                        pltpu.make_async_copy(
                            src.at[z], fpad.at[k, m, pl.ds(row, p.ra)], sem_t.at[k]
                        ).start()
        if first:
            acc_t[...] = jnp.zeros_like(acc_t)
            acc_l[...] = jnp.zeros_like(acc_l)
        else:
            acc_t_in, acc_l_in, n1t_, n1l_, c0, c1, c2, c3, vt, vl = rest_refs
            acc_t[...] = acc_t_in[...]
            acc_l[...] = acc_l_in[...]

        def gelu(u, g_ref, gp_ref, k):
            cdf = 0.5 + 0.5 * lax.erf(u * root)
            low = (u * cdf).astype(BF16)
            g_ref[k] = low
            dens = jnp.exp(u * u * -0.5) * (1.0 / math.sqrt(2.0 * math.pi))
            gp_ref[k] = (cdf + u * dens).astype(gp_ref.dtype)
            return low

        def block(k, carry):
            wait_for(fpad.at[k], sem_t.at[k])
            if not exact_t:
                for m in range(2):
                    fpad[k, m, pl.ds(0, p.wt)] = dot(spt[...], fpad[k, m]).astype(BF16)
            out_copy = pltpu.make_async_copy(
                fpad.at[k, :, pl.ds(0, p.wt)], f_out.at[k], sem_out
            )
            out_copy.start()
            own_t = (2 * k + core) ^ my_t
            g = gelu(dot(ht[...], fpad[k, 0, pl.ds(0, p.wt)]) + bt[own_t], g_t, gp_t, k)
            acc_t[...] += dot(g, fpad[k, 1, pl.ds(0, p.wt)], 1, 1)
            w = wl[k]
            up = w[:, 4 * p.cl : 4 * p.cl + p.hl]
            down = w[:, 4 * p.cl + p.hl : p.lay_cols]
            g = gelu(dot(hl[...], up) + bl[own_t], g_l, gp_l, k)
            acc_l[...] += dot(g, down, 1, 1)
            out_copy.wait()
            return carry

        lax.fori_loop(0, nb, block, 0)
        if first:
            outs[5][...] = acc_t[...]
            outs[6][...] = acc_l[...]
        else:
            out_tl, dr_t, dr_l, df_t, df_l, gv_t, gv_l, _ = outs[5:]
            cot = jnp.concatenate([ref[...] for ref in (c0, c1, c2, c3)], axis=0).astype(F32)
            for n1, acc, vec, begin, dr_ref, df_ref, gv in (
                (n1t_, acc_t, vt, 0, dr_t, df_t, gv_t),
                (n1l_, acc_l, vl, p.wt, dr_l, df_l, gv_l),
            ):
                width = n1.shape[1]
                ct = cot[:, begin : begin + width]
                h1 = n1[...] * vec[3:4] + vec[4:5]
                n2, inv2 = norm_parts(h1 + acc[...] + vec[5:6])
                out_tl[:, pl.ds(begin, width)] = (n2 * vec[6:7] + vec[7:8]).astype(BF16)
                dr = norm_back(ct, n2, inv2, vec[6:7])
                dr_ref[...] = dr
                df_ref[...] = dr.astype(BF16)
                gv[...] = jnp.zeros_like(gv)
                gv[5:6] = col_sum(dr)
                gv[6:7] = col_sum(ct * n2)
                gv[7:8] = col_sum(ct)
            outs[12][...] = jnp.zeros_like(outs[12])

    outs = [
        shape((nb, 2, p.wt, p.ht), BF16),
        shape((nb, rows, p.ht), BF16),
        shape((nb, rows, p.ht), BF16),
        shape((nb, rows, p.hl), BF16),
        shape((nb, rows, p.hl), BF16),
    ]
    if first:
        outs += [shape((rows, p.wt), F32), shape((rows, p.wl), F32)]
    else:
        outs += [
            shape((rows, p.wt + p.wl), BF16),
            shape((rows, p.wt), F32),
            shape((rows, p.wl), F32),
            shape((rows, p.wt), BF16),
            shape((rows, p.wl), BF16),
            shape((8, p.wt), F32),
            shape((8, p.wl), F32),
            shape((8, 128), F32),
        ]
    scratch = [
        pltpu.VMEM((nb, 2, padded_t, p.ht), BF16),
        pltpu.VMEM((rows, p.wt), F32),
        pltpu.VMEM((rows, p.wl), F32),
        pltpu.SemaphoreType.DMA((nb,)),
        pltpu.SemaphoreType.DMA,
    ]
    args = (me2, w_lay, h_t, h_l, bin_t, bin_l, spread_t, *rest_in, *pieces)
    return kernel_call(
        body,
        outs,
        [SM] + [VM] * (6 + n_rest) + [ANY] * 4,
        [ANY] + [VM] * (len(outs) - 1),
        scratch,
        args,
    )


def store_slots(p, staged, slot_of, my_dp, sem, slices):
    for z in range(p.far):
        for y in range(2):
            at = (z * 2 + y) ^ my_dp
            for dst, per, begin, count, off in slices:
                pltpu.make_async_copy(
                    staged.at[pl.ds(pl.multiple_of(at * per + begin, 16), count)],
                    slot_of(dst, y, z).at[pl.ds(off, count)],
                    sem,
                ).start()


def feed_backward(p, me2, f_all, w_lay, h_t, h_l, df_t, df_l, g_t, gp_t, g_l, gp_l, spread_t, prev, last):
    n_t, rows = p.n_t, p.rows
    padded_t = p.n_dp * p.ra
    exact_t = p.ra == p.d_own
    blocks = [t for t in range(n_t) if t % 2 == (0 if last else 1)]

    def body(*refs):
        (me_ref, f_any, wl, ht, hl, dft, dfl, gt, gpt, gl, gpl, spt), refs = refs[:12], refs[12:]
        if last:
            (pt, pl_, drt, drl, n1t, i1t, n1l, i1l, vt, vl), refs = refs[:10], refs[10:]
            n_out = 11
        else:
            n_out = 7
        outs, scratch = refs[:n_out], refs[n_out:]
        low, high, gfl, dbt, dbl = outs[:5]
        f_in, staged, acc_t, acc_l, sem_in, sem_out = scratch
        my_dp, my_t = me_ref[0], me_ref[1]
        for k, t in enumerate(blocks):
            pltpu.make_async_copy(f_any.at[k], f_in.at[k], sem_in.at[k]).start()
        dfT, hT = dft[...].T, ht[...].T
        dfTl, hTl = dfl[...].T, hl[...].T
        if last:
            acc_t[...] = pt[...]
            acc_l[...] = pl_[...]
        else:
            acc_t[...] = jnp.zeros_like(acc_t)
            acc_l[...] = jnp.zeros_like(acc_l)
        for k, t in enumerate(blocks):
            wait_for(f_in.at[k], sem_in.at[k])
            du = dot(dft[...], f_in[k, 1]) * gpt[k].astype(F32)
            dbt[k] = col_sum(du)
            du_low = du.astype(BF16)
            grads = (dot(hT, du_low).astype(BF16), dot(dfT, gt[k]).astype(BF16))
            for m in range(2):
                value = grads[m]
                if not exact_t:
                    value = dot(spt[...], value, 0, 0).astype(BF16)
                staged[k, m] = value
                x = t // 2
                if m == 0:
                    store_slots(p, staged.at[k, m], lambda d, y, z: low.at[x, y, z], my_dp, sem_out, [(0, p.ra, 0, p.ra, 0)])
                else:
                    store_slots(p, staged.at[k, m], lambda d, y, z: high.at[y, x, z], my_dp, sem_out, [(0, p.ra, 0, p.ra, 0)])
            acc_t[...] += dot(du_low, f_in[k, 0], 1, 1)
            w = wl[k]
            up = w[:, 4 * p.cl : 4 * p.cl + p.hl]
            down = w[:, 4 * p.cl + p.hl : p.lay_cols]
            du = dot(dfl[...], down) * gpl[k].astype(F32)
            dbl[k] = col_sum(du)
            du_low = du.astype(BF16)
            gfl[k, :, pl.ds(0, p.hl)] = dot(hTl, du_low).astype(BF16)
            gfl[k, :, pl.ds(p.hl, p.hl)] = dot(dfTl, gl[k]).astype(BF16)
            acc_l[...] += dot(du_low, up, 1, 1)
        if last:
            dr1t, dr1l, dat, dal, gvt, gvl = outs[5:]
            for dr, acc, n1, i1, vec, o, low_o, gv in (
                (drt, acc_t, n1t, i1t, vt, dr1t, dat, gvt),
                (drl, acc_l, n1l, i1l, vl, dr1l, dal, gvl),
            ):
                dh = dr[...] + acc[...]
                n = n1[...]
                dr1 = norm_back(dh, n, i1[...], vec[3:4])
                o[...] = dr1
                low_o[...] = dr1.astype(BF16)
                gv[...] = jnp.zeros_like(gv)
                gv[2:3] = col_sum(dr1)
                gv[3:4] = col_sum(dh * n)
                gv[4:5] = col_sum(dh)
        else:
            outs[5][...] = acc_t[...]
            outs[6][...] = acc_l[...]
        wait_for(staged, sem_out)

    nb = len(blocks)
    outs = [
        shape((2, 2, p.far, p.ra, p.ht), BF16),
        shape((2, 2, p.far, p.ra, p.ht), BF16),
        shape((nb, p.wl, 2 * p.hl), BF16),
        shape((nb, 1, p.ht), F32),
        shape((nb, 1, p.hl), F32),
    ]
    args = [me2, f_all, w_lay, h_t, h_l, df_t, df_l, g_t, gp_t, g_l, gp_l, spread_t]
    if last:
        args += list(prev)
        outs += [
            shape((rows, p.wt), F32),
            shape((rows, p.wl), F32),
            shape((rows, p.wt), BF16),
            shape((rows, p.wl), BF16),
            shape((8, p.wt), F32),
            shape((8, p.wl), F32),
        ]
    else:
        outs += [shape((rows, p.wt), F32), shape((rows, p.wl), F32)]
    scratch = [
        pltpu.VMEM((nb, 2, p.wt, p.ht), BF16),
        pltpu.VMEM((nb, 2, padded_t, p.ht), BF16),
        pltpu.VMEM((rows, p.wt), F32),
        pltpu.VMEM((rows, p.wl), F32),
        pltpu.SemaphoreType.DMA((nb,)),
        pltpu.SemaphoreType.DMA,
    ]
    specs = [SM, ANY] + [VM] * (len(args) - 2)
    return kernel_call(
        body, outs, specs, [ANY, ANY] + [VM] * (len(outs) - 2), scratch, args
    )


def attend_backward(p, me2, w_all, w_lay, qkv, ctx, lse, x_low, lay_low, ints, ints_t, da_t, da_l, gfl, spread_t, spread_l, prev, last):
    n_t, rows, hw, nh = p.n_t, p.rows, p.hw, p.heads
    padded_t, padded_l = p.n_dp * p.ra, p.n_dp * p.rl
    exact_t = p.ra == p.d_own
    blocks = [t for t in range(n_t) if t % 2 == (0 if last else 1)]
    nb = len(blocks)

    def body(*refs):
        (me_ref, w_any, wl_ref, qkv_r, ctx_r, lse_r, xl, ll, ir, itr, dat, dal, gfl_r, spt, spl), refs = refs[:15], refs[15:]
        if last:
            (pt, pl_, dr1t, dr1l), refs = refs[:4], refs[4:]
        outs, scratch = refs[:8], refs[8:]
        low, high, gbq, gbv, gbql, gbvl, out_a, out_b = outs
        w_in, staged, staged_l, acc_t, acc_l, dctx, ctx_s, ctx_l, dp_t, dp_l, sem_in, sem_out = scratch
        my_dp = me_ref[0]
        for k, t in enumerate(blocks):
            pltpu.make_async_copy(w_any.at[k], w_in.at[k], sem_in.at[k]).start()
        xT, lT = xl[...].T, ll[...].T
        daT, dalT = dat[...].T, dal[...].T
        seg_col, seg_row = ir[:, 0:1], itr[0:1, :]
        if last:
            acc_t[...] = pt[...]
            acc_l[...] = pl_[...]
        else:
            acc_t[...] = jnp.zeros_like(acc_t)
            acc_l[...] = jnp.zeros_like(acc_l)
        gbq[...] = jnp.zeros_like(gbq)
        gbv[...] = jnp.zeros_like(gbv)
        gbql[...] = jnp.zeros_like(gbql)
        gbvl[...] = jnp.zeros_like(gbvl)
        for k, t in enumerate(blocks):
            wait_for(w_in.at[k], sem_in.at[k])
            w = w_in[k]
            wl = wl_ref[k]
            d_t = dot(dat[...], w[:, 3 * p.ct :]).T
            d_l = dot(dal[...], wl[:, 3 * p.cl : 4 * p.cl]).T
            for h in range(nh):
                dctx[h, pl.ds(0, HD)] = d_t[h * HD : (h + 1) * HD].astype(BF16)
                dctx[h, pl.ds(HD, LHD)] = d_l[h * LHD : (h + 1) * LHD].astype(BF16)
                ctx_s[pl.ds(h * HD, HD)] = ctx_r[k, h, pl.ds(0, HD)]
                ctx_l[pl.ds(h * LHD, LHD)] = ctx_r[k, h, pl.ds(HD, LHD)]

            for h in range(nh):
                q, key, val = qkv_r[k, h], qkv_r[k, nh + h], qkv_r[k, 2 * nh + h]
                dc = dctx[h]
                scores = dot(key, q, 0, 0)
                probs = jnp.exp(
                    jnp.where(seg_col == seg_row, scores, NEG_FILL) - lse_r[k, pl.ds(h, 1), :]
                )
                low_p = probs.astype(BF16)
                prod = dc.astype(F32) * ctx_r[k, h].astype(F32)
                sum_lay = jnp.sum(prod[HD:], axis=0, keepdims=True)
                sum_all = jnp.sum(prod[:HD], axis=0, keepdims=True) + sum_lay
                dz_all = probs * (dot(val, dc, 0, 0) - sum_all)
                dz_lay = probs * (dot(val[HD:], dc[HD:], 0, 0) - sum_lay)
                ds_t, ds_l = dz_all.astype(BF16), dz_lay.astype(BF16)
                dv = dot(dc, low_p, 1, 1)
                dq_t = dot(key[:HD], ds_t) * (1.0 / math.sqrt(HD))
                dq_l = dot(key[HD:], ds_l) * (1.0 / math.sqrt(LHD))
                dk_t = dot(q[:HD], ds_t, 1, 1)
                dk_l = dot(q[HD:], ds_l, 1, 1)
                for c, (top, bot) in enumerate(((dq_t, dq_l), (dk_t, dk_l), (dv[:HD], dv[HD:]))):
                    dp_t[pl.ds(c * p.ct + h * HD, HD)] = top.astype(BF16)
                    dp_l[pl.ds(c * p.cl + h * LHD, LHD)] = bot.astype(BF16)
                    if c != 1:
                        dst, dst_l = (gbq, gbql) if c == 0 else (gbv, gbvl)
                        dst[k, pl.ds(h * HD, HD)] = jnp.sum(top, axis=1, keepdims=True)
                        dst_l[k, pl.ds(h * LHD, LHD)] = jnp.sum(bot, axis=1, keepdims=True)
            acc_t[...] += dot(w[:, : 3 * p.ct], dp_t[...])
            acc_l[...] += dot(wl[:, : 3 * p.cl], dp_l[...])
            grad = jnp.concatenate(
                [dot(xT, dp_t[...], 1, 1), dot(daT, ctx_s[...], 1, 1)], axis=1
            ).astype(BF16)
            if not exact_t:
                grad = dot(spt[...], grad, 0, 0).astype(BF16)
            staged[k] = grad
            fill = p.cols - p.lay_cols
            grad_l = jnp.concatenate(
                [
                    dot(lT, dp_l[...], 1, 1),
                    dot(dalT, ctx_l[...], 1, 1),
                    gfl_r[k].astype(F32),
                    jnp.zeros((p.wl, fill), F32),
                ],
                axis=1,
            ).astype(BF16)
            staged_l[k] = dot(spl[...], grad_l, 0, 0).astype(BF16)
            x = t // 2
            rest = p.ra - p.half_a
            slot = lambda d, y, z: low.at[x, y, z] if d == 0 else high.at[y, x, z]
            slices = [(0, p.ra, 0, p.half_a, 0)]
            if rest:
                slices.append((1, p.ra, p.half_a, rest, 0))
            store_slots(p, staged.at[k], slot, my_dp, sem_out.at[0], slices)
            store_slots(p, staged_l.at[k], slot, my_dp, sem_out.at[1], [(1, p.rl, 0, p.rl, rest)])
        if last:
            gt = dr1t[...] + acc_t[...].T
            gl = dr1l[...] + acc_l[...].T
            out_a[:, pl.ds(0, p.wt)] = gt.astype(BF16)
            out_a[:, pl.ds(p.wt, p.wl)] = gl.astype(BF16)
            half = p.wl // 2
            bins = out_b.shape[0]
            levels = lax.broadcasted_iota(jnp.int32, (bins, 1), 0).astype(F32)
            for m in range(2):
                row = itr[1 + 2 * m : 2 + 2 * m, :] * 128.0 + itr[2 + 2 * m : 3 + 2 * m, :]
                hot = (levels == row).astype(F32).astype(BF16)
                part = gl[:, m * half : (m + 1) * half]
                top = part.astype(BF16)
                rest_part = (part - top.astype(F32)).astype(BF16)
                both = dot(hot, jnp.concatenate([top, rest_part], axis=1))
                out_b[:, pl.ds(m * half, half)] = both[:, :half] + both[:, half:]
        else:
            out_a[...] = acc_t[...]
            out_b[...] = acc_l[...]
        wait_for(staged, sem_out.at[0])
        wait_for(staged_l, sem_out.at[1])

    half_b = p.ra + p.rl - p.half_a
    outs = [
        shape((2, 2, p.far, p.half_a, p.cols), BF16),
        shape((2, 2, p.far, half_b, p.cols), BF16),
        shape((nb, p.ct, 1), F32),
        shape((nb, p.ct, 1), F32),
        shape((nb, p.cl, 1), F32),
        shape((nb, p.cl, 1), F32),
    ]
    args = [me2, w_all, w_lay, qkv, ctx, lse, x_low, lay_low, ints, ints_t, da_t, da_l, gfl, spread_t, spread_l]
    if last:
        *prev, bins = prev
        args += list(prev)
        outs += [shape((rows, p.wt + p.wl), BF16), shape((bins, p.wl), F32)]
    else:
        outs += [shape((p.wt, rows), F32), shape((p.wl, rows), F32)]
    scratch = [
        pltpu.VMEM((nb, p.wt, p.cols), BF16),
        pltpu.VMEM((nb, padded_t, p.cols), BF16),
        pltpu.VMEM((nb, padded_l, p.cols), BF16),
        pltpu.VMEM((p.wt, rows), F32),
        pltpu.VMEM((p.wl, rows), F32),
        pltpu.VMEM((nh, hw, rows), BF16),
        pltpu.VMEM((p.ct, rows), BF16),
        pltpu.VMEM((p.cl, rows), BF16),
        pltpu.VMEM((3 * p.ct, rows), BF16),
        pltpu.VMEM((3 * p.cl, rows), BF16),
        pltpu.SemaphoreType.DMA((nb,)),
        pltpu.SemaphoreType.DMA((2,)),
    ]
    specs = [SM, ANY] + [VM] * (len(args) - 2)
    return kernel_call(
        body, outs, specs, [ANY, ANY] + [VM] * (len(outs) - 2), scratch, args
    )


def tie(*groups):
    leaves, tree = jax.tree.flatten(groups)
    return jax.tree.unflatten(tree, lax.optimization_barrier(leaves))


def line_of(shard, total):
    return [shard] + [xor_send(shard, total, 8 * r) for r in range(1, total // 8)]


def halves_of(line, half):
    low = jnp.stack([member[:half] for member in line])
    high = jnp.stack([member[half:] for member in line])
    return low, high


def add_low(mine, theirs):
    return to_low(mine.astype(F32) + theirs.astype(F32))


def reduce_second(mine, got):
    send = [add_low(mine[k][1], got[k][1]) for k in range(2)]
    keep = [add_low(mine[k][0], got[k][0]) for k in range(2)]
    return send, keep


def reduce_last(keep, got, total):
    far = total // 8
    line = [
        jnp.concatenate([add_low(keep[k][z], got[k][z]) for k in range(2)], axis=0)
        for z in range(far)
    ]
    out = line[0].astype(F32)
    for z in range(1, far):
        out = out + xor_send(line[z], total, 8 * z).astype(F32)
    return out


def sum_everywhere(values, total):
    pair = values + xor_send(values, total, 1)
    chip = pair + xor_send(pair, total, 2)
    plane = chip + xor_send(chip, total, 4)
    distance = 8
    while distance < total:
        if 2 * distance < total:
            near, far, both = (xor_send(plane, total, distance * k) for k in (1, 2, 3))
            plane = (plane + near) + (far + both)
            distance = distance * 4
        else:
            plane = plane + xor_send(plane, total, distance)
            distance = distance * 2
    return plane


def reduce_small(values, total):
    me = lax.axis_index("dp") * lax.axis_size("tensor") + lax.axis_index("tensor")
    distance = 1
    sizes = []
    while distance < total:
        half = values.shape[0] // 2
        bit = (me // distance) % 2
        mine = lax.dynamic_slice_in_dim(values, bit * half, half)
        other = lax.dynamic_slice_in_dim(values, (1 - bit) * half, half)
        values = mine + xor_send(to_low(other), total, distance).astype(F32)
        sizes.append(distance)
        distance = distance * 2
    square_sum = jnp.sum(values * values)
    for distance in reversed(sizes):
        bit = (me // distance) % 2
        other = xor_send(values, total, distance)
        values = jnp.where(
            bit == 0, jnp.concatenate([values, other]), jnp.concatenate([other, values])
        )
    return values, square_sum


def on_device(
    text_in,
    layout_in,
    segment_ids,
    box_bins,
    text_cot,
    layout_cot,
    attend_text,
    attend_text_mean,
    attend_text_square,
    feed_text,
    feed_text_mean,
    feed_text_square,
    attend_layout,
    attend_layout_mean,
    attend_layout_square,
    feed_layout,
    feed_layout_mean,
    feed_layout_square,
    vectors,
    vectors_mean,
    vectors_square,
    tables,
    tables_mean,
    tables_square,
):
    n_dp, n_t = lax.axis_size("dp"), lax.axis_size("tensor")
    total = n_dp * n_t
    t_pos = lax.axis_index("tensor")
    pages, quarter, wt = text_in.shape
    wl = layout_in.shape[1] // quarter
    d_own, dl_own = attend_text.shape[0], attend_layout.shape[0]
    ct, cl = attend_text.shape[2], attend_layout.shape[2]
    ht, hl = feed_text.shape[2], feed_layout.shape[2]


    p = Plan(n_dp, n_t, quarter, wt, wl, ct, cl, ht, hl)
    me2 = jnp.stack([lax.axis_index("dp"), t_pos]).astype(jnp.int32)
    lay_cols = p.lay_cols

    def pad_rows(values, count):
        return jnp.pad(values, ((0, count - values.shape[0]), (0, 0)))

    lay_pack = jnp.concatenate(
        [
            to_low(attend_layout).reshape(dl_own, 4 * cl),
            to_low(feed_layout).reshape(dl_own, 2 * hl),
        ],
        axis=1,
    )
    lay_pack = jnp.pad(lay_pack, ((0, p.rl - dl_own), (0, p.cols - lay_cols)))
    attend_pack = jnp.concatenate(
        [pad_rows(to_low(attend_text).reshape(d_own, p.cols), p.ra), lay_pack]
    )
    low_feed = to_low(feed_text)
    feed_pack = jnp.concatenate(
        [pad_rows(low_feed[:, 0], p.ra), pad_rows(low_feed[:, 1], p.ra)]
    )
    bins = box_bins.reshape(pages, quarter, 2)
    digits = jnp.stack(
        [segment_ids, bins[..., 0] // 128, bins[..., 0] % 128, bins[..., 1] // 128, bins[..., 1] % 128],
        axis=-1,
    )
    packed_in = jnp.concatenate(
        [
            text_in,
            layout_in.reshape(pages, quarter, wl),
            jnp.pad(to_low(digits), ((0, 0), (0, 0), (0, 59))),
        ],
        axis=2,
    )
    packed_cot = jnp.concatenate([text_cot, layout_cot.reshape(pages, quarter, wl)], axis=2)

    def page_of(values):
        take = lambda r: lax.dynamic_index_in_dim(values, t_pos ^ r, 0, keepdims=False)
        return [take(0)] + [xor_send(take(r), total, r) for r in range(1, n_t)]

    def send_rows(page):
        blocks = page.reshape(n_t, quarter, page.shape[-1])
        return [blocks[0]] + [xor_send(blocks[r], total, r) for r in range(1, n_t)]

    def pages_of(blocks):
        out = jnp.zeros((n_t,) + blocks[0].shape, blocks[0].dtype)
        for r in range(n_t):
            out = lax.dynamic_update_slice(out, blocks[r][None], (t_pos ^ r, 0, 0))
        return out

    parts = split_vectors(vectors, [wt, wl], [n_t * ht, n_t * hl])
    biases, vecs, bins_in = [], [], []
    for s, width in ((0, ct), (1, cl)):
        vec, hidden = parts[s]
        biases.append(
            jnp.concatenate(
                [
                    vec[0].reshape(n_t, 1, width),
                    jnp.zeros((n_t, 1, width), F32),
                    vec[1].reshape(n_t, 1, width),
                ],
                axis=2,
            )
        )
        vecs.append(jnp.stack(vec))
        bins_in.append(hidden.reshape(n_t, 1, -1))
    table_rows = to_low(tables.reshape(-1, wl))
    spread_t = p.spread(d_own, p.ra) if p.ra != d_own else jnp.zeros((16, 128), BF16)
    spread_l = p.spread(dl_own, p.rl)

    send = lambda values, distance: xor_send(values, total, distance)

    line_a = line_of(attend_pack, total)
    xin = page_of(packed_in)
    line_a, feed_pack = tie(line_a, feed_pack)
    line_f = line_of(feed_pack, total)
    low, high = halves_of(line_a, p.half_a)
    low0, high0 = jnp.stack([low, send(low, 2)]), jnp.stack([high, send(high, 4)])
    low4, high2 = send(low0, 4), send(high0, 2)
    low1, high1 = send(low0, 1), send(high0, 1)
    pieces_a0 = [low0, low4, high0, high2]
    (low4, high2), line_f = tie((low4, high2), line_f)
    low5, high3 = send(low4, 1), send(high2, 1)
    flow, fhigh = halves_of(line_f, p.ra)
    flow_x, fhigh_y = send(flow, 2), send(fhigh, 4)
    xin, flow, fhigh = tie(xin, flow, fhigh)
    att_fix = (biases[0], biases[1], vecs[0], vecs[1], spread_t, spread_l)
    (w_all0, w_lay0, qkv0, ctx0, lse0, *row_state) = attend_forward(
        p, me2, 0, (*xin, table_rows), *att_fix, pieces_a0
    )
    row_state, (flow_x, fhigh_y) = tie(row_state, (flow_x, fhigh_y))
    flow0, fhigh0 = jnp.stack([flow, flow_x]), jnp.stack([fhigh, fhigh_y])
    flow4, fhigh2 = send(flow0, 4), send(fhigh0, 2)
    flow1, fhigh1 = send(flow0, 1), send(fhigh0, 1)
    row_state, flow0, fhigh0 = tie(row_state, flow0, fhigh0)
    (w_all1, w_lay1, qkv1, ctx1, lse1, n1t, i1t, h_t, n1l, i1l, h_l) = attend_forward(
        p, me2, 1, row_state, *att_fix, [low1, low5, high1, high3]
    )
    x_low, lay_low, _, ints, ints_t = row_state[:5]
    (flow4, fhigh2), h_t, packed_cot = tie((flow4, fhigh2), h_t, packed_cot)
    flow5, fhigh3 = send(flow4, 1), send(fhigh2, 1)
    cots = page_of(packed_cot)
    (f_all0, g_t0, gp_t0, g_l0, gp_l0, acc_t, acc_l) = feed_forward(
        p, me2, 0, [flow0, flow4, fhigh0, fhigh2], w_lay0, h_t, h_l, bins_in[0], bins_in[1], spread_t, ()
    )
    acc_t, flow5, fhigh3, cots = tie(acc_t, flow5, fhigh3, cots)
    (f_all1, g_t1, gp_t1, g_l1, gp_l1, out_rows, dr_t, dr_l, df_t, df_l, gv2t, gv2l, _) = feed_forward(
        p, me2, 1, [flow1, flow5, fhigh1, fhigh3], w_lay1, h_t, h_l, bins_in[0], bins_in[1], spread_t,
        (acc_t, acc_l, n1t, n1l, *cots, vecs[0], vecs[1]),
    )
    rows_out = send_rows(out_rows)
    (gf_low1, gf_high1, gfl1, dbt1, dbl1, acc_t, acc_l) = feed_backward(
        p, me2, f_all1, w_lay1, h_t, h_l, df_t, df_l, g_t1, gp_t1, g_l1, gp_l1, spread_t, None, False
    )
    acc_t, rows_out = tie(acc_t, rows_out)
    got = [send(gf_low1, 1), send(gf_high1, 1)]
    (gf_low0, gf_high0, gfl0, dbt0, dbl0, dr1t, dr1l, da_t, da_l, gv1t, gv1l) = feed_backward(
        p, me2, f_all0, w_lay0, h_t, h_l, df_t, df_l, g_t0, gp_t0, g_l0, gp_l0, spread_t,
        (acc_t, acc_l, dr_t, dr_l, n1t, i1t, n1l, i1l, vecs[0], vecs[1]), True
    )
    next_f, keep_f = reduce_second((gf_low0, gf_high0), got)
    next_f, keep_f, da_t = tie(next_f, keep_f, da_t)
    got_f = [send(next_f[0], 2), send(next_f[1], 4)]
    (ga_low1, ga_high1, bq1, bv1, bql1, bvl1, acc_t, acc_l) = attend_backward(
        p, me2, w_all1, w_lay1, qkv1, ctx1, lse1, x_low, lay_low, ints, ints_t, da_t, da_l,
        gfl1, spread_t, spread_l, None, False
    )
    got_f, acc_t = tie(got_f, acc_t)
    got = [send(ga_low1, 1), send(ga_high1, 1)]
    next_f, keep_f = reduce_second(keep_f, got_f)
    next_f, keep_f, acc_t = tie(next_f, keep_f, acc_t)
    got_f = [send(next_f[0], 4), send(next_f[1], 2)]
    (ga_low0, ga_high0, bq0, bv0, bql0, bvl0, grad_rows, table_grad) = attend_backward(
        p, me2, w_all0, w_lay0, qkv0, ctx0, lse0, x_low, lay_low, ints, ints_t, da_t, da_l,
        gfl0, spread_t, spread_l, (acc_t, acc_l, dr1t, dr1l, table_rows.shape[0]), True
    )
    got_f, got, grad_rows, table_grad, bq0 = tie(got_f, got, grad_rows, table_grad, bq0)
    next_a, keep_a = reduce_second((ga_low0, ga_high0), got)
    got_a = [send(next_a[0], 2), send(next_a[1], 4)]
    feed_sum = reduce_last(keep_f, got_f, total)
    next_a, keep_a = reduce_second(keep_a, got_a)
    got_a = [send(next_a[0], 4), send(next_a[1], 2)]
    attend_sum = reduce_last(keep_a, got_a, total)
    rows_grad = send_rows(grad_rows)

    def by_block(odd, even):
        both = jnp.stack([even[0], odd[0], even[1], odd[1]]).reshape(n_t, -1)
        order = jnp.arange(n_t) ^ t_pos
        hot = order[:, None] == jnp.arange(n_t)[None, :]
        return jnp.sum(jnp.where(hot[:, :, None], both[None], 0.0), axis=1).reshape(-1)

    gv_t, gv_l = gv2t + gv1t, gv2l + gv1l
    vector_grad = jnp.concatenate(
        [
            by_block(bq1, bq0),
            by_block(bv1, bv0),
            gv_t[2:].reshape(-1),
            by_block(dbt1, dbt0),
            by_block(bql1, bql0),
            by_block(bvl1, bvl0),
            gv_l[2:].reshape(-1),
            by_block(dbl1, dbl0),
        ]
    )
    small = jnp.concatenate([table_grad.reshape(-1), vector_grad])
    n_table, n_small = table_grad.size, small.shape[0]
    small_rows = round_up(-(-n_small // 128), 4 * total)
    small = jnp.pad(small, (0, small_rows * 128 - n_small)).reshape(small_rows, 128)
    small, small_sq = reduce_small(small, total)
    small = small.reshape(-1)
    table_grad, vector_grad = small[:n_table], small[n_table:n_small]
    shared_sq = sum_everywhere(
        (jnp.sum(feed_sum * feed_sum) + jnp.sum(attend_sum * attend_sum) + small_sq).reshape(1, 1),
        total,
    )[0, 0]
    clip_norm = jnp.sqrt(shared_sq)
    factor = jnp.minimum(1.0, CLIP_NORM / (clip_norm + 1e-06))
    lay_sum = attend_sum[p.ra : p.ra + dl_own]
    states = [
        (
            attend_text,
            attend_text_mean,
            attend_text_square,
            attend_sum[:d_own].reshape(d_own, 4, ct),
            WEIGHT_DECAY,
        ),
        (
            feed_text,
            feed_text_mean,
            feed_text_square,
            jnp.stack([feed_sum[:d_own], feed_sum[p.ra : p.ra + d_own]], axis=1),
            WEIGHT_DECAY,
        ),
        (
            attend_layout,
            attend_layout_mean,
            attend_layout_square,
            lay_sum[:, : 4 * cl].reshape(dl_own, 4, cl),
            WEIGHT_DECAY,
        ),
        (
            feed_layout,
            feed_layout_mean,
            feed_layout_square,
            lay_sum[:, 4 * cl : lay_cols].reshape(dl_own, 2, hl),
            WEIGHT_DECAY,
        ),
        (vectors, vectors_mean, vectors_square, vector_grad, 0.0),
        (tables, tables_mean, tables_square, table_grad, 0.0),
    ]
    updated = []
    for k in range(6):
        updated.extend(
            adamw_step(
                states[k][0],
                states[k][1],
                states[k][2],
                states[k][3] * factor,
                states[k][4],
                LEARN_RATES[k],
            )
        )
    rows_out, rows_grad = pages_of(rows_out), pages_of(rows_grad)
    return (
        rows_out[:, :, :wt],
        rows_out[:, :, wt:].reshape(pages, quarter * wl),
        rows_grad[:, :, :wt].astype(F32),
        rows_grad[:, :, wt:].astype(F32).reshape(pages, quarter * wl),
        *updated,
        clip_norm,
    )


def solution(mesh):
    rows3, rows2, cols3 = P("dp", "tensor", None), P("dp", "tensor"), P("dp", None, "tensor")
    in_specs = (rows3, rows2, rows2, rows2, rows3, rows2) + (cols3,) * 12 + (P(),) * 6
    out_specs = (rows3, rows2, rows3, rows2) + (cols3,) * 12 + (P(),) * 7
    return jax.shard_map(
        on_device, mesh=mesh, in_specs=in_specs, out_specs=out_specs, check_vma=False
    )
```

time: 851 us -> 435 us (0.51)
  local copies, waits for them, and re-layouts: 234 us -> 41.7 us
  matrix products: 142 us -> 0 us
  other arithmetic: 119 us -> 51.4 us
  Pallas kernels: 76.7 us -> 118 us
  waiting for transfers between devices: 173 us -> 134 us
    dot_general x38 -> x0, matrix products: 124 us -> none  [the longest x2 23 us: on_device(): gate = jnp.dot(h1_low, feeds[s][:, 0], preferred_element_type=F32) + bias_in]
    reshape x18 -> x20, local copies, waits for them, and re-layouts: 84.1 us -> 6.04 us  [the longest x1 1.07 us: on_device(): rows_grad[:, :, wt:].astype(F32).reshape(pages, quarter * wl)]
    pallas_call x4 -> x8, Pallas kernels: 76.7 us -> 118 us  [kernel_call(): pl.pallas_call(body, out_shape=outs, in_specs=in_specs, out_specs=out_spe...]
    ppermute x81 -> x68, waiting for transfers between devices: 173 us -> 134 us  [xor_send(): return lax.ppermute(values, AXES, [(i, i ^ distance) for i in range(total)])]
    another operation x14 -> x19, local copies, waits for them, and re-layouts: 36 us -> 1.71 us  [the longest x10 1.3 us: on_device(): vecs.append(jnp.stack(vec))]
    another operation x13 -> x12, other arithmetic: 29.2 us -> 5.24 us  [the longest x2 2.37 us: on_device(): flow0, fhigh0 = (jnp.stack([flow, flow_x]), jnp.stack([fhigh, fhigh_y]))]
    transpose x6 -> x0, other arithmetic: 18.5 us -> none  [the longest x3 12.7 us: by_owner(): grad.reshape(n_dp, own, grad.shape[1], n_t, cols).transpose(0, 3, 1, 2, 4)]
    sub x1 -> x0, matrix products: 17.8 us -> none  [softmax_back(): d_probs - jnp.sum(probs_full * d_probs, axis=-1, keepdims=True)]
  transfers between devices with their start and end apart: 81 -> 68, of which waited for: 30 -> 33; matrix products, arithmetic and copies ran while one was open for 37% -> 14% of each run, Pallas kernels for 7% -> 24%
where the time goes in v2:
time: 435 us; the launch traced here: 429 us
  waiting for transfers between devices  134 us (31%)
  Pallas kernels  118 us (27%)
  starting transfers between devices  75.4 us (17%)
  other arithmetic  51.4 us (12%)
  local copies, waits for them, and re-layouts  41.7 us (10%)
  between operations  9.4 us (2%)
    ppermute x68, waiting for transfers between devices, xor_send(): return lax.ppermute(values, AXES, [(i, i ^ distance) for i in range(total)])  134 us
    pallas_call x8, Pallas kernels, kernel_call(): pl.pallas_call(body, out_shape=outs, in_specs=in_specs, out_specs=out_spe...  118 us
    ppermute x68, starting transfers between devices, xor_send(): return lax.ppermute(values, AXES, [(i, i ^ distance) for i in range(total)])  75.4 us
    convert_element_type x16, other arithmetic, to_low(): return values.astype(BF16)  24.1 us
    slice x28, local copies, waits for them, and re-layouts, by_block(): both = jnp.stack([even[0], odd[0], even[1], odd[1]]).reshape(n_t, -1)  11.2 us
    unnamed x112, local copies, waits for them, and re-layouts  9.78 us
  transfers between devices with their start and end apart: 68, of which 33 were waited for; matrix products, arithmetic and copies ran while one was open for 14% of the time, Pallas kernels for 24%

profile of v2, /device:TPU:0, one launch (start us, length us, event | category | flops | bytes accessed | tf_op | source)
XLA Modules:
  0.0 429.1 jit_solution(11535741874518831283)
XLA Ops:
  10.2 5.2 %collective-permute-done.3 = bf16[128,768]{1,0:T(8,128)(2,1)S(1)} collective-permute-done((bf16[128,768]{1,0:T(8,128)(2,1)S(1)}, bf16[128,768]{1,0:T(8,128)(2,1)S(1)}, u32[]{:S(2)}, u32[]{:S(2)}) %collective-permute-start.3) | collective-permute-done | bytes 196640 | tf_op jit(solution)/shard_map/ppermute | solution.py:34
  15.4 8.8 %collective-permute-done.4 = bf16[128,768]{1,0:T(8,128)(2,1)S(1)} collective-permute-done((bf16[128,768]{1,0:T(8,128)(2,1)S(1)}, bf16[128,768]{1,0:T(8,128)(2,1)S(1)}, u32[]{:S(2)}, u32[]{:S(2)}) %collective-permute-start.4) | collective-permute-done | bytes 196640 | tf_op jit(solution)/shard_map/ppermute | solution.py:34
  40.1 4.7 %collective-permute-start.10 = (bf16[192,768]{1,0:T(8,128)(2,1)S(1)}, bf16[192,768]{1,0:T(8,128)(2,1)S(1)}, u32[]{:S(2)}, u32[]{:S(2)}) collective-permute-start(bf16[192,768]{1,0:T(8,128)(2,1)S(1)} %pad_maximum_fusion.9), channel_id=1, source_target_pairs={{0,8},{1,9},{2,10},{3,11},{4,12},{5,13},{6,14},{7,15},{8,0},{9,1},... | collective-permute-start | bytes 884744 | tf_op jit(solution)/shard_map/ppermute | solution.py:34
  48.0 5.3 %collective-permute-done.10 = bf16[192,768]{1,0:T(8,128)(2,1)S(1)} collective-permute-done((bf16[192,768]{1,0:T(8,128)(2,1)S(1)}, bf16[192,768]{1,0:T(8,128)(2,1)S(1)}, u32[]{:S(2)}, u32[]{:S(2)}) %collective-permute-start.10) | collective-permute-done | bytes 294944 | tf_op jit(solution)/shard_map/ppermute | solution.py:34
  53.3 14.1 %collective-permute-done.11 = bf16[192,768]{1,0:T(8,128)(2,1)S(1)} collective-permute-done((bf16[192,768]{1,0:T(8,128)(2,1)S(1)}, bf16[192,768]{1,0:T(8,128)(2,1)S(1)}, u32[]{:S(2)}, u32[]{:S(2)}) %collective-permute-start.11) | collective-permute-done | bytes 294944 | tf_op jit(solution)/shard_map/ppermute | solution.py:34
  80.2 4.5 %collective-permute-done.14 = bf16[4,96,768]{2,1,0:T(8,128)(2,1)} collective-permute-done((bf16[4,96,768]{2,1,0:T(8,128)(2,1)S(1)}, bf16[4,96,768]{2,1,0:T(8,128)(2,1)}, u32[]{:S(2)}, u32[]{:S(2)}) %collective-permute-start.14) | collective-permute-done | bytes 589856 | tf_op jit(solution)/shard_map/ppermute | solution.py:34
  85.9 13.9 %shard_map.407 = (bf16[2,768,768]{2,1,0:T(8,128)(2,1)}, bf16[2,192,768]{2,1,0:T(8,128)(2,1)}, bf16[2,9,80,512]{3,2,1,0:T(8,128)(2,1)}, bf16[2,3,80,512]{3,2,1,0:...) custom-call(s32[2]{0:T(128)} %pad_add_fusion.refs_0_, ...), custom_call_target="tpu_custom_call" | custom-call | flops 10000000000 | bytes 1048576 | tf_op jit(solution)/shard_map/pallas_call | solution.py:118
  106.3 13.6 %shard_map.408 = (bf16[2,768,768]{2,1,0:T(8,128)(2,1)}, bf16[2,192,768]{2,1,0:T(8,128)(2,1)}, bf16[2,9,80,512]{3,2,1,0:T(8,128)(2,1)}, bf16[2,3,80,512]{3,2,1,0:...) custom-call(s32[2]{0:T(128)} %pad_add_fusion.refs_0_, ...), custom_call_target="tpu_custom_call" | custom-call | flops 10000000000 | bytes 1048576 | tf_op jit(solution)/shard_map/pallas_call | solution.py:118
  120.0 9.9 %collective-permute-done.20.refs_10_ = bf16[2,4,96,768]{3,2,1,0:T(8,128)(2,1)} collective-permute-done((bf16[2,4,96,768]{3,2,1,0:T(8,128)(2,1)S(1)}, bf16[2,4,96,768]{3,2,1,0:T(8,128)(2,1)}, u32[]{:S(2)}, u32[]{:S(2)}) %collective-permute-start.20) | collective-permute-done | bytes 1179680 | tf_op jit(solution)/shard_map/ppermute | solution.py:34
  137.5 5.2 %collective-permute-done.24.refs_13_ = bf16[128,960]{1,0:T(8,128)(2,1)S(1)} collective-permute-done((bf16[128,960]{1,0:T(8,128)(2,1)S(1)}, bf16[128,960]{1,0:T(8,128)(2,1)S(1)}, u32[]{:S(2)}, u32[]{:S(2)}) %collective-permute-start.24) | collective-permute-done | bytes 245792 | tf_op jit(solution)/shard_map/ppermute | solution.py:34
  142.7 9.9 %shard_map.409 = (bf16[2,2,768,768]{3,2,1,0:T(8,128)(2,1)}, bf16[2,512,768]{2,1,0:T(8,128)(2,1)}, bf16[2,512,768]{2,1,0:T(8,128)(2,1)}, bf16[2,512,192]{2,1,0:T(...) custom-call(s32[2]{0:T(128)} %pad_add_fusion.refs_0_, ...), custom_call_target="tpu_custom_call" | custom-call | flops 10000000000 | bytes 1048576 | tf_op jit(solution)/shard_map/pallas_call | solution.py:118
  153.3 12.6 %shard_map.410 = (bf16[2,2,768,768]{3,2,1,0:T(8,128)(2,1)}, bf16[2,512,768]{2,1,0:T(8,128)(2,1)}, bf16[2,512,768]{2,1,0:T(8,128)(2,1)}, bf16[2,512,192]{2,1,0:T(...) custom-call(s32[2]{0:T(128)} %pad_add_fusion.refs_0_, ...), custom_call_target="tpu_custom_call" | custom-call | flops 10000000000 | bytes 1048576 | tf_op jit(solution)/shard_map/pallas_call | solution.py:118
  170.0 12.8 %shard_map.411 = (bf16[2,2,4,96,768]{4,3,2,1,0:T(8,128)(2,1)}, bf16[2,2,4,96,768]{4,3,2,1,0:T(8,128)(2,1)}, bf16[2,192,384]{2,1,0:T(8,128)(2,1)}, f32[2,1,768]{2...) custom-call(s32[2]{0:T(128)} %pad_add_fusion.refs_0_, ...), custom_call_target="tpu_custom_call" | custom-call | flops 10000000000 | bytes 1048576 | tf_op jit(solution)/shard_map/pallas_call | solution.py:118
  187.1 15.7 %shard_map.412 = (bf16[2,2,4,96,768]{4,3,2,1,0:T(8,128)(2,1)}, bf16[2,2,4,96,768]{4,3,2,1,0:T(8,128)(2,1)}, bf16[2,192,384]{2,1,0:T(8,128)(2,1)}, f32[2,1,768]{2...) custom-call(s32[2]{0:T(128)} %pad_add_fusion.refs_0_, ...), custom_call_target="tpu_custom_call" | custom-call | flops 10000000000 | bytes 1048576 | tf_op jit(solution)/shard_map/pallas_call | solution.py:118
  208.4 4.2 fusion.4
  218.1 18.5 %shard_map.413 = (bf16[2,2,4,64,768]{4,3,2,1,0:T(8,128)(2,1)}, bf16[2,2,4,64,768]{4,3,2,1,0:T(8,128)(2,1)}, f32[2,192,1]{2,1,0:T(8,128)}, f32[2,192,1]{2,1,0:T(8...) custom-call(s32[2]{0:T(128)} %pad_add_fusion.refs_0_, ...), custom_call_target="tpu_custom_call" | custom-call | flops 10000000000 | bytes 1048576 | tf_op jit(solution)/shard_map/pallas_call | solution.py:118
  251.0 20.5 %shard_map.414 = (bf16[2,2,4,64,768]{4,3,2,1,0:T(8,128)(2,1)}, bf16[2,2,4,64,768]{4,3,2,1,0:T(8,128)(2,1)}, f32[2,192,1]{2,1,0:T(8,128)}, f32[2,192,1]{2,1,0:T(8...) custom-call(s32[2]{0:T(128)} %pad_add_fusion.refs_0_, ...), custom_call_target="tpu_custom_call" | custom-call | flops 10000000000 | bytes 1048576 | tf_op jit(solution)/shard_map/pallas_call | solution.py:118
  275.8 11.5 %collective-permute-done.35 = bf16[4,96,768]{2,1,0:T(8,128)(2,1)S(1)} collective-permute-done((bf16[4,96,768]{2,1,0:T(8,128)(2,1)}, bf16[4,96,768]{2,1,0:T(8,128)(2,1)S(1)}, u32[]{:S(2)}, u32[]{:S(2)}) %collective-permute-start.35) | collective-permute-done | bytes 589856 | tf_op jit(solution)/shard_map/ppermute | solution.py:34
  313.7 4.2 collective-permute-done.55
  327.2 4.0 collective-permute-done.63
  342.0 14.4 %collective-permute-done.65 = f32[208,128]{1,0:T(8,128)S(1)} collective-permute-done((f32[208,128]{1,0:T(8,128)S(1)}, f32[208,128]{1,0:T(8,128)S(1)}, u32[]{:S(2)}, u32[]{:S(2)}) %collective-permute-start.65) | collective-permute-done | bytes 106528 | tf_op jit(solution)/shard_map/ppermute | solution.py:34
  375.6 4.6 %collective-permute-done.46 = bf16[128,768]{1,0:T(8,128)(2,1)S(1)} collective-permute-done((bf16[128,768]{1,0:T(8,128)(2,1)S(1)}, bf16[128,768]{1,0:T(8,128)(2,1)S(1)}, u32[]{:S(2)}, u32[]{:S(2)}) %collective-permute-start.46) | collective-permute-done | bytes 196640 | tf_op jit(solution)/shard_map/ppermute | solution.py:34
  380.2 6.1 %collective-permute-done.47 = bf16[128,768]{1,0:T(8,128)(2,1)S(1)} collective-permute-done((bf16[128,768]{1,0:T(8,128)(2,1)S(1)}, bf16[128,768]{1,0:T(8,128)(2,1)S(1)}, u32[]{:S(2)}, u32[]{:S(2)}) %collective-permute-start.47) | collective-permute-done | bytes 196640 | tf_op jit(solution)/shard_map/ppermute | solution.py:34
  399.9 4.0 collective-permute-start.61
  (416 shorter events, 191.5 us)
Async XLA Ops:
  33.8 34.2 %collective-permute-start.9 = (bf16[2,4,64,768]{3,2,1,0:T(8,128)(2,1)}, bf16[2,4,64,768]{3,2,1,0:T(8,128)(2,1)}, u32[]{:S(2)}, u32[]{:S(2)}) collective-permute-start(bf16[2,4,64,768]{3,2,1,0:T(8,128)(2,1)} %pad_maximum_fusion.4.refs_14_), channel_id=1, source_target_pairs={{0,2},{1,3},{2,0},{3,1},{4,6},{5,7},{6,4},{7,5},{8,10},{9,11},{10,... | collective-permute-start | bytes 2359304 | tf_op jit(solution)/shard_map/ppermute | solution.py:34
  36.2 31.7 %collective-permute-start.7 = (bf16[2,4,64,768]{3,2,1,0:T(8,128)(2,1)}, bf16[2,4,64,768]{3,2,1,0:T(8,128)(2,1)S(1)}, u32[]{:S(2)}, u32[]{:S(2)}) collective-permute-start(bf16[2,4,64,768]{3,2,1,0:T(8,128)(2,1)} %pad_maximum_fusion.3.refs_12_), channel_id=1, source_target_pairs={{0,4},{1,5},{2,6},{3,7},{4,0},{5,1},{6,2},{7,3},{8,12},{9,13},{10,... | collective-permute-start | bytes 2359304 | tf_op jit(solution)/shard_map/ppermute | solution.py:34
  44.8 22.6 %collective-permute-start.11 = (bf16[192,768]{1,0:T(8,128)(2,1)S(1)}, bf16[192,768]{1,0:T(8,128)(2,1)S(1)}, u32[]{:S(2)}, u32[]{:S(2)}) collective-permute-start(bf16[192,768]{1,0:T(8,128)(2,1)S(1)} %pad_maximum_fusion.9), channel_id=1, source_target_pairs={{0,16},{1,17},{2,18},{3,19},{4,20},{5,21},{6,22},{7,23},{8,24},{9,... | collective-permute-start | bytes 884744 | tf_op jit(solution)/shard_map/ppermute | solution.py:34
  45.8 22.1 %collective-permute-start.12 = (bf16[192,768]{1,0:T(8,128)(2,1)S(1)}, bf16[192,768]{1,0:T(8,128)(2,1)S(1)}, u32[]{:S(2)}, u32[]{:S(2)}) collective-permute-start(bf16[192,768]{1,0:T(8,128)(2,1)S(1)} %pad_maximum_fusion.9), channel_id=1, source_target_pairs={{0,24},{1,25},{2,26},{3,27},{4,28},{5,29},{6,30},{7,31},{8,16},{9,... | collective-permute-start | bytes 884744 | tf_op jit(solution)/shard_map/ppermute | solution.py:34
  53.3 22.1 %collective-permute-start = (bf16[128,1024]{1,0:T(8,128)(2,1)}, bf16[128,1024]{1,0:T(8,128)(2,1)}, u32[]{:S(2)}, u32[]{:S(2)}) collective-permute-start(bf16[128,1024]{1,0:T(8,128)(2,1)} %get-tuple-element.498), channel_id=1, source_target_pairs={{0,1},{1,0},{2,3},{3,2},{4,5},{5,4},{6,7},{7,6},{8,9},{9,8},{10,11... | collective-permute-start | bytes 786440 | tf_op jit(solution)/shard_map/ppermute | solution.py:34
  74.0 30.2 %collective-permute-start.17 = (bf16[2,4,64,768]{3,2,1,0:T(8,128)(2,1)}, bf16[2,4,64,768]{3,2,1,0:T(8,128)(2,1)}, u32[]{:S(2)}, u32[]{:S(2)}) collective-permute-start(bf16[2,4,64,768]{3,2,1,0:T(8,128)(2,1)} %pad_maximum_fusion.4.refs_14_), channel_id=1, source_target_pairs={{0,1},{1,0},{2,3},{3,2},{4,5},{5,4},{6,7},{7,6},{8,9},{9,8},{10,11... | collective-permute-start | bytes 2359304 | tf_op jit(solution)/shard_map/ppermute | solution.py:34
  75.4 30.9 %collective-permute-start.15 = (bf16[2,4,64,768]{3,2,1,0:T(8,128)(2,1)}, bf16[2,4,64,768]{3,2,1,0:T(8,128)(2,1)}, u32[]{:S(2)}, u32[]{:S(2)}) collective-permute-start(bf16[2,4,64,768]{3,2,1,0:T(8,128)(2,1)} %pad_maximum_fusion.3.refs_12_), channel_id=1, source_target_pairs={{0,1},{1,0},{2,3},{3,2},{4,5},{5,4},{6,7},{7,6},{8,9},{9,8},{10,11... | collective-permute-start | bytes 2359304 | tf_op jit(solution)/shard_map/ppermute | solution.py:34
  76.6 23.2 %collective-permute-start.13 = (bf16[4,96,768]{2,1,0:T(8,128)(2,1)S(1)}, bf16[4,96,768]{2,1,0:T(8,128)(2,1)S(1)}, u32[]{:S(2)}, u32[]{:S(2)}) collective-permute-start(bf16[4,96,768]{2,1,0:T(8,128)(2,1)S(1)} %pad_maximum_fusion.5), channel_id=1, source_target_pairs={{0,2},{1,3},{2,0},{3,1},{4,6},{5,7},{6,4},{7,5},{8,10},{9,11},{10,... | collective-permute-start | bytes 1769480 | tf_op jit(solution)/shard_map/ppermute | solution.py:34
  78.5 27.8 %collective-permute-start.16 = (bf16[2,4,64,768]{3,2,1,0:T(8,128)(2,1)}, bf16[2,4,64,768]{3,2,1,0:T(8,128)(2,1)}, u32[]{:S(2)}, u32[]{:S(2)}) collective-permute-start(bf16[2,4,64,768]{3,2,1,0:T(8,128)(2,1)} %copy-done.47), channel_id=1, source_target_pairs={{0,1},{1,0},{2,3},{3,2},{4,5},{5,4},{6,7},{7,6},{8,9},{9,8},{10,11... | collective-permute-start | bytes 2359304 | tf_op jit(solution)/shard_map/ppermute | solution.py:34
  84.7 21.6 %collective-permute-start.18 = (bf16[2,4,64,768]{3,2,1,0:T(8,128)(2,1)}, bf16[2,4,64,768]{3,2,1,0:T(8,128)(2,1)}, u32[]{:S(2)}, u32[]{:S(2)}) collective-permute-start(bf16[2,4,64,768]{3,2,1,0:T(8,128)(2,1)} %collective-permute-done.9.refs_15_), channel_id=1, source_target_pairs={{0,1},{1,0},{2,3},{3,2},{4,5},{5,4},{6,7},{7,6},{8,9},{9,8},{10,11... | collective-permute-start | bytes 2359304 | tf_op jit(solution)/shard_map/ppermute | solution.py:34
  101.9 28.0 %collective-permute-start.20 = (bf16[2,4,96,768]{3,2,1,0:T(8,128)(2,1)S(1)}, bf16[2,4,96,768]{3,2,1,0:T(8,128)(2,1)}, u32[]{:S(2)}, u32[]{:S(2)}) collective-permute-start(bf16[2,4,96,768]{3,2,1,0:T(8,128)(2,1)S(1)} %pad_maximum_fusion.1.refs_9_), channel_id=1, source_target_pairs={{0,2},{1,3},{2,0},{3,1},{4,6},{5,7},{6,4},{7,5},{8,10},{9,11},{10,... | collective-permute-start | bytes 3538952 | tf_op jit(solution)/shard_map/ppermute | solution.py:34
  104.2 28.4 %collective-permute-start.19 = (bf16[2,4,96,768]{3,2,1,0:T(8,128)(2,1)}, bf16[2,4,96,768]{3,2,1,0:T(8,128)(2,1)}, u32[]{:S(2)}, u32[]{:S(2)}) collective-permute-start(bf16[2,4,96,768]{3,2,1,0:T(8,128)(2,1)} %pad_maximum_fusion.refs_7_), channel_id=1, source_target_pairs={{0,4},{1,5},{2,6},{3,7},{4,0},{5,1},{6,2},{7,3},{8,12},{9,13},{10,... | collective-permute-start | bytes 3538952 | tf_op jit(solution)/shard_map/ppermute | solution.py:34
  133.5 19.2 %collective-permute-start.27 = (bf16[2,4,96,768]{3,2,1,0:T(8,128)(2,1)S(1)}, bf16[2,4,96,768]{3,2,1,0:T(8,128)(2,1)}, u32[]{:S(2)}, u32[]{:S(2)}) collective-permute-start(bf16[2,4,96,768]{3,2,1,0:T(8,128)(2,1)S(1)} %pad_maximum_fusion.1.refs_9_), channel_id=1, source_target_pairs={{0,1},{1,0},{2,3},{3,2},{4,5},{5,4},{6,7},{7,6},{8,9},{9,8},{10,11... | collective-permute-start | bytes 3538952 | tf_op jit(solution)/shard_map/ppermute | solution.py:34
  182.9 24.1 %collective-permute-start.32 = (bf16[2,2,4,96,768]{4,3,2,1,0:T(8,128)(2,1)}, bf16[2,2,4,96,768]{4,3,2,1,0:T(8,128)(2,1)S(1)}, u32[]{:S(2)}, u32[]{:S(2)}) collective-permute-start(bf16[2,2,4,96,768]{4,3,2,1,0:T(8,128)(2,1)} %get-tuple-element.258), channel_id=1, source_target_pairs={{0,1},{1,0},{2,3},{3,2},{4,5},{5,4},{6,7},{7,6},{8,9},{9,8},{10,11... | collective-permute-start | bytes 7077896 | tf_op jit(solution)/shard_map/ppermute | solution.py:34
  183.4 29.1 %collective-permute-start.31 = (bf16[2,2,4,96,768]{4,3,2,1,0:T(8,128)(2,1)}, bf16[2,2,4,96,768]{4,3,2,1,0:T(8,128)(2,1)}, u32[]{:S(2)}, u32[]{:S(2)}) collective-permute-start(bf16[2,2,4,96,768]{4,3,2,1,0:T(8,128)(2,1)} %get-tuple-element.256), channel_id=1, source_target_pairs={{0,1},{1,0},{2,3},{3,2},{4,5},{5,4},{6,7},{7,6},{8,9},{9,8},{10,11... | collective-permute-start | bytes 7077896 | tf_op jit(solution)/shard_map/ppermute | solution.py:34
  215.9 28.6 %collective-permute-start.33 = (bf16[2,4,96,768]{3,2,1,0:T(8,128)(2,1)}, bf16[2,4,96,768]{3,2,1,0:T(8,128)(2,1)}, u32[]{:S(2)}, u32[]{:S(2)}) collective-permute-start(bf16[2,4,96,768]{3,2,1,0:T(8,128)(2,1)} %get-tuple-element.261), channel_id=1, source_target_pairs={{0,2},{1,3},{2,0},{3,1},{4,6},{5,7},{6,4},{7,5},{8,10},{9,11},{10,... | collective-permute-start | bytes 3538952 | tf_op jit(solution)/shard_map/ppermute | solution.py:34
  217.6 28.4 %collective-permute-start.34 = (bf16[2,4,96,768]{3,2,1,0:T(8,128)(2,1)}, bf16[2,4,96,768]{3,2,1,0:T(8,128)(2,1)}, u32[]{:S(2)}, u32[]{:S(2)}) collective-permute-start(bf16[2,4,96,768]{3,2,1,0:T(8,128)(2,1)} %get-tuple-element.262), channel_id=1, source_target_pairs={{0,4},{1,5},{2,6},{3,7},{4,0},{5,1},{6,2},{7,3},{8,12},{9,13},{10,... | collective-permute-start | bytes 3538952 | tf_op jit(solution)/shard_map/ppermute | solution.py:34
  238.4 37.3 %collective-permute-start.37 = (bf16[2,2,4,64,768]{4,3,2,1,0:T(8,128)(2,1)}, bf16[2,2,4,64,768]{4,3,2,1,0:T(8,128)(2,1)}, u32[]{:S(2)}, u32[]{:S(2)}) collective-permute-start(bf16[2,2,4,64,768]{4,3,2,1,0:T(8,128)(2,1)} %get-tuple-element.277), channel_id=1, source_target_pairs={{0,1},{1,0},{2,3},{3,2},{4,5},{5,4},{6,7},{7,6},{8,9},{9,8},{10,11... | collective-permute-start | bytes 4718600 | tf_op jit(solution)/shard_map/ppermute | solution.py:34
  238.4 37.3 %collective-permute-start.38 = (bf16[2,2,4,64,768]{4,3,2,1,0:T(8,128)(2,1)}, bf16[2,2,4,64,768]{4,3,2,1,0:T(8,128)(2,1)}, u32[]{:S(2)}, u32[]{:S(2)}) collective-permute-start(bf16[2,2,4,64,768]{4,3,2,1,0:T(8,128)(2,1)} %get-tuple-element.278), channel_id=1, source_target_pairs={{0,1},{1,0},{2,3},{3,2},{4,5},{5,4},{6,7},{7,6},{8,9},{9,8},{10,11... | collective-permute-start | bytes 4718600 | tf_op jit(solution)/shard_map/ppermute | solution.py:34
  292.8 46.8 %collective-permute-start.49 = (bf16[192,768]{1,0:T(8,128)(2,1)}, bf16[192,768]{1,0:T(8,128)(2,1)}, u32[]{:S(2)}, u32[]{:S(2)}) collective-permute-start(bf16[192,768]{1,0:T(8,128)(2,1)} %pad_maximum_fusion.10), channel_id=1, source_target_pairs={{0,8},{1,9},{2,10},{3,11},{4,12},{5,13},{6,14},{7,15},{8,0},{9,1},... | collective-permute-start | bytes 884744 | tf_op jit(solution)/shard_map/ppermute | solution.py:34
  295.1 45.0 %collective-permute-start.50 = (bf16[192,768]{1,0:T(8,128)(2,1)S(1)}, bf16[192,768]{1,0:T(8,128)(2,1)}, u32[]{:S(2)}, u32[]{:S(2)}) collective-permute-start(bf16[192,768]{1,0:T(8,128)(2,1)S(1)} %pad_maximum_fusion.11), channel_id=1, source_target_pairs={{0,16},{1,17},{2,18},{3,19},{4,20},{5,21},{6,22},{7,23},{8,24},{9,... | collective-permute-start | bytes 884744 | tf_op jit(solution)/shard_map/ppermute | solution.py:34
  296.9 43.2 %collective-permute-start.51 = (bf16[192,768]{1,0:T(8,128)(2,1)}, bf16[192,768]{1,0:T(8,128)(2,1)}, u32[]{:S(2)}, u32[]{:S(2)}) collective-permute-start(bf16[192,768]{1,0:T(8,128)(2,1)} %pad_maximum_fusion.12), channel_id=1, source_target_pairs={{0,24},{1,25},{2,26},{3,27},{4,28},{5,29},{6,30},{7,31},{8,16},{9,... | collective-permute-start | bytes 884744 | tf_op jit(solution)/shard_map/ppermute | solution.py:34
  323.7 33.9 %collective-permute-start.42 = (bf16[2,4,64,768]{3,2,1,0:T(8,128)(2,1)}, bf16[2,4,64,768]{3,2,1,0:T(8,128)(2,1)}, u32[]{:S(2)}, u32[]{:S(2)}) collective-permute-start(bf16[2,4,64,768]{3,2,1,0:T(8,128)(2,1)} %get-tuple-element.466), channel_id=1, source_target_pairs={{0,2},{1,3},{2,0},{3,1},{4,6},{5,7},{6,4},{7,5},{8,10},{9,11},{10,... | collective-permute-start | bytes 2359304 | tf_op jit(solution)/shard_map/ppermute | solution.py:34
  336.0 24.6 %collective-permute-start.44 = (bf16[2,4,64,768]{3,2,1,0:T(8,128)(2,1)}, bf16[2,4,64,768]{3,2,1,0:T(8,128)(2,1)}, u32[]{:S(2)}, u32[]{:S(2)}) collective-permute-start(bf16[2,4,64,768]{3,2,1,0:T(8,128)(2,1)} %get-tuple-element.468), channel_id=1, source_target_pairs={{0,4},{1,5},{2,6},{3,7},{4,0},{5,1},{6,2},{7,3},{8,12},{9,13},{10,... | collective-permute-start | bytes 2359304 | tf_op jit(solution)/shard_map/ppermute | solution.py:34
  (95 other events, 774.2 us)

commit v3 on v2

--- a/solution.py
+++ b/solution.py
@@ -88,7 +88,7 @@
 
 
 class Plan:
-    def __init__(self, n_dp, n_t, quarter, wt, wl, ct, cl, ht, hl):
+    def __init__(self, n_dp, n_t, quarter, wt, wl, ct, cl, ht, hl, bins):
         self.n_dp, self.n_t, self.total = n_dp, n_t, n_dp * n_t
         self.far = self.total // 8
         self.quarter, self.rows = quarter, quarter * n_t
@@ -100,6 +100,7 @@
         self.heads = ct // HD
         self.hw = HD + LHD
         self.lay_cols = 4 * cl + 2 * hl
+        self.per = bins // self.total
 
     def spread(self, own, padded):
         out = jnp.arange(own * self.n_dp, dtype=jnp.int32)
@@ -550,57 +551,54 @@
     )
 
 
-def attend_backward(p, me2, w_all, w_lay, qkv, ctx, lse, x_low, lay_low, ints, ints_t, da_t, da_l, gfl, spread_t, spread_l, prev, last):
+def attend_backward(p, me2, xs, w_all, w_lay, qkv, ctx, lse, x_low, lay_low, ints, ints_t, da_t, da_l, gfl, spread_t, spread_l, prev, last):
     n_t, rows, hw, nh = p.n_t, p.rows, p.hw, p.heads
     padded_t, padded_l = p.n_dp * p.ra, p.n_dp * p.rl
     exact_t = p.ra == p.d_own
-    blocks = [t for t in range(n_t) if t % 2 == (0 if last else 1)]
-    nb = len(blocks)
+    nb = len(xs)
+    n_prev = len(prev)
 
     def body(*refs):
         (me_ref, w_any, wl_ref, qkv_r, ctx_r, lse_r, xl, ll, ir, itr, dat, dal, gfl_r, spt, spl), refs = refs[:15], refs[15:]
-        if last:
-            (pt, pl_, dr1t, dr1l), refs = refs[:4], refs[4:]
-        outs, scratch = refs[:8], refs[8:]
-        low, high, gbq, gbv, gbql, gbvl, out_a, out_b = outs
-        w_in, staged, staged_l, acc_t, acc_l, dctx, ctx_s, ctx_l, dp_t, dp_l, sem_in, sem_out = scratch
-        my_dp = me_ref[0]
-        for k, t in enumerate(blocks):
-            pltpu.make_async_copy(w_any.at[k], w_in.at[k], sem_in.at[k]).start()
+        prev_refs, refs = refs[:n_prev], refs[n_prev:]
+        outs, scratch = refs[:6], refs[6:]
+        low, high, gb_t, gb_l, out_a, out_b = outs
+        (w_in, staged, staged_l, acc_t, acc_l, dctx, ctx_s, ctx_l, dp_t, dp_l, bin_rows, sem_in,
+         sem_out, sem_bin) = scratch
+        my_dp, my_t = me_ref[0], me_ref[1]
+        for k, x in enumerate(xs):
+            pltpu.make_async_copy(w_any.at[x], w_in.at[k], sem_in.at[k]).start()
         xT, lT = xl[...].T, ll[...].T
         daT, dalT = dat[...].T, dal[...].T
         seg_col, seg_row = ir[:, 0:1], itr[0:1, :]
-        if last:
-            acc_t[...] = pt[...]
-            acc_l[...] = pl_[...]
+        if prev:
+            acc_t[...] = prev_refs[0][...]
+            acc_l[...] = prev_refs[1][...]
         else:
             acc_t[...] = jnp.zeros_like(acc_t)
             acc_l[...] = jnp.zeros_like(acc_l)
-        gbq[...] = jnp.zeros_like(gbq)
-        gbv[...] = jnp.zeros_like(gbv)
-        gbql[...] = jnp.zeros_like(gbql)
-        gbvl[...] = jnp.zeros_like(gbvl)
-        for k, t in enumerate(blocks):
+        ones = jnp.ones((16, rows), BF16)
+        for k, x in enumerate(xs):
             wait_for(w_in.at[k], sem_in.at[k])
             w = w_in[k]
-            wl = wl_ref[k]
+            wl = wl_ref[x]
             d_t = dot(dat[...], w[:, 3 * p.ct :]).T
             d_l = dot(dal[...], wl[:, 3 * p.cl : 4 * p.cl]).T
             for h in range(nh):
                 dctx[h, pl.ds(0, HD)] = d_t[h * HD : (h + 1) * HD].astype(BF16)
                 dctx[h, pl.ds(HD, LHD)] = d_l[h * LHD : (h + 1) * LHD].astype(BF16)
-                ctx_s[pl.ds(h * HD, HD)] = ctx_r[k, h, pl.ds(0, HD)]
-                ctx_l[pl.ds(h * LHD, LHD)] = ctx_r[k, h, pl.ds(HD, LHD)]
+                ctx_s[pl.ds(h * HD, HD)] = ctx_r[x, h, pl.ds(0, HD)]
+                ctx_l[pl.ds(h * LHD, LHD)] = ctx_r[x, h, pl.ds(HD, LHD)]
 
             for h in range(nh):
-                q, key, val = qkv_r[k, h], qkv_r[k, nh + h], qkv_r[k, 2 * nh + h]
+                q, key, val = qkv_r[x, h], qkv_r[x, nh + h], qkv_r[x, 2 * nh + h]
                 dc = dctx[h]
                 scores = dot(key, q, 0, 0)
                 probs = jnp.exp(
-                    jnp.where(seg_col == seg_row, scores, NEG_FILL) - lse_r[k, pl.ds(h, 1), :]
+                    jnp.where(seg_col == seg_row, scores, NEG_FILL) - lse_r[x, pl.ds(h, 1), :]
                 )
                 low_p = probs.astype(BF16)
-                prod = dc.astype(F32) * ctx_r[k, h].astype(F32)
+                prod = dc.astype(F32) * ctx_r[x, h].astype(F32)
                 sum_lay = jnp.sum(prod[HD:], axis=0, keepdims=True)
                 sum_all = jnp.sum(prod[:HD], axis=0, keepdims=True) + sum_lay
                 dz_all = probs * (dot(val, dc, 0, 0) - sum_all)
@@ -614,10 +612,8 @@
                 for c, (top, bot) in enumerate(((dq_t, dq_l), (dk_t, dk_l), (dv[:HD], dv[HD:]))):
                     dp_t[pl.ds(c * p.ct + h * HD, HD)] = top.astype(BF16)
                     dp_l[pl.ds(c * p.cl + h * LHD, LHD)] = bot.astype(BF16)
-                    if c != 1:
-                        dst, dst_l = (gbq, gbql) if c == 0 else (gbv, gbvl)
-                        dst[k, pl.ds(h * HD, HD)] = jnp.sum(top, axis=1, keepdims=True)
-                        dst_l[k, pl.ds(h * LHD, LHD)] = jnp.sum(bot, axis=1, keepdims=True)
+            gb_t[k] = dot(ones, dp_t[...], 1, 1)[:8]
+            gb_l[k] = dot(ones, dp_l[...], 1, 1)[:8]
             acc_t[...] += dot(w[:, : 3 * p.ct], dp_t[...])
             acc_l[...] += dot(wl[:, : 3 * p.cl], dp_l[...])
             grad = jnp.concatenate(
@@ -631,27 +627,26 @@
                 [
                     dot(lT, dp_l[...], 1, 1),
                     dot(dalT, ctx_l[...], 1, 1),
-                    gfl_r[k].astype(F32),
+                    gfl_r[x].astype(F32),
                     jnp.zeros((p.wl, fill), F32),
                 ],
                 axis=1,
             ).astype(BF16)
             staged_l[k] = dot(spl[...], grad_l, 0, 0).astype(BF16)
-            x = t // 2
             rest = p.ra - p.half_a
-            slot = lambda d, y, z: low.at[x, y, z] if d == 0 else high.at[y, x, z]
+            slot = lambda d, y, z: (high if d else low).at[k, y, z]
             slices = [(0, p.ra, 0, p.half_a, 0)]
             if rest:
                 slices.append((1, p.ra, p.half_a, rest, 0))
             store_slots(p, staged.at[k], slot, my_dp, sem_out.at[0], slices)
             store_slots(p, staged_l.at[k], slot, my_dp, sem_out.at[1], [(1, p.rl, 0, p.rl, rest)])
         if last:
-            gt = dr1t[...] + acc_t[...].T
-            gl = dr1l[...] + acc_l[...].T
+            gt = prev_refs[2][...] + acc_t[...].T
+            gl = prev_refs[3][...] + acc_l[...].T
             out_a[:, pl.ds(0, p.wt)] = gt.astype(BF16)
             out_a[:, pl.ds(p.wt, p.wl)] = gl.astype(BF16)
             half = p.wl // 2
-            bins = out_b.shape[0]
+            bins = bin_rows.shape[0]
             levels = lax.broadcasted_iota(jnp.int32, (bins, 1), 0).astype(F32)
             for m in range(2):
                 row = itr[1 + 2 * m : 2 + 2 * m, :] * 128.0 + itr[2 + 2 * m : 3 + 2 * m, :]
@@ -660,7 +655,19 @@
                 top = part.astype(BF16)
                 rest_part = (part - top.astype(F32)).astype(BF16)
                 both = dot(hot, jnp.concatenate([top, rest_part], axis=1))
-                out_b[:, pl.ds(m * half, half)] = both[:, :half] + both[:, half:]
+                bin_rows[:, pl.ds(m * half, half)] = (both[:, :half] + both[:, half:]).astype(BF16)
+            if p.per % 16:
+                pltpu.make_async_copy(bin_rows, out_b, sem_bin).start()
+            else:
+                for r in range(p.total):
+                    z, y, x, c = r // 8, (r // 4) % 2, (r // 2) % 2, r % 2
+                    at = ((r // n_t) ^ my_dp) * n_t + ((r % n_t) ^ my_t)
+                    pltpu.make_async_copy(
+                        bin_rows.at[pl.ds(pl.multiple_of(at * p.per, 16), p.per)],
+                        out_b.at[c, x, y, z],
+                        sem_bin,
+                    ).start()
+            wait_for(bin_rows, sem_bin)
         else:
             out_a[...] = acc_t[...]
             out_b[...] = acc_l[...]
@@ -669,18 +676,17 @@
 
     half_b = p.ra + p.rl - p.half_a
     outs = [
-        shape((2, 2, p.far, p.half_a, p.cols), BF16),
-        shape((2, 2, p.far, half_b, p.cols), BF16),
-        shape((nb, p.ct, 1), F32),
-        shape((nb, p.ct, 1), F32),
-        shape((nb, p.cl, 1), F32),
-        shape((nb, p.cl, 1), F32),
+        shape((nb, 2, p.far, p.half_a, p.cols), BF16),
+        shape((nb, 2, p.far, half_b, p.cols), BF16),
+        shape((nb, 8, 3 * p.ct), F32),
+        shape((nb, 8, 3 * p.cl), F32),
     ]
     args = [me2, w_all, w_lay, qkv, ctx, lse, x_low, lay_low, ints, ints_t, da_t, da_l, gfl, spread_t, spread_l]
+    args += list(prev)
     if last:
-        *prev, bins = prev
-        args += list(prev)
-        outs += [shape((rows, p.wt + p.wl), BF16), shape((bins, p.wl), F32)]
+        bins = p.per * p.total
+        slots = (bins,) if p.per % 16 else (2, 2, 2, p.far, p.per)
+        outs += [shape((rows, p.wt + p.wl), BF16), shape((*slots, p.wl), BF16)]
     else:
         outs += [shape((p.wt, rows), F32), shape((p.wl, rows), F32)]
     scratch = [
@@ -694,13 +700,14 @@
         pltpu.VMEM((p.cl, rows), BF16),
         pltpu.VMEM((3 * p.ct, rows), BF16),
         pltpu.VMEM((3 * p.cl, rows), BF16),
+        pltpu.VMEM((p.per * p.total, p.wl), BF16),
         pltpu.SemaphoreType.DMA((nb,)),
         pltpu.SemaphoreType.DMA((2,)),
+        pltpu.SemaphoreType.DMA,
     ]
     specs = [SM, ANY] + [VM] * (len(args) - 2)
-    return kernel_call(
-        body, outs, specs, [ANY, ANY] + [VM] * (len(outs) - 2), scratch, args
-    )
+    out_specs = [ANY, ANY] + [VM] * (len(outs) - 3) + [ANY if last else VM]
+    return kernel_call(body, outs, specs, out_specs, scratch, args)
 
 
 def tie(*groups):
@@ -708,8 +715,23 @@
     return jax.tree.unflatten(tree, lax.optimization_barrier(leaves))
 
 
+def after(values, *others):
+    return tie(values, *others)[0]
+
+
 def line_of(shard, total):
     return [shard] + [xor_send(shard, total, 8 * r) for r in range(1, total // 8)]
+
+
+def line_doubled(shard, total, others):
+    line = [shard]
+    while 8 * len(line) < total:
+        held = jnp.stack(line)
+        if len(line) > 1:
+            held = after(held, others)
+        theirs = xor_send(held, total, 8 * len(line))
+        line = line + [theirs[z] for z in range(len(line))]
+    return line
 
 
 def halves_of(line, half):
@@ -728,54 +750,60 @@
     return send, keep
 
 
-def reduce_last(keep, got, total):
-    far = total // 8
-    line = [
+def reduce_line_parts(keep, got):
+    return [
         jnp.concatenate([add_low(keep[k][z], got[k][z]) for k in range(2)], axis=0)
-        for z in range(far)
+        for z in range(keep[0].shape[0])
     ]
+
+
+def send_line(line, total):
+    return line[:1] + [xor_send(line[z], total, 8 * z) for z in range(1, len(line))]
+
+
+def add_line(line):
     out = line[0].astype(F32)
-    for z in range(1, far):
-        out = out + xor_send(line[z], total, 8 * z).astype(F32)
+    for member in line[1:]:
+        out = out + member.astype(F32)
     return out
 
 
-def sum_everywhere(values, total):
-    pair = values + xor_send(values, total, 1)
-    chip = pair + xor_send(pair, total, 2)
-    plane = chip + xor_send(chip, total, 4)
-    distance = 8
-    while distance < total:
-        if 2 * distance < total:
-            near, far, both = (xor_send(plane, total, distance * k) for k in (1, 2, 3))
-            plane = (plane + near) + (far + both)
-            distance = distance * 4
-        else:
-            plane = plane + xor_send(plane, total, distance)
-            distance = distance * 2
-    return plane
-
-
-def reduce_small(values, total):
-    me = lax.axis_index("dp") * lax.axis_size("tensor") + lax.axis_index("tensor")
-    distance = 1
-    sizes = []
-    while distance < total:
-        half = values.shape[0] // 2
-        bit = (me // distance) % 2
-        mine = lax.dynamic_slice_in_dim(values, bit * half, half)
-        other = lax.dynamic_slice_in_dim(values, (1 - bit) * half, half)
-        values = mine + xor_send(to_low(other), total, distance).astype(F32)
-        sizes.append(distance)
-        distance = distance * 2
-    square_sum = jnp.sum(values * values)
-    for distance in reversed(sizes):
-        bit = (me // distance) % 2
-        other = xor_send(values, total, distance)
-        values = jnp.where(
-            bit == 0, jnp.concatenate([values, other]), jnp.concatenate([other, values])
+def update_all(factor, matrices, flat, grads):
+    states = [member for group in (*matrices, *flat) for member in group]
+
+    def body(*refs):
+        factor_ref, grads = refs[0], refs[1:7]
+        ins, outs = refs[7:25], refs[25:]
+        scale = factor_ref[0, 0]
+        for k in range(6):
+            w, m, v = (ins[3 * k + j][...] for j in range(3))
+            results = adamw_step(
+                w, m, v, grads[k][...] * scale, WEIGHT_DECAY if k < 4 else 0.0, LEARN_RATES[k]
+            )
+            for j in range(3):
+                outs[3 * k + j][...] = results[j]
+
+    return list(
+        kernel_call(
+            body,
+            [shape(v.shape, F32) for v in states],
+            [SM] + [VM] * 24,
+            [VM] * 18,
+            [],
+            (factor.reshape(1, 1), *grads, *states),
         )
-    return values, square_sum
+    )
+
+
+def relative(blocks, me):
+    total = blocks.shape[0]
+    step = 1
+    while step < total:
+        pairs = blocks.reshape(total // (2 * step), 2, step, *blocks.shape[1:])
+        swapped = jnp.stack([pairs[:, 1], pairs[:, 0]], axis=1)
+        blocks = jnp.where((me // step) % 2 == 0, pairs, swapped).reshape(blocks.shape)
+        step = step * 2
+    return blocks
 
 
 def on_device(
@@ -814,7 +842,8 @@
     ht, hl = feed_text.shape[2], feed_layout.shape[2]
 
 
-    p = Plan(n_dp, n_t, quarter, wt, wl, ct, cl, ht, hl)
+    p = Plan(n_dp, n_t, quarter, wt, wl, ct, cl, ht, hl, tables.shape[0] // wl)
+    me = lax.axis_index("dp") * n_t + t_pos
     me2 = jnp.stack([lax.axis_index("dp"), t_pos]).astype(jnp.int32)
     lay_cols = p.lay_cols
 
@@ -865,7 +894,18 @@
             out = lax.dynamic_update_slice(out, blocks[r][None], (t_pos ^ r, 0, 0))
         return out
 
-    parts = split_vectors(vectors, [wt, wl], [n_t * ht, n_t * hl])
+    send = lambda values, distance: xor_send(values, total, distance)
+
+    line_a = line_of(attend_pack, total)
+    xin = page_of(packed_in)
+    low, high = halves_of(line_a, p.half_a)
+    low, high = after((low, high), xin)
+    line_f = line_doubled(feed_pack, total, line_a)
+    low0, high0 = jnp.stack([low, send(low, 2)]), jnp.stack([high, send(high, 4)])
+    low4, high2 = send(low0, 4), send(high0, 2)
+    low1, high1 = send(low0, 1), send(high0, 1)
+    late_vectors, late_tables = after((vectors, tables), low0, high0)
+    parts = split_vectors(late_vectors, [wt, wl], [n_t * ht, n_t * hl])
     biases, vecs, bins_in = [], [], []
     for s, width in ((0, ct), (1, cl)):
         vec, hidden = parts[s]
@@ -881,46 +921,40 @@
         )
         vecs.append(jnp.stack(vec))
         bins_in.append(hidden.reshape(n_t, 1, -1))
-    table_rows = to_low(tables.reshape(-1, wl))
+    table_rows = to_low(late_tables.reshape(-1, wl))
     spread_t = p.spread(d_own, p.ra) if p.ra != d_own else jnp.zeros((16, 128), BF16)
     spread_l = p.spread(dl_own, p.rl)
 
-    send = lambda values, distance: xor_send(values, total, distance)
-
-    line_a = line_of(attend_pack, total)
-    xin = page_of(packed_in)
-    line_a, feed_pack = tie(line_a, feed_pack)
-    line_f = line_of(feed_pack, total)
-    low, high = halves_of(line_a, p.half_a)
-    low0, high0 = jnp.stack([low, send(low, 2)]), jnp.stack([high, send(high, 4)])
-    low4, high2 = send(low0, 4), send(high0, 2)
-    low1, high1 = send(low0, 1), send(high0, 1)
-    pieces_a0 = [low0, low4, high0, high2]
-    (low4, high2), line_f = tie((low4, high2), line_f)
+    flow, fhigh = halves_of(after(line_f, low0, high0), p.ra)
+    flow, fhigh = after((flow, fhigh), low4, high2)
+    att_fix = (biases[0], biases[1], vecs[0], vecs[1], spread_t, spread_l)
     low5, high3 = send(low4, 1), send(high2, 1)
-    flow, fhigh = halves_of(line_f, p.ra)
     flow_x, fhigh_y = send(flow, 2), send(fhigh, 4)
-    xin, flow, fhigh = tie(xin, flow, fhigh)
-    att_fix = (biases[0], biases[1], vecs[0], vecs[1], spread_t, spread_l)
     (w_all0, w_lay0, qkv0, ctx0, lse0, *row_state) = attend_forward(
-        p, me2, 0, (*xin, table_rows), *att_fix, pieces_a0
-    )
-    row_state, (flow_x, fhigh_y) = tie(row_state, (flow_x, fhigh_y))
+        p, me2, 0, (*xin, table_rows), *att_fix, [low0, low4, high0, high2]
+    )
+    row_state, qkv0, low5, high3, low1, high1, flow_x, fhigh_y = tie(
+        row_state, qkv0, low5, high3, low1, high1, flow_x, fhigh_y
+    )
     flow0, fhigh0 = jnp.stack([flow, flow_x]), jnp.stack([fhigh, fhigh_y])
+    row_state = after(row_state, flow0, fhigh0)
     flow4, fhigh2 = send(flow0, 4), send(fhigh0, 2)
     flow1, fhigh1 = send(flow0, 1), send(fhigh0, 1)
-    row_state, flow0, fhigh0 = tie(row_state, flow0, fhigh0)
     (w_all1, w_lay1, qkv1, ctx1, lse1, n1t, i1t, h_t, n1l, i1l, h_l) = attend_forward(
         p, me2, 1, row_state, *att_fix, [low1, low5, high1, high3]
     )
     x_low, lay_low, _, ints, ints_t = row_state[:5]
-    (flow4, fhigh2), h_t, packed_cot = tie((flow4, fhigh2), h_t, packed_cot)
+    n1t, n1l, h_t, h_l, w_lay1, flow4, fhigh2, packed_cot = tie(
+        n1t, n1l, h_t, h_l, w_lay1, flow4, fhigh2, packed_cot
+    )
     flow5, fhigh3 = send(flow4, 1), send(fhigh2, 1)
     cots = page_of(packed_cot)
     (f_all0, g_t0, gp_t0, g_l0, gp_l0, acc_t, acc_l) = feed_forward(
         p, me2, 0, [flow0, flow4, fhigh0, fhigh2], w_lay0, h_t, h_l, bins_in[0], bins_in[1], spread_t, ()
     )
-    acc_t, flow5, fhigh3, cots = tie(acc_t, flow5, fhigh3, cots)
+    acc_t, acc_l, f_all0, flow5, fhigh3, flow1, fhigh1, cots = tie(
+        acc_t, acc_l, f_all0, flow5, fhigh3, flow1, fhigh1, cots
+    )
     (f_all1, g_t1, gp_t1, g_l1, gp_l1, out_rows, dr_t, dr_l, df_t, df_l, gv2t, gv2l, _) = feed_forward(
         p, me2, 1, [flow1, flow5, fhigh1, fhigh3], w_lay1, h_t, h_l, bins_in[0], bins_in[1], spread_t,
         (acc_t, acc_l, n1t, n1l, *cots, vecs[0], vecs[1]),
@@ -929,36 +963,88 @@
     (gf_low1, gf_high1, gfl1, dbt1, dbl1, acc_t, acc_l) = feed_backward(
         p, me2, f_all1, w_lay1, h_t, h_l, df_t, df_l, g_t1, gp_t1, g_l1, gp_l1, spread_t, None, False
     )
-    acc_t, rows_out = tie(acc_t, rows_out)
+    rows_out, gf_low1, gf_high1, gfl1, dbt1, dbl1, acc_t, acc_l = tie(
+        rows_out, gf_low1, gf_high1, gfl1, dbt1, dbl1, acc_t, acc_l
+    )
     got = [send(gf_low1, 1), send(gf_high1, 1)]
     (gf_low0, gf_high0, gfl0, dbt0, dbl0, dr1t, dr1l, da_t, da_l, gv1t, gv1l) = feed_backward(
         p, me2, f_all0, w_lay0, h_t, h_l, df_t, df_l, g_t0, gp_t0, g_l0, gp_l0, spread_t,
         (acc_t, acc_l, dr_t, dr_l, n1t, i1t, n1l, i1l, vecs[0], vecs[1]), True
     )
+    got, gf_low0, gf_high0, gfl0, dbt0, dbl0, dr1t, dr1l, da_t, da_l, gv1t, gv1l = tie(
+        got, gf_low0, gf_high0, gfl0, dbt0, dbl0, dr1t, dr1l, da_t, da_l, gv1t, gv1l
+    )
     next_f, keep_f = reduce_second((gf_low0, gf_high0), got)
-    next_f, keep_f, da_t = tie(next_f, keep_f, da_t)
+    da_t = after(da_t, next_f, keep_f)
     got_f = [send(next_f[0], 2), send(next_f[1], 4)]
-    (ga_low1, ga_high1, bq1, bv1, bql1, bvl1, acc_t, acc_l) = attend_backward(
-        p, me2, w_all1, w_lay1, qkv1, ctx1, lse1, x_low, lay_low, ints, ints_t, da_t, da_l,
-        gfl1, spread_t, spread_l, None, False
-    )
-    got_f, acc_t = tie(got_f, acc_t)
+    att_args = (x_low, lay_low, ints, ints_t, da_t, da_l)
+    (ga_low1, ga_high1, gb_t1, gb_l1, acc_t, acc_l) = attend_backward(
+        p, me2, (0, 1), w_all1, w_lay1, qkv1, ctx1, lse1, *att_args, gfl1, spread_t, spread_l, (), False
+    )
+    got_f, ga_low1, ga_high1, gb_t1, gb_l1, acc_t, acc_l = tie(
+        got_f, ga_low1, ga_high1, gb_t1, gb_l1, acc_t, acc_l
+    )
+    next_f, keep_f = reduce_second(keep_f, got_f)
+    acc_t = after(acc_t, next_f, keep_f)
     got = [send(ga_low1, 1), send(ga_high1, 1)]
-    next_f, keep_f = reduce_second(keep_f, got_f)
-    next_f, keep_f, acc_t = tie(next_f, keep_f, acc_t)
     got_f = [send(next_f[0], 4), send(next_f[1], 2)]
-    (ga_low0, ga_high0, bq0, bv0, bql0, bvl0, grad_rows, table_grad) = attend_backward(
-        p, me2, w_all0, w_lay0, qkv0, ctx0, lse0, x_low, lay_low, ints, ints_t, da_t, da_l,
-        gfl0, spread_t, spread_l, (acc_t, acc_l, dr1t, dr1l, table_rows.shape[0]), True
-    )
-    got_f, got, grad_rows, table_grad, bq0 = tie(got_f, got, grad_rows, table_grad, bq0)
-    next_a, keep_a = reduce_second((ga_low0, ga_high0), got)
-    got_a = [send(next_a[0], 2), send(next_a[1], 4)]
-    feed_sum = reduce_last(keep_f, got_f, total)
-    next_a, keep_a = reduce_second(keep_a, got_a)
-    got_a = [send(next_a[0], 4), send(next_a[1], 2)]
-    attend_sum = reduce_last(keep_a, got_a, total)
-    rows_grad = send_rows(grad_rows)
+    core_args = (w_all0, w_lay0, qkv0, ctx0, lse0, *att_args, gfl0, spread_t, spread_l)
+    (low_x1, high_x1, gb_t02, gb_l02, acc_t, acc_l) = attend_backward(
+        p, me2, (1,), *core_args, (acc_t, acc_l), False
+    )
+    got, got_f, low_x1, high_x1, gb_t02, gb_l02, acc_t, acc_l = tie(
+        got, got_f, low_x1, high_x1, gb_t02, gb_l02, acc_t, acc_l
+    )
+    low_x1 = add_low(low_x1[0], got[0][1])
+    high_x1 = add_low(high_x1[0], got[1][1])
+    line_f = reduce_line_parts(keep_f, got_f)
+    acc_t = after(acc_t, low_x1, high_x1, line_f)
+    got_low = send(low_x1, 2)
+    got_high1 = send(high_x1[1], 4)
+    early = (p.far + 2) // 2
+    line_f, late_f = send_line(line_f[:early], total), line_f[early:]
+    (low_x0, high_x0, gb_t00, gb_l00, grad_rows, table_grad) = attend_backward(
+        p, me2, (0,), *core_args, (acc_t, acc_l, dr1t, dr1l), True
+    )
+    low_x0, high_x0, gb_t00, gb_l00, grad_rows, table_grad = after(
+        (low_x0, high_x0, gb_t00, gb_l00, grad_rows, table_grad), got_high1, got_low, line_f
+    )
+    line_f = line_f + [send(late_f[z], 8 * (early + z)) for z in range(len(late_f))]
+    if p.per % 16:
+        table_grad = relative(table_grad.reshape(total, p.per, wl), me)
+        table_grad = table_grad.reshape(p.far, 2, 2, 2, p.per, wl).transpose(3, 2, 1, 0, 4, 5)
+    table_got = send(table_grad[1], 1)
+    table_sum = add_low(table_grad[0], table_got)
+    rest = p.ra - p.half_a
+    spare = high_x0.shape[-2] - rest - p.per
+
+    def placed(part):
+        edges = ((0, 0),) * (part.ndim - 2) + ((rest, spare), (lay_cols, p.cols - lay_cols - wl))
+        return jnp.pad(part, edges).astype(F32)
+
+    high_x0 = to_low(high_x0[0].astype(F32) + got[1][0].astype(F32) + placed(table_sum[0]))
+    got_high0 = send(high_x0[1], 4)
+    got_table = send(table_sum[1, 1], 4)
+    low_x0, got_low = after((low_x0, got_low), high_x0)
+    low = to_low(low_x0[0].astype(F32) + got[0][0].astype(F32) + got_low.astype(F32))
+    got_low = send(low[1], 4)
+    table_x1 = add_low(table_sum[1, 0], got_table)
+    high_1 = to_low(high_x1[0].astype(F32) + got_high1.astype(F32) + placed(table_x1))
+    got_high = send(high_1, 2)
+    pieces = (gb_t1, gb_l1, gb_t02, gb_l02, gb_t00, gb_l00, dbt0, dbt1, dbl0, dbl1, gv1t, gv1l, gv2t, gv2l)
+    (gb_t1, gb_l1, gb_t02, gb_l02, gb_t00, gb_l00, dbt0, dbt1, dbl0, dbl1, gv1t, gv1l, gv2t, gv2l) = after(
+        pieces, high_1, low
+    )
+    gb_t0 = jnp.concatenate([gb_t00, gb_t02])
+    gb_l0 = jnp.concatenate([gb_l00, gb_l02])
+    feed_sum = add_line(after(line_f, high_1, low))
+    high_0 = add_low(high_x0[0], got_high0)
+    line_a = send_line(reduce_line_parts((low[0], high_0), (got_low, got_high)), total)
+    got_a = (got_low, got_high)
+    feed_sum = after(feed_sum, got_a)
+    attend_sum = add_line(line_a)
+    rows_grad = send_rows(after(grad_rows, got_a))
+    rows_out = after(rows_out, got_a)
 
     def by_block(odd, even):
         both = jnp.stack([even[0], odd[0], even[1], odd[1]]).reshape(n_t, -1)
@@ -969,74 +1055,63 @@
     gv_t, gv_l = gv2t + gv1t, gv2l + gv1l
     vector_grad = jnp.concatenate(
         [
-            by_block(bq1, bq0),
-            by_block(bv1, bv0),
+            by_block(gb_t1[:, 0, : ct], gb_t0[:, 0, : ct]),
+            by_block(gb_t1[:, 0, 2 * ct :], gb_t0[:, 0, 2 * ct :]),
             gv_t[2:].reshape(-1),
             by_block(dbt1, dbt0),
-            by_block(bql1, bql0),
-            by_block(bvl1, bvl0),
+            by_block(gb_l1[:, 0, : cl], gb_l0[:, 0, : cl]),
+            by_block(gb_l1[:, 0, 2 * cl :], gb_l0[:, 0, 2 * cl :]),
             gv_l[2:].reshape(-1),
             by_block(dbl1, dbl0),
         ]
     )
-    small = jnp.concatenate([table_grad.reshape(-1), vector_grad])
-    n_table, n_small = table_grad.size, small.shape[0]
-    small_rows = round_up(-(-n_small // 128), 4 * total)
-    small = jnp.pad(small, (0, small_rows * 128 - n_small)).reshape(small_rows, 128)
-    small, small_sq = reduce_small(small, total)
-    small = small.reshape(-1)
-    table_grad, vector_grad = small[:n_table], small[n_table:n_small]
-    shared_sq = sum_everywhere(
-        (jnp.sum(feed_sum * feed_sum) + jnp.sum(attend_sum * attend_sum) + small_sq).reshape(1, 1),
-        total,
-    )[0, 0]
+    own_sq = jnp.sum(feed_sum * feed_sum) + jnp.sum(attend_sum * attend_sum)
+    n_vec = vector_grad.shape[0]
+    summed = jnp.pad(vector_grad, (0, round_up(n_vec + 1, 1024) - n_vec)).reshape(-1, 128)
+    spot = (lax.broadcasted_iota(jnp.int32, summed.shape, 0) == n_vec // 128) & (
+        lax.broadcasted_iota(jnp.int32, summed.shape, 1) == n_vec % 128
+    )
+    summed = jnp.where(spot, own_sq, summed)
+    spread_table = to_low(attend_sum[p.ra : p.ra + p.per, lay_cols : lay_cols + wl])
+    distance = total // 2
+    while distance:
+        other = send(summed, distance)
+        theirs = send(after(spread_table, summed), distance)
+        summed = summed + other
+        bit = (me // distance) % 2
+        spread_table = jnp.where(
+            bit == 0, jnp.stack([spread_table, theirs]), jnp.stack([theirs, spread_table])
+        )
+        distance = distance // 2
+    deep = spread_table.ndim - 2
+    order = tuple(range(deep - 1, -1, -1)) + (deep, deep + 1)
+    table_grad = spread_table.transpose(order).reshape(-1, 128).astype(F32)
+    vector_grad = summed
+    all_sq = jnp.sum(jnp.where(spot, 0.0, summed * summed))
+    shared_sq = all_sq + summed[n_vec // 128, n_vec % 128]
     clip_norm = jnp.sqrt(shared_sq)
     factor = jnp.minimum(1.0, CLIP_NORM / (clip_norm + 1e-06))
+    flat = [
+        [v.reshape(-1, 128) for v in group]
+        for group in ((vectors, vectors_mean, vectors_square), (tables, tables_mean, tables_square))
+    ]
     lay_sum = attend_sum[p.ra : p.ra + dl_own]
-    states = [
-        (
-            attend_text,
-            attend_text_mean,
-            attend_text_square,
-            attend_sum[:d_own].reshape(d_own, 4, ct),
-            WEIGHT_DECAY,
-        ),
-        (
-            feed_text,
-            feed_text_mean,
-            feed_text_square,
-            jnp.stack([feed_sum[:d_own], feed_sum[p.ra : p.ra + d_own]], axis=1),
-            WEIGHT_DECAY,
-        ),
-        (
-            attend_layout,
-            attend_layout_mean,
-            attend_layout_square,
-            lay_sum[:, : 4 * cl].reshape(dl_own, 4, cl),
-            WEIGHT_DECAY,
-        ),
-        (
-            feed_layout,
-            feed_layout_mean,
-            feed_layout_square,
-            lay_sum[:, 4 * cl : lay_cols].reshape(dl_own, 2, hl),
-            WEIGHT_DECAY,
-        ),
-        (vectors, vectors_mean, vectors_square, vector_grad, 0.0),
-        (tables, tables_mean, tables_square, table_grad, 0.0),
-    ]
-    updated = []
-    for k in range(6):
-        updated.extend(
-            adamw_step(
-                states[k][0],
-                states[k][1],
-                states[k][2],
-                states[k][3] * factor,
-                states[k][4],
-                LEARN_RATES[k],
-            )
-        )
+    grads = (
+        attend_sum[:d_own].reshape(d_own, 4, ct),
+        jnp.stack([feed_sum[:d_own], feed_sum[p.ra : p.ra + d_own]], axis=1),
+        lay_sum[:, : 4 * cl].reshape(dl_own, 4, cl),
+        lay_sum[:, 4 * cl : lay_cols].reshape(dl_own, 2, hl),
+        vector_grad[: n_vec // 128],
+        table_grad,
+    )
+    matrices = (
+        (attend_text, attend_text_mean, attend_text_square),
+        (feed_text, feed_text_mean, feed_text_square),
+        (attend_layout, attend_layout_mean, attend_layout_square),
+        (feed_layout, feed_layout_mean, feed_layout_square),
+    )
+    updated = update_all(factor, matrices, flat, grads)
+    updated[12:] = [v.reshape(-1) for v in updated[12:]]
     rows_out, rows_grad = pages_of(rows_out), pages_of(rows_grad)
     return (
         rows_out[:, :, :wt],

time: 435 us -> 355 us (0.82)
  waiting for transfers between devices: 134 us -> 71.7 us
  starting transfers between devices: 75.4 us -> 58.9 us
  Pallas kernels: 118 us -> 131 us
  local copies, waits for them, and re-layouts: 41.7 us -> 35.3 us
  other arithmetic: 51.4 us -> 45.7 us
    ppermute x68 -> x64, waiting for transfers between devices: 134 us -> 71.7 us  [xor_send(): return lax.ppermute(values, AXES, [(i, i ^ distance) for i in range(total)])]
    ppermute x68 -> x64, starting transfers between devices: 75.4 us -> 58.9 us  [xor_send(): return lax.ppermute(values, AXES, [(i, i ^ distance) for i in range(total)])]
    pallas_call x8 -> x10, Pallas kernels: 118 us -> 131 us  [kernel_call(): pl.pallas_call(body, out_shape=outs, in_specs=in_specs, out_specs=out_spe...]
    sub x6 -> x0, other arithmetic: 8.55 us -> none  [adamw_step(): weight - rate_now * (moment_hat / (jnp.sqrt(square_hat) + ADAM_EPS) + dec...]
    slice x28 -> x10, local copies, waits for them, and re-layouts: 11.2 us -> 4.73 us  [by_block(): both = jnp.stack([even[0], odd[0], even[1], odd[1]]).reshape(n_t, -1)]
    unnamed x112 -> x99, local copies, waits for them, and re-layouts: 9.78 us -> 6.14 us
    convert_element_type x16 -> x20, other arithmetic: 24.1 us -> 22.8 us  [to_low(): return values.astype(BF16)]
  transfers between devices with their start and end apart: 68 -> 64, of which waited for: 33 -> 21; matrix products, arithmetic and copies ran while one was open for 14% -> 16% of each run, Pallas kernels for 24% -> 32%
where the time goes in v3:
time: 355 us; the launch traced here: 349 us
  Pallas kernels  131 us (37%)
  waiting for transfers between devices  71.7 us (20%)
  starting transfers between devices  58.9 us (17%)
  other arithmetic  45.7 us (13%)
  local copies, waits for them, and re-layouts  35.3 us (10%)
  between operations  6.17 us (2%)
    pallas_call x10, Pallas kernels, kernel_call(): pl.pallas_call(body, out_shape=outs, in_specs=in_specs, out_specs=out_spe...  131 us
    ppermute x64, waiting for transfers between devices, xor_send(): return lax.ppermute(values, AXES, [(i, i ^ distance) for i in range(total)])  71.7 us
    ppermute x64, starting transfers between devices, xor_send(): return lax.ppermute(values, AXES, [(i, i ^ distance) for i in range(total)])  58.9 us
    convert_element_type x20, other arithmetic, to_low(): return values.astype(BF16)  22.8 us
  transfers between devices with their start and end apart: 64, of which 21 were waited for; matrix products, arithmetic and copies ran while one was open for 16% of the time, Pallas kernels for 32%

profile of v3, /device:TPU:0, one launch (start us, length us, event | category | flops | bytes accessed | tf_op | source)
XLA Modules:
  0.0 349.1 jit_solution(17702512382352164433)
XLA Ops:
  4.0 3.1 collective-permute-start
  15.4 8.8 %collective-permute-done.1 = bf16[128,768]{1,0:T(8,128)(2,1)S(1)} collective-permute-done((bf16[128,768]{1,0:T(8,128)(2,1)S(1)}, bf16[128,768]{1,0:T(8,128)(2,1)S(1)}, u32[]{:S(2)}, u32[]{:S(2)}) %collective-permute-start.1) | collective-permute-done | bytes 196640 | tf_op jit(solution)/shard_map/ppermute | solution.py:34
  34.2 2.7 collective-permute-done.7
  48.1 11.9 %collective-permute-done.15 = bf16[2,192,768]{2,1,0:T(8,128)(2,1)} collective-permute-done((bf16[2,192,768]{2,1,0:T(8,128)(2,1)}, bf16[2,192,768]{2,1,0:T(8,128)(2,1)}, u32[]{:S(2)}, u32[]{:S(2)}) %collective-permute-start.15) | collective-permute-done | bytes 589856 | tf_op jit(solution)/shard_map/ppermute | solution.py:34
  63.9 13.7 %shard_map.407 = (bf16[2,768,768]{2,1,0:T(8,128)(2,1)}, bf16[2,192,768]{2,1,0:T(8,128)(2,1)}, bf16[2,9,80,512]{3,2,1,0:T(8,128)(2,1)}, bf16[2,3,80,512]{3,2,1,0:...) custom-call(s32[2]{0:T(128)} %pad_add_fusion.refs_0_, ...), custom_call_target="tpu_custom_call" | custom-call | flops 10000000000 | bytes 1048576 | tf_op jit(solution)/shard_map/pallas_call | solution.py:119
  86.2 13.6 %shard_map.408 = (bf16[2,768,768]{2,1,0:T(8,128)(2,1)}, bf16[2,192,768]{2,1,0:T(8,128)(2,1)}, bf16[2,9,80,512]{3,2,1,0:T(8,128)(2,1)}, bf16[2,3,80,512]{3,2,1,0:...) custom-call(s32[2]{0:T(128)} %pad_add_fusion.refs_0_, ...), custom_call_target="tpu_custom_call" | custom-call | flops 10000000000 | bytes 1048576 | tf_op jit(solution)/shard_map/pallas_call | solution.py:119
  99.8 8.4 %collective-permute-done.19.refs_10_ = bf16[2,4,96,768]{3,2,1,0:T(8,128)(2,1)} collective-permute-done((bf16[2,4,96,768]{3,2,1,0:T(8,128)(2,1)S(1)}, bf16[2,4,96,768]{3,2,1,0:T(8,128)(2,1)}, u32[]{:S(2)}, u32[]{:S(2)}) %collective-permute-start.19) | collective-permute-done | bytes 1179680 | tf_op jit(solution)/shard_map/ppermute | solution.py:34
  114.2 9.8 %shard_map.409 = (bf16[2,2,768,768]{3,2,1,0:T(8,128)(2,1)}, bf16[2,512,768]{2,1,0:T(8,128)(2,1)}, bf16[2,512,768]{2,1,0:T(8,128)(2,1)}, bf16[2,512,192]{2,1,0:T(...) custom-call(s32[2]{0:T(128)} %pad_add_fusion.refs_0_, ...), custom_call_target="tpu_custom_call" | custom-call | flops 10000000000 | bytes 1048576 | tf_op jit(solution)/shard_map/pallas_call | solution.py:119
  126.9 13.0 %shard_map.410 = (bf16[2,2,768,768]{3,2,1,0:T(8,128)(2,1)}, bf16[2,512,768]{2,1,0:T(8,128)(2,1)}, bf16[2,512,768]{2,1,0:T(8,128)(2,1)}, bf16[2,512,192]{2,1,0:T(...) custom-call(s32[2]{0:T(128)} %pad_add_fusion.refs_0_, ...), custom_call_target="tpu_custom_call" | custom-call | flops 10000000000 | bytes 1048576 | tf_op jit(solution)/shard_map/pallas_call | solution.py:119
  143.7 12.7 %shard_map.411 = (bf16[2,2,4,96,768]{4,3,2,1,0:T(8,128)(2,1)}, bf16[2,2,4,96,768]{4,3,2,1,0:T(8,128)(2,1)}, bf16[2,192,384]{2,1,0:T(8,128)(2,1)}, f32[2,1,768]{2...) custom-call(s32[2]{0:T(128)} %pad_add_fusion.refs_0_, ...), custom_call_target="tpu_custom_call" | custom-call | flops 10000000000 | bytes 1048576 | tf_op jit(solution)/shard_map/pallas_call | solution.py:119
  157.9 15.6 %shard_map.412 = (bf16[2,2,4,96,768]{4,3,2,1,0:T(8,128)(2,1)}, bf16[2,2,4,96,768]{4,3,2,1,0:T(8,128)(2,1)}, bf16[2,192,384]{2,1,0:T(8,128)(2,1)}, f32[2,1,768]{2...) custom-call(s32[2]{0:T(128)} %pad_add_fusion.refs_0_, ...), custom_call_target="tpu_custom_call" | custom-call | flops 10000000000 | bytes 1048576 | tf_op jit(solution)/shard_map/pallas_call | solution.py:119
  174.9 4.2 %add_convert_fusion = (bf16[1,2,4,96,768]{4,3,2,1,0:T(8,128)(2,1)S(1)}, bf16[2,4,96,768]{3,2,1,0:T(8,128)(2,1)}) fusion(bf16[2,2,4,96,768]{4,3,2,1,0:T(8,128)(2,1)} %collective-permute-done.31, bf16[2,2,4,96,768]{4,3,2,1,0:T(8,128)(2,1)} %get-tuple-element.368), kind=kLoop, calls=%fused_computation | loop fusion | flops 4718592 | bytes 7077888 | tf_op jit(solution)/shard_map/convert_element_type | solution.py:30
  182.7 18.8 %shard_map.413 = (bf16[2,2,4,64,768]{4,3,2,1,0:T(8,128)(2,1)}, bf16[2,2,4,64,768]{4,3,2,1,0:T(8,128)(2,1)}, f32[2,8,576]{2,1,0:T(8,128)}, f32[2,8,144]{2,1,0:T(8...) custom-call(s32[2]{0:T(128)} %pad_add_fusion.refs_0_, bf16[2,768,768]{2,1,0:T(8,128)(2,1)} %get-tuple-element.373.refs_1_, ...), custom_call_target="tpu_custom_call" | custom-call | flops 10000000000 | bytes 1048576 | tf_op jit(solution)/shard_map/pallas_call | solution.py:119
  201.4 6.4 %collective-permute-done.33 = bf16[2,4,96,768]{3,2,1,0:T(8,128)(2,1)} collective-permute-done((bf16[2,4,96,768]{3,2,1,0:T(8,128)(2,1)}, bf16[2,4,96,768]{3,2,1,0:T(8,128)(2,1)}, u32[]{:S(2)}, u32[]{:S(2)}) %collective-permute-start.33) | collective-permute-done | bytes 1179680 | tf_op jit(solution)/shard_map/ppermute | solution.py:34
  207.8 2.6 collective-permute-done.32
  216.3 12.8 %shard_map.414 = (bf16[1,2,4,64,768]{4,3,2,1,0:T(8,128)(2,1)}, bf16[1,2,4,64,768]{4,3,2,1,0:T(8,128)(2,1)}, f32[1,8,576]{2,1,0:T(8,128)}, f32[1,8,144]{2,1,0:T(8...) custom-call(s32[2]{0:T(128)} %pad_add_fusion.refs_0_, bf16[2,768,768]{2,1,0:T(8,128)(2,1)} %get-tuple-element.337.refs_1_, ...), custom_call_target="tpu_custom_call" | custom-call | flops 10000000000 | bytes 1048576 | tf_op jit(solution)/shard_map/pallas_call | solution.py:119
  236.0 3.3 collective-permute-start.40
  242.9 14.8 %shard_map.415 = (bf16[1,2,4,64,768]{4,3,2,1,0:T(8,128)(2,1)}, bf16[1,2,4,64,768]{4,3,2,1,0:T(8,128)(2,1)}, f32[1,8,576]{2,1,0:T(8,128)}, f32[1,8,144]{2,1,0:T(8...) custom-call(s32[2]{0:T(128)} %pad_add_fusion.refs_0_, ...), custom_call_target="tpu_custom_call" | custom-call | flops 10000000000 | bytes 1048576 | tf_op jit(solution)/shard_map/pallas_call | solution.py:119
  279.2 6.2 %collective-permute-done.50 = bf16[4,64,768]{2,1,0:T(8,128)(2,1)} collective-permute-done((bf16[4,64,768]{2,1,0:T(8,128)(2,1)}, bf16[4,64,768]{2,1,0:T(8,128)(2,1)}, u32[]{:S(2)}, u32[]{:S(2)}) %collective-permute-start.50) | collective-permute-done | bytes 393248 | tf_op jit(solution)/shard_map/ppermute | solution.py:34
  291.0 2.8 collective-permute-start.52
  301.6 6.7 %collective-permute-done.52 = bf16[128,768]{1,0:T(8,128)(2,1)} collective-permute-done((bf16[128,768]{1,0:T(8,128)(2,1)}, bf16[128,768]{1,0:T(8,128)(2,1)}, u32[]{:S(2)}, u32[]{:S(2)}) %collective-permute-start.52) | collective-permute-done | bytes 196640 | tf_op jit(solution)/shard_map/ppermute | solution.py:34
  311.7 3.9 %collective-permute-start.59 = (bf16[32,192]{1,0:T(8,128)(2,1)S(1)}, bf16[32,192]{1,0:T(8,128)(2,1)S(1)}, u32[]{:S(2)}, u32[]{:S(2)}) collective-permute-start(bf16[32,192]{1,0:T(8,128)(2,1)S(1)} %slice.1004), channel_id=1, source_target_pairs={{0,16},{1,17},{2,18},{3,19},{4,20},{5,21},{6,22},{7,23},{8,24},{9,... | collective-permute-start | bytes 36872 | tf_op jit(solution)/shard_map/ppermute | solution.py:34
  333.9 2.7 collective-permute-done.62
  341.2 6.6 %shard_map.416 = (f32[96,4,192]{2,1,0:T(4,128)}, f32[96,4,192]{2,1,0:T(4,128)}, f32[96,4,192]{2,1,0:T(4,128)}, f32[96,2,768]{2,1,0:T(2,128)}, f32[96,2,768]{2,1,...) custom-call(f32[1,1]{1,0:T(1,128)} %bitcast.125.refs_0_, ...), custom_call_target="tpu_custom_call" | custom-call | flops 10000000000 | bytes 1048576 | tf_op jit(solution)/shard_map/pallas_call | solution.py:119
  (402 shorter events, 137.9 us)
Async XLA Ops:
  7.1 17.2 %collective-permute-start.1 = (bf16[128,768]{1,0:T(8,128)(2,1)S(1)}, bf16[128,768]{1,0:T(8,128)(2,1)S(1)}, u32[]{:S(2)}, u32[]{:S(2)}) collective-permute-start(bf16[128,768]{1,0:T(8,128)(2,1)S(1)} %pad_maximum_fusion.16), channel_id=1, source_target_pairs={{0,16},{1,17},{2,18},{3,19},{4,20},{5,21},{6,22},{7,23},{8,24},{9,... | collective-permute-start | bytes 589832 | tf_op jit(solution)/shard_map/ppermute | solution.py:34
  31.8 28.2 %collective-permute-start.15 = (bf16[2,192,768]{2,1,0:T(8,128)(2,1)}, bf16[2,192,768]{2,1,0:T(8,128)(2,1)}, u32[]{:S(2)}, u32[]{:S(2)}) collective-permute-start(bf16[2,192,768]{2,1,0:T(8,128)(2,1)} %pad_maximum_fusion.5), channel_id=1, source_target_pairs={{0,16},{1,17},{2,18},{3,19},{4,20},{5,21},{6,22},{7,23},{8,24},{9,... | collective-permute-start | bytes 1769480 | tf_op jit(solution)/shard_map/ppermute | solution.py:34
  38.1 23.3 %collective-permute-start.9 = (bf16[2,4,64,768]{3,2,1,0:T(8,128)(2,1)S(1)}, bf16[2,4,64,768]{3,2,1,0:T(8,128)(2,1)}, u32[]{:S(2)}, u32[]{:S(2)}) collective-permute-start(bf16[2,4,64,768]{3,2,1,0:T(8,128)(2,1)S(1)} %pad_maximum_fusion.4.refs_14_), channel_id=1, source_target_pairs={{0,2},{1,3},{2,0},{3,1},{4,6},{5,7},{6,4},{7,5},{8,10},{9,11},{10,... | collective-permute-start | bytes 2359304 | tf_op jit(solution)/shard_map/ppermute | solution.py:34
  41.8 19.6 %collective-permute-start.8 = (bf16[2,4,64,768]{3,2,1,0:T(8,128)(2,1)}, bf16[2,4,64,768]{3,2,1,0:T(8,128)(2,1)}, u32[]{:S(2)}, u32[]{:S(2)}) collective-permute-start(bf16[2,4,64,768]{3,2,1,0:T(8,128)(2,1)} %pad_maximum_fusion.3.refs_12_), channel_id=1, source_target_pairs={{0,4},{1,5},{2,6},{3,7},{4,0},{5,1},{6,2},{7,3},{8,12},{9,13},{10,... | collective-permute-start | bytes 2359304 | tf_op jit(solution)/shard_map/ppermute | solution.py:34
  43.5 19.2 %collective-permute-start.13 = (bf16[2,4,64,768]{3,2,1,0:T(8,128)(2,1)S(1)}, bf16[2,4,64,768]{3,2,1,0:T(8,128)(2,1)}, u32[]{:S(2)}, u32[]{:S(2)}) collective-permute-start(bf16[2,4,64,768]{3,2,1,0:T(8,128)(2,1)S(1)} %pad_maximum_fusion.4.refs_14_), channel_id=1, source_target_pairs={{0,1},{1,0},{2,3},{3,2},{4,5},{5,4},{6,7},{7,6},{8,9},{9,8},{10,11... | collective-permute-start | bytes 2359304 | tf_op jit(solution)/shard_map/ppermute | solution.py:34
  43.5 34.0 %collective-permute-start.12 = (bf16[2,4,64,768]{3,2,1,0:T(8,128)(2,1)}, bf16[2,4,64,768]{3,2,1,0:T(8,128)(2,1)}, u32[]{:S(2)}, u32[]{:S(2)}) collective-permute-start(bf16[2,4,64,768]{3,2,1,0:T(8,128)(2,1)} %pad_maximum_fusion.3.refs_12_), channel_id=1, source_target_pairs={{0,1},{1,0},{2,3},{3,2},{4,5},{5,4},{6,7},{7,6},{8,9},{9,8},{10,11... | collective-permute-start | bytes 2359304 | tf_op jit(solution)/shard_map/ppermute | solution.py:34
  80.2 28.0 %collective-permute-start.19 = (bf16[2,4,96,768]{3,2,1,0:T(8,128)(2,1)S(1)}, bf16[2,4,96,768]{3,2,1,0:T(8,128)(2,1)}, u32[]{:S(2)}, u32[]{:S(2)}) collective-permute-start(bf16[2,4,96,768]{3,2,1,0:T(8,128)(2,1)S(1)} %pad_maximum_fusion.1.refs_9_), channel_id=1, source_target_pairs={{0,2},{1,3},{2,0},{3,1},{4,6},{5,7},{6,4},{7,5},{8,10},{9,11},{10,... | collective-permute-start | bytes 3538952 | tf_op jit(solution)/shard_map/ppermute | solution.py:34
  81.9 27.8 %collective-permute-start.18 = (bf16[2,4,96,768]{3,2,1,0:T(8,128)(2,1)S(1)}, bf16[2,4,96,768]{3,2,1,0:T(8,128)(2,1)}, u32[]{:S(2)}, u32[]{:S(2)}) collective-permute-start(bf16[2,4,96,768]{3,2,1,0:T(8,128)(2,1)S(1)} %pad_maximum_fusion.refs_7_), channel_id=1, source_target_pairs={{0,4},{1,5},{2,6},{3,7},{4,0},{5,1},{6,2},{7,3},{8,12},{9,13},{10,... | collective-permute-start | bytes 3538952 | tf_op jit(solution)/shard_map/ppermute | solution.py:34
  85.6 26.7 %collective-permute-start.23 = (bf16[2,4,96,768]{3,2,1,0:T(8,128)(2,1)S(1)}, bf16[2,4,96,768]{3,2,1,0:T(8,128)(2,1)}, u32[]{:S(2)}, u32[]{:S(2)}) collective-permute-start(bf16[2,4,96,768]{3,2,1,0:T(8,128)(2,1)S(1)} %pad_maximum_fusion.1.refs_9_), channel_id=1, source_target_pairs={{0,1},{1,0},{2,3},{3,2},{4,5},{5,4},{6,7},{7,6},{8,9},{9,8},{10,11... | collective-permute-start | bytes 3538952 | tf_op jit(solution)/shard_map/ppermute | solution.py:34
  85.7 27.2 %collective-permute-start.22 = (bf16[2,4,96,768]{3,2,1,0:T(8,128)(2,1)S(1)}, bf16[2,4,96,768]{3,2,1,0:T(8,128)(2,1)}, u32[]{:S(2)}, u32[]{:S(2)}) collective-permute-start(bf16[2,4,96,768]{3,2,1,0:T(8,128)(2,1)S(1)} %pad_maximum_fusion.refs_7_), channel_id=1, source_target_pairs={{0,1},{1,0},{2,3},{3,2},{4,5},{5,4},{6,7},{7,6},{8,9},{9,8},{10,11... | collective-permute-start | bytes 3538952 | tf_op jit(solution)/shard_map/ppermute | solution.py:34
  179.1 28.7 %collective-permute-start.33 = (bf16[2,4,96,768]{3,2,1,0:T(8,128)(2,1)}, bf16[2,4,96,768]{3,2,1,0:T(8,128)(2,1)}, u32[]{:S(2)}, u32[]{:S(2)}) collective-permute-start(bf16[2,4,96,768]{3,2,1,0:T(8,128)(2,1)} %get-tuple-element.491), channel_id=1, source_target_pairs={{0,4},{1,5},{2,6},{3,7},{4,0},{5,1},{6,2},{7,3},{8,12},{9,13},{10,... | collective-permute-start | bytes 3538952 | tf_op jit(solution)/shard_map/ppermute | solution.py:34
  182.1 28.3 %collective-permute-start.32 = (bf16[2,4,96,768]{3,2,1,0:T(8,128)(2,1)}, bf16[2,4,96,768]{3,2,1,0:T(8,128)(2,1)S(1)}, u32[]{:S(2)}, u32[]{:S(2)}) collective-permute-start(bf16[2,4,96,768]{3,2,1,0:T(8,128)(2,1)} %get-tuple-element.493), channel_id=1, source_target_pairs={{0,2},{1,3},{2,0},{3,1},{4,6},{5,7},{6,4},{7,5},{8,10},{9,11},{10,... | collective-permute-start | bytes 3538952 | tf_op jit(solution)/shard_map/ppermute | solution.py:34
  210.4 19.8 %collective-permute-start.34 = (bf16[2,2,4,64,768]{4,3,2,1,0:T(8,128)(2,1)}, bf16[2,2,4,64,768]{4,3,2,1,0:T(8,128)(2,1)}, u32[]{:S(2)}, u32[]{:S(2)}) collective-permute-start(bf16[2,2,4,64,768]{4,3,2,1,0:T(8,128)(2,1)} %get-tuple-element.384), channel_id=1, source_target_pairs={{0,1},{1,0},{2,3},{3,2},{4,5},{5,4},{6,7},{7,6},{8,9},{9,8},{10,11... | collective-permute-start | bytes 4718600 | tf_op jit(solution)/shard_map/ppermute | solution.py:34
  210.4 19.8 %collective-permute-start.35 = (bf16[2,2,4,64,768]{4,3,2,1,0:T(8,128)(2,1)}, bf16[2,2,4,64,768]{4,3,2,1,0:T(8,128)(2,1)}, u32[]{:S(2)}, u32[]{:S(2)}) collective-permute-start(bf16[2,2,4,64,768]{4,3,2,1,0:T(8,128)(2,1)} %get-tuple-element.385), channel_id=1, source_target_pairs={{0,1},{1,0},{2,3},{3,2},{4,5},{5,4},{6,7},{7,6},{8,9},{9,8},{10,11... | collective-permute-start | bytes 4718600 | tf_op jit(solution)/shard_map/ppermute | solution.py:34
  232.6 25.2 %collective-permute-start.38 = (bf16[4,64,768]{2,1,0:T(8,128)(2,1)}, bf16[4,64,768]{2,1,0:T(8,128)(2,1)}, u32[]{:S(2)}, u32[]{:S(2)}) collective-permute-start(bf16[4,64,768]{2,1,0:T(8,128)(2,1)} %slice_bitcast_fusion.8), channel_id=1, source_target_pairs={{0,4},{1,5},{2,6},{3,7},{4,0},{5,1},{6,2},{7,3},{8,12},{9,13},{10,... | collective-permute-start | bytes 1179656 | tf_op jit(solution)/shard_map/ppermute | solution.py:34
  234.4 23.4 %collective-permute-start.41 = (bf16[192,768]{1,0:T(8,128)(2,1)}, bf16[192,768]{1,0:T(8,128)(2,1)}, u32[]{:S(2)}, u32[]{:S(2)}) collective-permute-start(bf16[192,768]{1,0:T(8,128)(2,1)} %pad_maximum_fusion.14), channel_id=1, source_target_pairs={{0,16},{1,17},{2,18},{3,19},{4,20},{5,21},{6,22},{7,23},{8,24},{9,... | collective-permute-start | bytes 884744 | tf_op jit(solution)/shard_map/ppermute | solution.py:34
  236.0 21.8 %collective-permute-start.40 = (bf16[192,768]{1,0:T(8,128)(2,1)}, bf16[192,768]{1,0:T(8,128)(2,1)}, u32[]{:S(2)}, u32[]{:S(2)}) collective-permute-start(bf16[192,768]{1,0:T(8,128)(2,1)} %pad_maximum_fusion.13), channel_id=1, source_target_pairs={{0,8},{1,9},{2,10},{3,11},{4,12},{5,13},{6,14},{7,15},{8,0},{9,1},... | collective-permute-start | bytes 884744 | tf_op jit(solution)/shard_map/ppermute | solution.py:34
  240.6 17.2 %collective-permute-start.39 = (bf16[2,4,64,768]{3,2,1,0:T(8,128)(2,1)S(1)}, bf16[2,4,64,768]{3,2,1,0:T(8,128)(2,1)S(1)}, u32[]{:S(2)}, u32[]{:S(2)}) collective-permute-start(bf16[2,4,64,768]{3,2,1,0:T(8,128)(2,1)S(1)} %fusion.10), channel_id=1, source_target_pairs={{0,2},{1,3},{2,0},{3,1},{4,6},{5,7},{6,4},{7,5},{8,10},{9,11},{10,... | collective-permute-start | bytes 2359304 | tf_op jit(solution)/shard_map/ppermute | solution.py:34
  267.4 17.9 %collective-permute-start.50 = (bf16[4,64,768]{2,1,0:T(8,128)(2,1)}, bf16[4,64,768]{2,1,0:T(8,128)(2,1)}, u32[]{:S(2)}, u32[]{:S(2)}) collective-permute-start(bf16[4,64,768]{2,1,0:T(8,128)(2,1)} %slice_bitcast_fusion.4), channel_id=1, source_target_pairs={{0,4},{1,5},{2,6},{3,7},{4,0},{5,1},{6,2},{7,3},{8,12},{9,13},{10,... | collective-permute-start | bytes 1179656 | tf_op jit(solution)/shard_map/ppermute | solution.py:34
  269.1 17.3 %collective-permute-start.45 = (bf16[4,64,768]{2,1,0:T(8,128)(2,1)S(1)}, bf16[4,64,768]{2,1,0:T(8,128)(2,1)S(1)}, u32[]{:S(2)}, u32[]{:S(2)}) collective-permute-start(bf16[4,64,768]{2,1,0:T(8,128)(2,1)S(1)} %fusion.13), channel_id=1, source_target_pairs={{0,2},{1,3},{2,0},{3,1},{4,6},{5,7},{6,4},{7,5},{8,10},{9,11},{10,... | collective-permute-start | bytes 1179656 | tf_op jit(solution)/shard_map/ppermute | solution.py:34
  291.0 17.2 %collective-permute-start.52 = (bf16[128,768]{1,0:T(8,128)(2,1)}, bf16[128,768]{1,0:T(8,128)(2,1)}, u32[]{:S(2)}, u32[]{:S(2)}) collective-permute-start(bf16[128,768]{1,0:T(8,128)(2,1)} %pad_maximum_fusion.18), channel_id=1, source_target_pairs={{0,16},{1,17},{2,18},{3,19},{4,20},{5,21},{6,22},{7,23},{8,24},{9,... | collective-permute-start | bytes 589832 | tf_op jit(solution)/shard_map/ppermute | solution.py:34
  297.2 25.7 %collective-permute-start.46 = (bf16[128,960]{1,0:T(8,128)(2,1)}, bf16[128,960]{1,0:T(8,128)(2,1)S(1)}, u32[]{:S(2)}, u32[]{:S(2)}) collective-permute-start(bf16[128,960]{1,0:T(8,128)(2,1)} %get-tuple-element.512), channel_id=1, source_target_pairs={{0,1},{1,0},{2,3},{3,2},{4,5},{5,4},{6,7},{7,6},{8,9},{9,8},{10,11... | collective-permute-start | bytes 737288 | tf_op jit(solution)/shard_map/ppermute | solution.py:34
  297.2 25.7 %collective-permute-start.47 = (bf16[128,960]{1,0:T(8,128)(2,1)S(1)}, bf16[128,960]{1,0:T(8,128)(2,1)S(1)}, u32[]{:S(2)}, u32[]{:S(2)}) collective-permute-start(bf16[128,960]{1,0:T(8,128)(2,1)S(1)} %get-tuple-element.511), channel_id=1, source_target_pairs={{0,2},{1,3},{2,0},{3,1},{4,6},{5,7},{6,4},{7,5},{8,10},{9,11},{10,... | collective-permute-start | bytes 737288 | tf_op jit(solution)/shard_map/ppermute | solution.py:34
  301.1 21.8 %collective-permute-start.48 = (bf16[128,960]{1,0:T(8,128)(2,1)S(1)}, bf16[128,960]{1,0:T(8,128)(2,1)S(1)}, u32[]{:S(2)}, u32[]{:S(2)}) collective-permute-start(bf16[128,960]{1,0:T(8,128)(2,1)S(1)} %get-tuple-element.510), channel_id=1, source_target_pairs={{0,3},{1,2},{2,1},{3,0},{4,7},{5,6},{6,5},{7,4},{8,11},{9,10},{10,... | collective-permute-start | bytes 737288 | tf_op jit(solution)/shard_map/ppermute | solution.py:34
  (86 other events, 655.0 us)

commit v4 on v3

--- a/solution.py
+++ b/solution.py
@@ -305,21 +305,17 @@
     )
 
 
-def feed_forward(p, me2, core, pieces, w_lay, h_t, h_l, bin_t, bin_l, spread_t, rest_in):
+def feed_forward(p, me2, pieces, w_lay, h_t, h_l, bin_t, bin_l, spread_t):
     rows = p.rows
     padded_t = p.n_dp * p.ra
     exact_t = p.ra == p.d_own
     root = 1.0 / math.sqrt(2.0)
-    first = core == 0
     nb = p.n_t // 2
-    n_rest = len(rest_in)
 
     def body(*refs):
         (me_ref, wl, ht, hl, bt, bl, spt), refs = refs[:7], refs[7:]
-        rest_refs, refs = refs[:n_rest], refs[n_rest:]
         piece_refs, refs = refs[:4], refs[4:]
-        n_out = 7 if first else 13
-        outs, scratch = refs[:n_out], refs[n_out:]
+        outs, scratch = refs[:7], refs[7:]
         f_out, g_t, gp_t, g_l, gp_l = outs[:5]
         fpad, acc_t, acc_l, sem_t, sem_out = scratch
         my_dp, my_t = me_ref[0], me_ref[1]
@@ -332,13 +328,8 @@
                         pltpu.make_async_copy(
                             src.at[z], fpad.at[k, m, pl.ds(row, p.ra)], sem_t.at[k]
                         ).start()
-        if first:
-            acc_t[...] = jnp.zeros_like(acc_t)
-            acc_l[...] = jnp.zeros_like(acc_l)
-        else:
-            acc_t_in, acc_l_in, n1t_, n1l_, c0, c1, c2, c3, vt, vl = rest_refs
-            acc_t[...] = acc_t_in[...]
-            acc_l[...] = acc_l_in[...]
+        acc_t[...] = jnp.zeros_like(acc_t)
+        acc_l[...] = jnp.zeros_like(acc_l)
 
         def gelu(u, g_ref, gp_ref, k):
             cdf = 0.5 + 0.5 * lax.erf(u * root)
@@ -357,7 +348,7 @@
                 fpad.at[k, :, pl.ds(0, p.wt)], f_out.at[k], sem_out
             )
             out_copy.start()
-            own_t = (2 * k + core) ^ my_t
+            own_t = (2 * k) ^ my_t
             g = gelu(dot(ht[...], fpad[k, 0, pl.ds(0, p.wt)]) + bt[own_t], g_t, gp_t, k)
             acc_t[...] += dot(g, fpad[k, 1, pl.ds(0, p.wt)], 1, 1)
             w = wl[k]
@@ -369,29 +360,8 @@
             return carry
 
         lax.fori_loop(0, nb, block, 0)
-        if first:
-            outs[5][...] = acc_t[...]
-            outs[6][...] = acc_l[...]
-        else:
-            out_tl, dr_t, dr_l, df_t, df_l, gv_t, gv_l, _ = outs[5:]
-            cot = jnp.concatenate([ref[...] for ref in (c0, c1, c2, c3)], axis=0).astype(F32)
-            for n1, acc, vec, begin, dr_ref, df_ref, gv in (
-                (n1t_, acc_t, vt, 0, dr_t, df_t, gv_t),
-                (n1l_, acc_l, vl, p.wt, dr_l, df_l, gv_l),
-            ):
-                width = n1.shape[1]
-                ct = cot[:, begin : begin + width]
-                h1 = n1[...] * vec[3:4] + vec[4:5]
-                n2, inv2 = norm_parts(h1 + acc[...] + vec[5:6])
-                out_tl[:, pl.ds(begin, width)] = (n2 * vec[6:7] + vec[7:8]).astype(BF16)
-                dr = norm_back(ct, n2, inv2, vec[6:7])
-                dr_ref[...] = dr
-                df_ref[...] = dr.astype(BF16)
-                gv[...] = jnp.zeros_like(gv)
-                gv[5:6] = col_sum(dr)
-                gv[6:7] = col_sum(ct * n2)
-                gv[7:8] = col_sum(ct)
-            outs[12][...] = jnp.zeros_like(outs[12])
+        outs[5][...] = acc_t[...]
+        outs[6][...] = acc_l[...]
 
     outs = [
         shape((nb, 2, p.wt, p.ht), BF16),
@@ -400,19 +370,7 @@
         shape((nb, rows, p.hl), BF16),
         shape((nb, rows, p.hl), BF16),
     ]
-    if first:
-        outs += [shape((rows, p.wt), F32), shape((rows, p.wl), F32)]
-    else:
-        outs += [
-            shape((rows, p.wt + p.wl), BF16),
-            shape((rows, p.wt), F32),
-            shape((rows, p.wl), F32),
-            shape((rows, p.wt), BF16),
-            shape((rows, p.wl), BF16),
-            shape((8, p.wt), F32),
-            shape((8, p.wl), F32),
-            shape((8, 128), F32),
-        ]
+    outs += [shape((rows, p.wt), F32), shape((rows, p.wl), F32)]
     scratch = [
         pltpu.VMEM((nb, 2, padded_t, p.ht), BF16),
         pltpu.VMEM((rows, p.wt), F32),
@@ -420,14 +378,147 @@
         pltpu.SemaphoreType.DMA((nb,)),
         pltpu.SemaphoreType.DMA,
     ]
-    args = (me2, w_lay, h_t, h_l, bin_t, bin_l, spread_t, *rest_in, *pieces)
+    args = (me2, w_lay, h_t, h_l, bin_t, bin_l, spread_t, *pieces)
     return kernel_call(
         body,
         outs,
-        [SM] + [VM] * (6 + n_rest) + [ANY] * 4,
+        [SM] + [VM] * 6 + [ANY] * 4,
         [ANY] + [VM] * (len(outs) - 1),
         scratch,
         args,
+    )
+
+
+def feed_middle(p, me2, pieces, w_lay, h_t, h_l, bin_t, bin_l, spread_t, rest_in):
+    rows = p.rows
+    padded_t = p.n_dp * p.ra
+    exact_t = p.ra == p.d_own
+    root = 1.0 / math.sqrt(2.0)
+    nb = p.n_t // 2
+
+    def body(*refs):
+        (me_ref, wl, ht, hl, bt, bl, spt), refs = refs[:7], refs[7:]
+        (acc_t_in, acc_l_in, n1t_, n1l_, c0, c1, c2, c3, vt, vl), refs = refs[:10], refs[10:]
+        piece_refs, refs = refs[:4], refs[4:]
+        outs, scratch = refs[:14], refs[14:]
+        (low, high, gfl, dbt, dbl, out_tl, dr_t, dr_l, df_t, df_l, gv_t, gv_l, dh_t, dh_l) = outs
+        fpad, staged, acc_t, acc_l, g_t, gp_t, g_l, gp_l, sem_t, sem_out = scratch
+        my_dp, my_t = me_ref[0], me_ref[1]
+        for k in range(nb):
+            for m in range(2):
+                for y in range(2):
+                    src = piece_refs[y].at[k] if m == 0 else piece_refs[2 + k].at[y]
+                    for z in range(p.far):
+                        row = pl.multiple_of(((z * 2 + y) ^ my_dp) * p.ra, 16)
+                        pltpu.make_async_copy(
+                            src.at[z], fpad.at[k, m, pl.ds(row, p.ra)], sem_t.at[k]
+                        ).start()
+        acc_t[...] = acc_t_in[...]
+        acc_l[...] = acc_l_in[...]
+
+        def gelu(u, g_ref, gp_ref, k):
+            cdf = 0.5 + 0.5 * lax.erf(u * root)
+            value = (u * cdf).astype(BF16)
+            g_ref[k] = value
+            dens = jnp.exp(u * u * -0.5) * (1.0 / math.sqrt(2.0 * math.pi))
+            gp_ref[k] = cdf + u * dens
+            return value
+
+        for k in range(nb):
+            wait_for(fpad.at[k], sem_t.at[k])
+            if not exact_t:
+                for m in range(2):
+                    fpad[k, m, pl.ds(0, p.wt)] = dot(spt[...], fpad[k, m]).astype(BF16)
+            own_t = (2 * k + 1) ^ my_t
+            g = gelu(dot(ht[...], fpad[k, 0, pl.ds(0, p.wt)]) + bt[own_t], g_t, gp_t, k)
+            acc_t[...] += dot(g, fpad[k, 1, pl.ds(0, p.wt)], 1, 1)
+            w = wl[k]
+            up = w[:, 4 * p.cl : 4 * p.cl + p.hl]
+            down = w[:, 4 * p.cl + p.hl : p.lay_cols]
+            g = gelu(dot(hl[...], up) + bl[own_t], g_l, gp_l, k)
+            acc_l[...] += dot(g, down, 1, 1)
+        for n1, acc, vec, begin, dr_ref, df_ref, gv in (
+            (n1t_, acc_t, vt, 0, dr_t, df_t, gv_t),
+            (n1l_, acc_l, vl, p.wt, dr_l, df_l, gv_l),
+        ):
+            width = n1.shape[1]
+            per = p.quarter
+            h1 = n1[...] * vec[3:4] + vec[4:5]
+            n2, inv2 = norm_parts(h1 + acc[...] + vec[5:6])
+            out_tl[:, pl.ds(begin, width)] = (n2 * vec[6:7] + vec[7:8]).astype(BF16)
+            ct = jnp.concatenate([ref[:, begin : begin + width] for ref in (c0, c1, c2, c3)], axis=0).astype(F32)
+            dr = norm_back(ct, n2, inv2, vec[6:7])
+            dr_ref[...] = dr
+            df_ref[...] = dr.astype(BF16)
+            gv[...] = jnp.zeros_like(gv)
+            gv[5:6] = col_sum(dr)
+            gv[6:7] = col_sum(ct * n2)
+            gv[7:8] = col_sum(ct)
+        df, dfl = df_t[...], df_l[...]
+        dfT, hT, dfTl, hTl = df.T, ht[...].T, dfl.T, hl[...].T
+        for k in range(nb):
+            du = dot(df, fpad[k, 1, pl.ds(0, p.wt)]) * gp_t[k]
+            dbt[k] = col_sum(du)
+            du_low = du.astype(BF16)
+            grads = (dot(hT, du_low).astype(BF16), dot(dfT, g_t[k]).astype(BF16))
+            for m in range(2):
+                value = grads[m]
+                if not exact_t:
+                    value = dot(spt[...], value, 0, 0).astype(BF16)
+                staged[k, m] = value
+                slot = (lambda d, y, z: low.at[k, y, z]) if m == 0 else (lambda d, y, z: high.at[y, k, z])
+                store_slots(p, staged.at[k, m], slot, my_dp, sem_out, [(0, p.ra, 0, p.ra, 0)])
+            more = dot(du_low, fpad[k, 0, pl.ds(0, p.wt)], 1, 1)
+            if k == 0:
+                dh_t[...] = more
+            else:
+                dh_t[...] += more
+            w = wl[k]
+            up = w[:, 4 * p.cl : 4 * p.cl + p.hl]
+            down = w[:, 4 * p.cl + p.hl : p.lay_cols]
+            du = dot(dfl, down) * gp_l[k]
+            dbl[k] = col_sum(du)
+            du_low = du.astype(BF16)
+            gfl[k, :, pl.ds(0, p.hl)] = dot(hTl, du_low).astype(BF16)
+            gfl[k, :, pl.ds(p.hl, p.hl)] = dot(dfTl, g_l[k]).astype(BF16)
+            more = dot(du_low, up, 1, 1)
+            if k == 0:
+                dh_l[...] = more
+            else:
+                dh_l[...] += more
+        wait_for(staged, sem_out)
+
+    outs = [
+        shape((2, 2, p.far, p.ra, p.ht), BF16),
+        shape((2, 2, p.far, p.ra, p.ht), BF16),
+        shape((nb, p.wl, 2 * p.hl), BF16),
+        shape((nb, 1, p.ht), F32),
+        shape((nb, 1, p.hl), F32),
+        shape((rows, p.wt + p.wl), BF16),
+        shape((rows, p.wt), F32),
+        shape((rows, p.wl), F32),
+        shape((rows, p.wt), BF16),
+        shape((rows, p.wl), BF16),
+        shape((8, p.wt), F32),
+        shape((8, p.wl), F32),
+        shape((rows, p.wt), F32),
+        shape((rows, p.wl), F32),
+    ]
+    scratch = [
+        pltpu.VMEM((nb, 2, padded_t, p.ht), BF16),
+        pltpu.VMEM((nb, 2, padded_t, p.ht), BF16),
+        pltpu.VMEM((rows, p.wt), F32),
+        pltpu.VMEM((rows, p.wl), F32),
+        pltpu.VMEM((nb, rows, p.ht), BF16),
+        pltpu.VMEM((nb, rows, p.ht), F32),
+        pltpu.VMEM((nb, rows, p.hl), BF16),
+        pltpu.VMEM((nb, rows, p.hl), F32),
+        pltpu.SemaphoreType.DMA((nb,)),
+        pltpu.SemaphoreType.DMA,
+    ]
+    args = (me2, w_lay, h_t, h_l, bin_t, bin_l, spread_t, *rest_in, *pieces)
+    return kernel_call(
+        body, outs, [SM] + [VM] * 16 + [ANY] * 4, [ANY, ANY] + [VM] * 12, scratch, args
     )
 
 
@@ -443,34 +534,26 @@
                 ).start()
 
 
-def feed_backward(p, me2, f_all, w_lay, h_t, h_l, df_t, df_l, g_t, gp_t, g_l, gp_l, spread_t, prev, last):
+def feed_backward(p, me2, f_all, w_lay, h_t, h_l, df_t, df_l, g_t, gp_t, g_l, gp_l, spread_t, prev):
     n_t, rows = p.n_t, p.rows
     padded_t = p.n_dp * p.ra
     exact_t = p.ra == p.d_own
-    blocks = [t for t in range(n_t) if t % 2 == (0 if last else 1)]
+    nb = n_t // 2
 
     def body(*refs):
         (me_ref, f_any, wl, ht, hl, dft, dfl, gt, gpt, gl, gpl, spt), refs = refs[:12], refs[12:]
-        if last:
-            (pt, pl_, drt, drl, n1t, i1t, n1l, i1l, vt, vl), refs = refs[:10], refs[10:]
-            n_out = 11
-        else:
-            n_out = 7
-        outs, scratch = refs[:n_out], refs[n_out:]
+        (pt, pl_, drt, drl, n1t, i1t, n1l, i1l, vt, vl), refs = refs[:10], refs[10:]
+        outs, scratch = refs[:11], refs[11:]
         low, high, gfl, dbt, dbl = outs[:5]
         f_in, staged, acc_t, acc_l, sem_in, sem_out = scratch
         my_dp, my_t = me_ref[0], me_ref[1]
-        for k, t in enumerate(blocks):
+        for k in range(nb):
             pltpu.make_async_copy(f_any.at[k], f_in.at[k], sem_in.at[k]).start()
         dfT, hT = dft[...].T, ht[...].T
         dfTl, hTl = dfl[...].T, hl[...].T
-        if last:
-            acc_t[...] = pt[...]
-            acc_l[...] = pl_[...]
-        else:
-            acc_t[...] = jnp.zeros_like(acc_t)
-            acc_l[...] = jnp.zeros_like(acc_l)
-        for k, t in enumerate(blocks):
+        acc_t[...] = pt[...]
+        acc_l[...] = pl_[...]
+        for k in range(nb):
             wait_for(f_in.at[k], sem_in.at[k])
             du = dot(dft[...], f_in[k, 1]) * gpt[k].astype(F32)
             dbt[k] = col_sum(du)
@@ -481,11 +564,10 @@
                 if not exact_t:
                     value = dot(spt[...], value, 0, 0).astype(BF16)
                 staged[k, m] = value
-                x = t // 2
                 if m == 0:
-                    store_slots(p, staged.at[k, m], lambda d, y, z: low.at[x, y, z], my_dp, sem_out, [(0, p.ra, 0, p.ra, 0)])
+                    store_slots(p, staged.at[k, m], lambda d, y, z: low.at[k, y, z], my_dp, sem_out, [(0, p.ra, 0, p.ra, 0)])
                 else:
-                    store_slots(p, staged.at[k, m], lambda d, y, z: high.at[y, x, z], my_dp, sem_out, [(0, p.ra, 0, p.ra, 0)])
+                    store_slots(p, staged.at[k, m], lambda d, y, z: high.at[y, k, z], my_dp, sem_out, [(0, p.ra, 0, p.ra, 0)])
             acc_t[...] += dot(du_low, f_in[k, 0], 1, 1)
             w = wl[k]
             up = w[:, 4 * p.cl : 4 * p.cl + p.hl]
@@ -496,27 +578,22 @@
             gfl[k, :, pl.ds(0, p.hl)] = dot(hTl, du_low).astype(BF16)
             gfl[k, :, pl.ds(p.hl, p.hl)] = dot(dfTl, gl[k]).astype(BF16)
             acc_l[...] += dot(du_low, up, 1, 1)
-        if last:
-            dr1t, dr1l, dat, dal, gvt, gvl = outs[5:]
-            for dr, acc, n1, i1, vec, o, low_o, gv in (
-                (drt, acc_t, n1t, i1t, vt, dr1t, dat, gvt),
-                (drl, acc_l, n1l, i1l, vl, dr1l, dal, gvl),
-            ):
-                dh = dr[...] + acc[...]
-                n = n1[...]
-                dr1 = norm_back(dh, n, i1[...], vec[3:4])
-                o[...] = dr1
-                low_o[...] = dr1.astype(BF16)
-                gv[...] = jnp.zeros_like(gv)
-                gv[2:3] = col_sum(dr1)
-                gv[3:4] = col_sum(dh * n)
-                gv[4:5] = col_sum(dh)
-        else:
-            outs[5][...] = acc_t[...]
-            outs[6][...] = acc_l[...]
+        dr1t, dr1l, dat, dal, gvt, gvl = outs[5:]
+        for dr, acc, n1, i1, vec, o, low_o, gv in (
+            (drt, acc_t, n1t, i1t, vt, dr1t, dat, gvt),
+            (drl, acc_l, n1l, i1l, vl, dr1l, dal, gvl),
+        ):
+            dh = dr[...] + acc[...]
+            n = n1[...]
+            dr1 = norm_back(dh, n, i1[...], vec[3:4])
+            o[...] = dr1
+            low_o[...] = dr1.astype(BF16)
+            gv[...] = jnp.zeros_like(gv)
+            gv[2:3] = col_sum(dr1)
+            gv[3:4] = col_sum(dh * n)
+            gv[4:5] = col_sum(dh)
         wait_for(staged, sem_out)
 
-    nb = len(blocks)
     outs = [
         shape((2, 2, p.far, p.ra, p.ht), BF16),
         shape((2, 2, p.far, p.ra, p.ht), BF16),
@@ -525,18 +602,15 @@
         shape((nb, 1, p.hl), F32),
     ]
     args = [me2, f_all, w_lay, h_t, h_l, df_t, df_l, g_t, gp_t, g_l, gp_l, spread_t]
-    if last:
-        args += list(prev)
-        outs += [
-            shape((rows, p.wt), F32),
-            shape((rows, p.wl), F32),
-            shape((rows, p.wt), BF16),
-            shape((rows, p.wl), BF16),
-            shape((8, p.wt), F32),
-            shape((8, p.wl), F32),
-        ]
-    else:
-        outs += [shape((rows, p.wt), F32), shape((rows, p.wl), F32)]
+    args += list(prev)
+    outs += [
+        shape((rows, p.wt), F32),
+        shape((rows, p.wl), F32),
+        shape((rows, p.wt), BF16),
+        shape((rows, p.wl), BF16),
+        shape((8, p.wt), F32),
+        shape((8, p.wl), F32),
+    ]
     scratch = [
         pltpu.VMEM((nb, 2, p.wt, p.ht), BF16),
         pltpu.VMEM((nb, 2, padded_t, p.ht), BF16),
@@ -551,23 +625,27 @@
     )
 
 
-def attend_backward(p, me2, xs, w_all, w_lay, qkv, ctx, lse, x_low, lay_low, ints, ints_t, da_t, da_l, gfl, spread_t, spread_l, prev, last):
+def attend_backward(p, me2, xs, cores, x_low, lay_low, ints, ints_t, da_t, da_l, spread_t, spread_l, prev, last):
     n_t, rows, hw, nh = p.n_t, p.rows, p.hw, p.heads
     padded_t, padded_l = p.n_dp * p.ra, p.n_dp * p.rl
     exact_t = p.ra == p.d_own
     nb = len(xs)
-    n_prev = len(prev)
+    n_prev, n_core = len(prev), len(cores)
 
     def body(*refs):
-        (me_ref, w_any, wl_ref, qkv_r, ctx_r, lse_r, xl, ll, ir, itr, dat, dal, gfl_r, spt, spl), refs = refs[:15], refs[15:]
+        (me_ref, xl, ll, ir, itr, dat, dal, spt, spl), refs = refs[:9], refs[9:]
+        core_refs = [refs[6 * c : 6 * c + 6] for c in range(n_core)]
+        refs = refs[6 * n_core :]
         prev_refs, refs = refs[:n_prev], refs[n_prev:]
-        outs, scratch = refs[:6], refs[6:]
-        low, high, gb_t, gb_l, out_a, out_b = outs
+        n_out = 2 * n_core + 4
+        outs, scratch = refs[:n_out], refs[n_out:]
+        slot_refs = [outs[2 * c : 2 * c + 2] for c in range(n_core)]
+        gb_t, gb_l, out_a, out_b = outs[2 * n_core :]
         (w_in, staged, staged_l, acc_t, acc_l, dctx, ctx_s, ctx_l, dp_t, dp_l, bin_rows, sem_in,
          sem_out, sem_bin) = scratch
         my_dp, my_t = me_ref[0], me_ref[1]
-        for k, x in enumerate(xs):
-            pltpu.make_async_copy(w_any.at[x], w_in.at[k], sem_in.at[k]).start()
+        for k, (c, x) in enumerate(xs):
+            pltpu.make_async_copy(core_refs[c][0].at[x], w_in.at[k], sem_in.at[k]).start()
         xT, lT = xl[...].T, ll[...].T
         daT, dalT = dat[...].T, dal[...].T
         seg_col, seg_row = ir[:, 0:1], itr[0:1, :]
@@ -578,7 +656,10 @@
             acc_t[...] = jnp.zeros_like(acc_t)
             acc_l[...] = jnp.zeros_like(acc_l)
         ones = jnp.ones((16, rows), BF16)
-        for k, x in enumerate(xs):
+        for k, (c, x) in enumerate(xs):
+            _, wl_ref, qkv_r, ctx_r, lse_r, gfl_r = core_refs[c]
+            low, high = slot_refs[c]
+            at_k = sum(1 for d, _ in xs[:k] if d == c)
             wait_for(w_in.at[k], sem_in.at[k])
             w = w_in[k]
             wl = wl_ref[x]
@@ -609,9 +690,9 @@
                 dq_l = dot(key[HD:], ds_l) * (1.0 / math.sqrt(LHD))
                 dk_t = dot(q[:HD], ds_t, 1, 1)
                 dk_l = dot(q[HD:], ds_l, 1, 1)
-                for c, (top, bot) in enumerate(((dq_t, dq_l), (dk_t, dk_l), (dv[:HD], dv[HD:]))):
-                    dp_t[pl.ds(c * p.ct + h * HD, HD)] = top.astype(BF16)
-                    dp_l[pl.ds(c * p.cl + h * LHD, LHD)] = bot.astype(BF16)
+                for m, (top, bot) in enumerate(((dq_t, dq_l), (dk_t, dk_l), (dv[:HD], dv[HD:]))):
+                    dp_t[pl.ds(m * p.ct + h * HD, HD)] = top.astype(BF16)
+                    dp_l[pl.ds(m * p.cl + h * LHD, LHD)] = bot.astype(BF16)
             gb_t[k] = dot(ones, dp_t[...], 1, 1)[:8]
             gb_l[k] = dot(ones, dp_l[...], 1, 1)[:8]
             acc_t[...] += dot(w[:, : 3 * p.ct], dp_t[...])
@@ -634,7 +715,7 @@
             ).astype(BF16)
             staged_l[k] = dot(spl[...], grad_l, 0, 0).astype(BF16)
             rest = p.ra - p.half_a
-            slot = lambda d, y, z: (high if d else low).at[k, y, z]
+            slot = lambda d, y, z: high.at[y, at_k, z] if d else low.at[at_k, y, z]
             slices = [(0, p.ra, 0, p.half_a, 0)]
             if rest:
                 slices.append((1, p.ra, p.half_a, rest, 0))
@@ -664,7 +745,7 @@
                     at = ((r // n_t) ^ my_dp) * n_t + ((r % n_t) ^ my_t)
                     pltpu.make_async_copy(
                         bin_rows.at[pl.ds(pl.multiple_of(at * p.per, 16), p.per)],
-                        out_b.at[c, x, y, z],
+                        out_b.at[c, y, x, z],
                         sem_bin,
                     ).start()
             wait_for(bin_rows, sem_bin)
@@ -675,14 +756,20 @@
         wait_for(staged_l, sem_out.at[1])
 
     half_b = p.ra + p.rl - p.half_a
-    outs = [
-        shape((nb, 2, p.far, p.half_a, p.cols), BF16),
-        shape((nb, 2, p.far, half_b, p.cols), BF16),
+    slots_out = []
+    for c in range(n_core):
+        held = sum(1 for d, _ in xs if d == c)
+        slots_out += [
+            shape((held, 2, p.far, p.half_a, p.cols), BF16),
+            shape((2, held, p.far, half_b, p.cols), BF16),
+        ]
+    outs = slots_out + [
         shape((nb, 8, 3 * p.ct), F32),
         shape((nb, 8, 3 * p.cl), F32),
     ]
-    args = [me2, w_all, w_lay, qkv, ctx, lse, x_low, lay_low, ints, ints_t, da_t, da_l, gfl, spread_t, spread_l]
-    args += list(prev)
+    args = [me2, x_low, lay_low, ints, ints_t, da_t, da_l, spread_t, spread_l]
+    specs = [SM] + [VM] * 8 + ([ANY] + [VM] * 5) * n_core + [VM] * n_prev
+    args += [member for core in cores for member in core] + list(prev)
     if last:
         bins = p.per * p.total
         slots = (bins,) if p.per % 16 else (2, 2, 2, p.far, p.per)
@@ -705,8 +792,7 @@
         pltpu.SemaphoreType.DMA((2,)),
         pltpu.SemaphoreType.DMA,
     ]
-    specs = [SM, ANY] + [VM] * (len(args) - 2)
-    out_specs = [ANY, ANY] + [VM] * (len(outs) - 3) + [ANY if last else VM]
+    out_specs = [ANY] * (2 * n_core) + [VM] * 3 + [ANY if last else VM]
     return kernel_call(body, outs, specs, out_specs, scratch, args)
 
 
@@ -950,101 +1036,88 @@
     flow5, fhigh3 = send(flow4, 1), send(fhigh2, 1)
     cots = page_of(packed_cot)
     (f_all0, g_t0, gp_t0, g_l0, gp_l0, acc_t, acc_l) = feed_forward(
-        p, me2, 0, [flow0, flow4, fhigh0, fhigh2], w_lay0, h_t, h_l, bins_in[0], bins_in[1], spread_t, ()
+        p, me2, [flow0, flow4, fhigh0, fhigh2], w_lay0, h_t, h_l, bins_in[0], bins_in[1], spread_t
     )
     acc_t, acc_l, f_all0, flow5, fhigh3, flow1, fhigh1, cots = tie(
         acc_t, acc_l, f_all0, flow5, fhigh3, flow1, fhigh1, cots
     )
-    (f_all1, g_t1, gp_t1, g_l1, gp_l1, out_rows, dr_t, dr_l, df_t, df_l, gv2t, gv2l, _) = feed_forward(
-        p, me2, 1, [flow1, flow5, fhigh1, fhigh3], w_lay1, h_t, h_l, bins_in[0], bins_in[1], spread_t,
+    (gf_low1, gf_high1, gfl1, dbt1, dbl1, out_rows, dr_t, dr_l, df_t, df_l, gv2t, gv2l, acc_t, acc_l) = feed_middle(
+        p, me2, [flow1, flow5, fhigh1, fhigh3], w_lay1, h_t, h_l, bins_in[0], bins_in[1], spread_t,
         (acc_t, acc_l, n1t, n1l, *cots, vecs[0], vecs[1]),
     )
     rows_out = send_rows(out_rows)
-    (gf_low1, gf_high1, gfl1, dbt1, dbl1, acc_t, acc_l) = feed_backward(
-        p, me2, f_all1, w_lay1, h_t, h_l, df_t, df_l, g_t1, gp_t1, g_l1, gp_l1, spread_t, None, False
-    )
-    rows_out, gf_low1, gf_high1, gfl1, dbt1, dbl1, acc_t, acc_l = tie(
-        rows_out, gf_low1, gf_high1, gfl1, dbt1, dbl1, acc_t, acc_l
-    )
     got = [send(gf_low1, 1), send(gf_high1, 1)]
     (gf_low0, gf_high0, gfl0, dbt0, dbl0, dr1t, dr1l, da_t, da_l, gv1t, gv1l) = feed_backward(
         p, me2, f_all0, w_lay0, h_t, h_l, df_t, df_l, g_t0, gp_t0, g_l0, gp_l0, spread_t,
-        (acc_t, acc_l, dr_t, dr_l, n1t, i1t, n1l, i1l, vecs[0], vecs[1]), True
-    )
-    got, gf_low0, gf_high0, gfl0, dbt0, dbl0, dr1t, dr1l, da_t, da_l, gv1t, gv1l = tie(
-        got, gf_low0, gf_high0, gfl0, dbt0, dbl0, dr1t, dr1l, da_t, da_l, gv1t, gv1l
+        (acc_t, acc_l, dr_t, dr_l, n1t, i1t, n1l, i1l, vecs[0], vecs[1])
+    )
+    got, rows_out, gf_low0, gf_high0, gfl0, dbt0, dbl0, dr1t, dr1l, da_t, da_l, gv1t, gv1l = tie(
+        got, rows_out, gf_low0, gf_high0, gfl0, dbt0, dbl0, dr1t, dr1l, da_t, da_l, gv1t, gv1l
     )
     next_f, keep_f = reduce_second((gf_low0, gf_high0), got)
-    da_t = after(da_t, next_f, keep_f)
+    da_t = after(da_t, next_f)
     got_f = [send(next_f[0], 2), send(next_f[1], 4)]
-    att_args = (x_low, lay_low, ints, ints_t, da_t, da_l)
-    (ga_low1, ga_high1, gb_t1, gb_l1, acc_t, acc_l) = attend_backward(
-        p, me2, (0, 1), w_all1, w_lay1, qkv1, ctx1, lse1, *att_args, gfl1, spread_t, spread_l, (), False
-    )
-    got_f, ga_low1, ga_high1, gb_t1, gb_l1, acc_t, acc_l = tie(
-        got_f, ga_low1, ga_high1, gb_t1, gb_l1, acc_t, acc_l
+    att_args = (x_low, lay_low, ints, ints_t, da_t, da_l, spread_t, spread_l)
+    cores = ((w_all0, w_lay0, qkv0, ctx0, lse0, gfl0), (w_all1, w_lay1, qkv1, ctx1, lse1, gfl1))
+    (low_x1, high_x1, ga_low1, ga_high1, gb_t1, gb_l1, acc_t, acc_l) = attend_backward(
+        p, me2, ((1, 0), (1, 1), (0, 1)), cores, *att_args, (), False
+    )
+    got_f, low_x1, high_x1, ga_low1, ga_high1, gb_t1, gb_l1, acc_t, acc_l = tie(
+        got_f, low_x1, high_x1, ga_low1, ga_high1, gb_t1, gb_l1, acc_t, acc_l
     )
     next_f, keep_f = reduce_second(keep_f, got_f)
-    acc_t = after(acc_t, next_f, keep_f)
+    acc_t = after(acc_t, next_f)
     got = [send(ga_low1, 1), send(ga_high1, 1)]
     got_f = [send(next_f[0], 4), send(next_f[1], 2)]
-    core_args = (w_all0, w_lay0, qkv0, ctx0, lse0, *att_args, gfl0, spread_t, spread_l)
-    (low_x1, high_x1, gb_t02, gb_l02, acc_t, acc_l) = attend_backward(
-        p, me2, (1,), *core_args, (acc_t, acc_l), False
-    )
-    got, got_f, low_x1, high_x1, gb_t02, gb_l02, acc_t, acc_l = tie(
-        got, got_f, low_x1, high_x1, gb_t02, gb_l02, acc_t, acc_l
-    )
-    low_x1 = add_low(low_x1[0], got[0][1])
-    high_x1 = add_low(high_x1[0], got[1][1])
-    line_f = reduce_line_parts(keep_f, got_f)
-    acc_t = after(acc_t, low_x1, high_x1, line_f)
-    got_low = send(low_x1, 2)
-    got_high1 = send(high_x1[1], 4)
-    early = (p.far + 2) // 2
-    line_f, late_f = send_line(line_f[:early], total), line_f[early:]
     (low_x0, high_x0, gb_t00, gb_l00, grad_rows, table_grad) = attend_backward(
-        p, me2, (0,), *core_args, (acc_t, acc_l, dr1t, dr1l), True
-    )
-    low_x0, high_x0, gb_t00, gb_l00, grad_rows, table_grad = after(
-        (low_x0, high_x0, gb_t00, gb_l00, grad_rows, table_grad), got_high1, got_low, line_f
-    )
-    line_f = line_f + [send(late_f[z], 8 * (early + z)) for z in range(len(late_f))]
+        p, me2, ((0, 0),), cores[:1], *att_args, (acc_t, acc_l, dr1t, dr1l), True
+    )
+    got, got_f, low_x0, high_x0, gb_t00, gb_l00, grad_rows, table_grad = tie(
+        got, got_f, low_x0, high_x0, gb_t00, gb_l00, grad_rows, table_grad
+    )
     if p.per % 16:
         table_grad = relative(table_grad.reshape(total, p.per, wl), me)
-        table_grad = table_grad.reshape(p.far, 2, 2, 2, p.per, wl).transpose(3, 2, 1, 0, 4, 5)
+        table_grad = table_grad.reshape(p.far, 2, 2, 2, p.per, wl).transpose(3, 1, 2, 0, 4, 5)
     table_got = send(table_grad[1], 1)
-    table_sum = add_low(table_grad[0], table_got)
+    low_x1 = add_low(low_x1[0], got[0][1])
+    got_low = send(low_x1, 2)
     rest = p.ra - p.half_a
     spare = high_x0.shape[-2] - rest - p.per
-
-    def placed(part):
-        edges = ((0, 0),) * (part.ndim - 2) + ((rest, spare), (lay_cols, p.cols - lay_cols - wl))
-        return jnp.pad(part, edges).astype(F32)
-
-    high_x0 = to_low(high_x0[0].astype(F32) + got[1][0].astype(F32) + placed(table_sum[0]))
-    got_high0 = send(high_x0[1], 4)
-    got_table = send(table_sum[1, 1], 4)
-    low_x0, got_low = after((low_x0, got_low), high_x0)
+    edges = ((0, 0), (0, 0), (0, 0), (rest, spare), (lay_cols, p.cols - lay_cols - wl))
+    table_sum = jnp.pad(add_low(table_grad[0], after(table_got, low_x1)), edges)
+    both = [jnp.concatenate([high_x0[y], high_x1[y]]) for y in range(2)]
+    next_high = to_low(both[1].astype(F32) + got[1][1].astype(F32) + table_sum[1].astype(F32))
+    got_high = send(next_high, 4)
+    line_f = send_line(reduce_line_parts(keep_f, after(got_f, next_high)), total)
     low = to_low(low_x0[0].astype(F32) + got[0][0].astype(F32) + got_low.astype(F32))
     got_low = send(low[1], 4)
-    table_x1 = add_low(table_sum[1, 0], got_table)
-    high_1 = to_low(high_x1[0].astype(F32) + got_high1.astype(F32) + placed(table_x1))
-    got_high = send(high_1, 2)
-    pieces = (gb_t1, gb_l1, gb_t02, gb_l02, gb_t00, gb_l00, dbt0, dbt1, dbl0, dbl1, gv1t, gv1l, gv2t, gv2l)
-    (gb_t1, gb_l1, gb_t02, gb_l02, gb_t00, gb_l00, dbt0, dbt1, dbl0, dbl1, gv1t, gv1l, gv2t, gv2l) = after(
-        pieces, high_1, low
-    )
-    gb_t0 = jnp.concatenate([gb_t00, gb_t02])
-    gb_l0 = jnp.concatenate([gb_l00, gb_l02])
-    feed_sum = add_line(after(line_f, high_1, low))
-    high_0 = add_low(high_x0[0], got_high0)
-    line_a = send_line(reduce_line_parts((low[0], high_0), (got_low, got_high)), total)
-    got_a = (got_low, got_high)
-    feed_sum = after(feed_sum, got_a)
-    attend_sum = add_line(line_a)
-    rows_grad = send_rows(after(grad_rows, got_a))
-    rows_out = after(rows_out, got_a)
+    high = to_low(
+        both[0].astype(F32)
+        + got[1][0].astype(F32)
+        + table_sum[0].astype(F32)
+        + got_high.astype(F32)
+    )
+    got_high = send(high[1], 2)
+    pieces = (gb_t1, gb_l1, gb_t00, gb_l00, dbt0, dbt1, dbl0, dbl1, gv1t, gv1l, gv2t, gv2l)
+    (gb_t1, gb_l1, gb_t00, gb_l00, dbt0, dbt1, dbl0, dbl1, gv1t, gv1l, gv2t, gv2l) = after(
+        pieces, next_high
+    )
+    gb_t0 = jnp.concatenate([gb_t00, gb_t1[2:]])
+    gb_l0 = jnp.concatenate([gb_l00, gb_l1[2:]])
+    feed_sum = add_line(after(line_f, low, high))
+    line_a = reduce_line_parts((low[0], high[0]), (got_low, got_high))
+    rows_out, grad_rows = after((rows_out, grad_rows), line_a)
+    line_a = send_line(line_a, total)
+    rows_grad = send_rows(grad_rows)
+    feed_sum = after(feed_sum, line_a[1])
+    rows_out, rows_grad = pages_of(rows_out), pages_of(rows_grad)
+    row_outputs = (
+        rows_out[:, :, :wt],
+        rows_out[:, :, wt:].reshape(pages, quarter * wl),
+        rows_grad[:, :, :wt].astype(F32),
+        rows_grad[:, :, wt:].astype(F32).reshape(pages, quarter * wl),
+    )
+    attend_sum = add_line(after(line_a, row_outputs[:2]))
 
     def by_block(odd, even):
         both = jnp.stack([even[0], odd[0], even[1], odd[1]]).reshape(n_t, -1)
@@ -1112,12 +1185,8 @@
     )
     updated = update_all(factor, matrices, flat, grads)
     updated[12:] = [v.reshape(-1) for v in updated[12:]]
-    rows_out, rows_grad = pages_of(rows_out), pages_of(rows_grad)
     return (
-        rows_out[:, :, :wt],
-        rows_out[:, :, wt:].reshape(pages, quarter * wl),
-        rows_grad[:, :, :wt].astype(F32),
-        rows_grad[:, :, wt:].astype(F32).reshape(pages, quarter * wl),
+        *row_outputs,
         *updated,
         clip_norm,
     )

time: 355 us -> 333 us (0.938)
  Pallas kernels: 131 us -> 119 us
  starting transfers between devices: 58.9 us -> 54 us
    pallas_call x10 -> x8, Pallas kernels: 131 us -> 119 us  [kernel_call(): pl.pallas_call(body, out_shape=outs, in_specs=in_specs, out_specs=out_spe...]
    ppermute x64 -> x62, starting transfers between devices: 58.9 us -> 54 us  [xor_send(): return lax.ppermute(values, AXES, [(i, i ^ distance) for i in range(total)])]
    convert_element_type x20 -> x17, other arithmetic: 22.8 us -> 20.8 us  [to_low(): return values.astype(BF16)]
    ppermute x64 -> x62, waiting for transfers between devices: 71.7 us -> 71.2 us  [xor_send(): return lax.ppermute(values, AXES, [(i, i ^ distance) for i in range(total)])]
  transfers between devices with their start and end apart: 64 -> 62, of which waited for: 21 -> 21; matrix products, arithmetic and copies ran while one was open for 16% -> 17% of each run, Pallas kernels for 32% -> 29%
where the time goes in v4:
time: 333 us; the launch traced here: 327 us
  Pallas kernels  119 us (36%)
  waiting for transfers between devices  71.2 us (21%)
  starting transfers between devices  54 us (16%)
  other arithmetic  43.8 us (13%)
  local copies, waits for them, and re-layouts  32.8 us (10%)
  between operations  6.15 us (2%)
    pallas_call x8, Pallas kernels, kernel_call(): pl.pallas_call(body, out_shape=outs, in_specs=in_specs, out_specs=out_spe...  119 us
    ppermute x62, waiting for transfers between devices, xor_send(): return lax.ppermute(values, AXES, [(i, i ^ distance) for i in range(total)])  71.2 us
    ppermute x62, starting transfers between devices, xor_send(): return lax.ppermute(values, AXES, [(i, i ^ distance) for i in range(total)])  54 us
    convert_element_type x17, other arithmetic, to_low(): return values.astype(BF16)  20.8 us
  transfers between devices with their start and end apart: 62, of which 21 were waited for; matrix products, arithmetic and copies ran while one was open for 17% of the time, Pallas kernels for 29%

profile of v4, /device:TPU:0, one launch (start us, length us, event | category | flops | bytes accessed | tf_op | source)
XLA Modules:
  0.0 327.3 jit_solution(5246806116199146073)
XLA Ops:
  4.0 3.1 collective-permute-start
  7.1 2.6 collective-permute-start.1
  15.4 8.8 %collective-permute-done.1 = bf16[128,768]{1,0:T(8,128)(2,1)S(1)} collective-permute-done((bf16[128,768]{1,0:T(8,128)(2,1)S(1)}, bf16[128,768]{1,0:T(8,128)(2,1)S(1)}, u32[]{:S(2)}, u32[]{:S(2)}) %collective-permute-start.1) | collective-permute-done | bytes 196640 | tf_op jit(solution)/shard_map/ppermute | solution.py:34
  31.8 2.4 collective-permute-start.15
  34.2 2.7 collective-permute-done.7
  48.1 11.8 %collective-permute-done.15 = bf16[2,192,768]{2,1,0:T(8,128)(2,1)} collective-permute-done((bf16[2,192,768]{2,1,0:T(8,128)(2,1)}, bf16[2,192,768]{2,1,0:T(8,128)(2,1)}, u32[]{:S(2)}, u32[]{:S(2)}) %collective-permute-start.15) | collective-permute-done | bytes 589856 | tf_op jit(solution)/shard_map/ppermute | solution.py:34
  63.9 13.7 %shard_map.407 = (bf16[2,768,768]{2,1,0:T(8,128)(2,1)}, bf16[2,192,768]{2,1,0:T(8,128)(2,1)}, bf16[2,9,80,512]{3,2,1,0:T(8,128)(2,1)}, bf16[2,3,80,512]{3,2,1,0:...) custom-call(s32[2]{0:T(128)} %pad_add_fusion.refs_0_, ...), custom_call_target="tpu_custom_call" | custom-call | flops 10000000000 | bytes 1048576 | tf_op jit(solution)/shard_map/pallas_call | solution.py:119
  86.1 13.6 %shard_map.408 = (bf16[2,768,768]{2,1,0:T(8,128)(2,1)}, bf16[2,192,768]{2,1,0:T(8,128)(2,1)}, bf16[2,9,80,512]{3,2,1,0:T(8,128)(2,1)}, bf16[2,3,80,512]{3,2,1,0:...) custom-call(s32[2]{0:T(128)} %pad_add_fusion.refs_0_, ...), custom_call_target="tpu_custom_call" | custom-call | flops 10000000000 | bytes 1048576 | tf_op jit(solution)/shard_map/pallas_call | solution.py:119
  99.7 8.5 %collective-permute-done.19.refs_10_ = bf16[2,4,96,768]{3,2,1,0:T(8,128)(2,1)} collective-permute-done((bf16[2,4,96,768]{3,2,1,0:T(8,128)(2,1)S(1)}, bf16[2,4,96,768]{3,2,1,0:T(8,128)(2,1)}, u32[]{:S(2)}, u32[]{:S(2)}) %collective-permute-start.19) | collective-permute-done | bytes 1179680 | tf_op jit(solution)/shard_map/ppermute | solution.py:34
  114.1 10.3 %shard_map.409 = (bf16[2,2,768,768]{3,2,1,0:T(8,128)(2,1)}, bf16[2,512,768]{2,1,0:T(8,128)(2,1)}, bf16[2,512,768]{2,1,0:T(8,128)(2,1)}, bf16[2,512,192]{2,1,0:T(...) custom-call(s32[2]{0:T(128)} %pad_add_fusion.refs_0_, ...), custom_call_target="tpu_custom_call" | custom-call | flops 10000000000 | bytes 1048576 | tf_op jit(solution)/shard_map/pallas_call | solution.py:119
  126.9 19.2 %shard_map.410 = (bf16[2,2,4,96,768]{4,3,2,1,0:T(8,128)(2,1)}, bf16[2,2,4,96,768]{4,3,2,1,0:T(8,128)(2,1)}, bf16[2,192,384]{2,1,0:T(8,128)(2,1)}, f32[2,1,768]{2...) custom-call(s32[2]{0:T(128)} %pad_add_fusion.refs_0_, ...), custom_call_target="tpu_custom_call" | custom-call | flops 10000000000 | bytes 1048576 | tf_op jit(solution)/shard_map/pallas_call | solution.py:119
  150.6 15.6 %shard_map.411 = (bf16[2,2,4,96,768]{4,3,2,1,0:T(8,128)(2,1)}, bf16[2,2,4,96,768]{4,3,2,1,0:T(8,128)(2,1)}, bf16[2,192,384]{2,1,0:T(8,128)(2,1)}, f32[2,1,768]{2...) custom-call(s32[2]{0:T(128)} %pad_add_fusion.refs_0_, ...), custom_call_target="tpu_custom_call" | custom-call | flops 10000000000 | bytes 1048576 | tf_op jit(solution)/shard_map/pallas_call | solution.py:119
  167.8 4.2 %add_convert_fusion = (bf16[1,2,4,96,768]{4,3,2,1,0:T(8,128)(2,1)S(1)}, bf16[2,4,96,768]{3,2,1,0:T(8,128)(2,1)}) fusion(bf16[2,2,4,96,768]{4,3,2,1,0:T(8,128)(2,1)} %collective-permute-done.28, bf16[2,2,4,96,768]{4,3,2,1,0:T(8,128)(2,1)} %get-tuple-element.333), kind=kLoop, calls=%fused_computation | loop fusion | flops 4718592 | bytes 7077888 | tf_op jit(solution)/shard_map/convert_element_type | solution.py:30
  175.6 25.6 %shard_map.412 = (bf16[1,2,4,64,768]{4,3,2,1,0:T(8,128)(2,1)}, bf16[2,1,4,64,768]{4,3,2,1,0:T(8,128)(2,1)}, bf16[2,2,4,64,768]{4,3,2,1,0:T(8,128)(2,1)}, bf16[2,...) custom-call(s32[2]{0:T(128)} %pad_add_fusion.refs_0_, ...), custom_call_target="tpu_custom_call" | custom-call | flops 10000000000 | bytes 1048576 | tf_op jit(solution)/shard_map/pallas_call | solution.py:119
  204.3 2.4 fusion.7
  209.2 14.9 %shard_map.413 = (bf16[1,2,4,64,768]{4,3,2,1,0:T(8,128)(2,1)}, bf16[2,1,4,64,768]{4,3,2,1,0:T(8,128)(2,1)}, f32[1,8,576]{2,1,0:T(8,128)}, f32[1,8,144]{2,1,0:T(8...) custom-call(s32[2]{0:T(128)} %pad_add_fusion.refs_0_, ...), custom_call_target="tpu_custom_call" | custom-call | flops 10000000000 | bytes 1048576 | tf_op jit(solution)/shard_map/pallas_call | solution.py:119
  235.5 2.9 collective-permute-start.48
  249.4 4.5 %collective-permute-done.41 = bf16[2,4,64,768]{3,2,1,0:T(8,128)(2,1)} collective-permute-done((bf16[2,4,64,768]{3,2,1,0:T(8,128)(2,1)}, bf16[2,4,64,768]{3,2,1,0:T(8,128)(2,1)}, u32[]{:S(2)}, u32[]{:S(2)}) %collective-permute-start.41) | collective-permute-done | bytes 786464 | tf_op jit(solution)/shard_map/ppermute | solution.py:34
  256.2 6.9 %collective-permute-done.47 = bf16[192,768]{1,0:T(8,128)(2,1)} collective-permute-done((bf16[192,768]{1,0:T(8,128)(2,1)}, bf16[192,768]{1,0:T(8,128)(2,1)}, u32[]{:S(2)}, u32[]{:S(2)}) %collective-permute-start.47) | collective-permute-done | bytes 294944 | tf_op jit(solution)/shard_map/ppermute | solution.py:34
  269.4 3.7 %collective-permute-start.51 = (bf16[128,768]{1,0:T(8,128)(2,1)}, bf16[128,768]{1,0:T(8,128)(2,1)}, u32[]{:S(2)}, u32[]{:S(2)}) collective-permute-start(bf16[128,768]{1,0:T(8,128)(2,1)} %pad_maximum_fusion.20), channel_id=1, source_target_pairs={{0,24},{1,25},{2,26},{3,27},{4,28},{5,29},{6,30},{7,31},{8,16},{9,... | collective-permute-start | bytes 589832 | tf_op jit(solution)/shard_map/ppermute | solution.py:34
  276.4 3.0 collective-permute-done.51
  279.4 7.8 %collective-permute-done.50 = bf16[128,768]{1,0:T(8,128)(2,1)} collective-permute-done((bf16[128,768]{1,0:T(8,128)(2,1)}, bf16[128,768]{1,0:T(8,128)(2,1)}, u32[]{:S(2)}, u32[]{:S(2)}) %collective-permute-start.50) | collective-permute-done | bytes 196640 | tf_op jit(solution)/shard_map/ppermute | solution.py:34
  291.5 2.9 collective-permute-start.57
  319.4 6.6 %shard_map.414 = (f32[96,4,192]{2,1,0:T(4,128)}, f32[96,4,192]{2,1,0:T(4,128)}, f32[96,4,192]{2,1,0:T(4,128)}, f32[96,2,768]{2,1,0:T(2,128)}, f32[96,2,768]{2,1,...) custom-call(f32[1,1]{1,0:T(1,128)} %bitcast.130.refs_0_, ...), custom_call_target="tpu_custom_call" | custom-call | flops 10000000000 | bytes 1048576 | tf_op jit(solution)/shard_map/pallas_call | solution.py:119
  (395 shorter events, 123.5 us)
Async XLA Ops:
  31.8 28.1 %collective-permute-start.15 = (bf16[2,192,768]{2,1,0:T(8,128)(2,1)}, bf16[2,192,768]{2,1,0:T(8,128)(2,1)}, u32[]{:S(2)}, u32[]{:S(2)}) collective-permute-start(bf16[2,192,768]{2,1,0:T(8,128)(2,1)} %pad_maximum_fusion.5), channel_id=1, source_target_pairs={{0,16},{1,17},{2,18},{3,19},{4,20},{5,21},{6,22},{7,23},{8,24},{9,... | collective-permute-start | bytes 1769480 | tf_op jit(solution)/shard_map/ppermute | solution.py:34
  38.1 23.2 %collective-permute-start.9 = (bf16[2,4,64,768]{3,2,1,0:T(8,128)(2,1)S(1)}, bf16[2,4,64,768]{3,2,1,0:T(8,128)(2,1)}, u32[]{:S(2)}, u32[]{:S(2)}) collective-permute-start(bf16[2,4,64,768]{3,2,1,0:T(8,128)(2,1)S(1)} %pad_maximum_fusion.4.refs_14_), channel_id=1, source_target_pairs={{0,2},{1,3},{2,0},{3,1},{4,6},{5,7},{6,4},{7,5},{8,10},{9,11},{10,... | collective-permute-start | bytes 2359304 | tf_op jit(solution)/shard_map/ppermute | solution.py:34
  41.8 19.5 %collective-permute-start.8 = (bf16[2,4,64,768]{3,2,1,0:T(8,128)(2,1)}, bf16[2,4,64,768]{3,2,1,0:T(8,128)(2,1)}, u32[]{:S(2)}, u32[]{:S(2)}) collective-permute-start(bf16[2,4,64,768]{3,2,1,0:T(8,128)(2,1)} %pad_maximum_fusion.3.refs_12_), channel_id=1, source_target_pairs={{0,4},{1,5},{2,6},{3,7},{4,0},{5,1},{6,2},{7,3},{8,12},{9,13},{10,... | collective-permute-start | bytes 2359304 | tf_op jit(solution)/shard_map/ppermute | solution.py:34
  43.5 19.2 %collective-permute-start.13 = (bf16[2,4,64,768]{3,2,1,0:T(8,128)(2,1)S(1)}, bf16[2,4,64,768]{3,2,1,0:T(8,128)(2,1)}, u32[]{:S(2)}, u32[]{:S(2)}) collective-permute-start(bf16[2,4,64,768]{3,2,1,0:T(8,128)(2,1)S(1)} %pad_maximum_fusion.4.refs_14_), channel_id=1, source_target_pairs={{0,1},{1,0},{2,3},{3,2},{4,5},{5,4},{6,7},{7,6},{8,9},{9,8},{10,11... | collective-permute-start | bytes 2359304 | tf_op jit(solution)/shard_map/ppermute | solution.py:34
  43.5 34.0 %collective-permute-start.12 = (bf16[2,4,64,768]{3,2,1,0:T(8,128)(2,1)}, bf16[2,4,64,768]{3,2,1,0:T(8,128)(2,1)}, u32[]{:S(2)}, u32[]{:S(2)}) collective-permute-start(bf16[2,4,64,768]{3,2,1,0:T(8,128)(2,1)} %pad_maximum_fusion.3.refs_12_), channel_id=1, source_target_pairs={{0,1},{1,0},{2,3},{3,2},{4,5},{5,4},{6,7},{7,6},{8,9},{9,8},{10,11... | collective-permute-start | bytes 2359304 | tf_op jit(solution)/shard_map/ppermute | solution.py:34
  80.2 28.0 %collective-permute-start.19 = (bf16[2,4,96,768]{3,2,1,0:T(8,128)(2,1)S(1)}, bf16[2,4,96,768]{3,2,1,0:T(8,128)(2,1)}, u32[]{:S(2)}, u32[]{:S(2)}) collective-permute-start(bf16[2,4,96,768]{3,2,1,0:T(8,128)(2,1)S(1)} %pad_maximum_fusion.1.refs_9_), channel_id=1, source_target_pairs={{0,2},{1,3},{2,0},{3,1},{4,6},{5,7},{6,4},{7,5},{8,10},{9,11},{10,... | collective-permute-start | bytes 3538952 | tf_op jit(solution)/shard_map/ppermute | solution.py:34
  81.9 27.8 %collective-permute-start.18 = (bf16[2,4,96,768]{3,2,1,0:T(8,128)(2,1)S(1)}, bf16[2,4,96,768]{3,2,1,0:T(8,128)(2,1)}, u32[]{:S(2)}, u32[]{:S(2)}) collective-permute-start(bf16[2,4,96,768]{3,2,1,0:T(8,128)(2,1)S(1)} %pad_maximum_fusion.refs_7_), channel_id=1, source_target_pairs={{0,4},{1,5},{2,6},{3,7},{4,0},{5,1},{6,2},{7,3},{8,12},{9,13},{10,... | collective-permute-start | bytes 3538952 | tf_op jit(solution)/shard_map/ppermute | solution.py:34
  85.5 26.7 %collective-permute-start.23 = (bf16[2,4,96,768]{3,2,1,0:T(8,128)(2,1)S(1)}, bf16[2,4,96,768]{3,2,1,0:T(8,128)(2,1)}, u32[]{:S(2)}, u32[]{:S(2)}) collective-permute-start(bf16[2,4,96,768]{3,2,1,0:T(8,128)(2,1)S(1)} %pad_maximum_fusion.1.refs_9_), channel_id=1, source_target_pairs={{0,1},{1,0},{2,3},{3,2},{4,5},{5,4},{6,7},{7,6},{8,9},{9,8},{10,11... | collective-permute-start | bytes 3538952 | tf_op jit(solution)/shard_map/ppermute | solution.py:34
  85.6 27.2 %collective-permute-start.22 = (bf16[2,4,96,768]{3,2,1,0:T(8,128)(2,1)S(1)}, bf16[2,4,96,768]{3,2,1,0:T(8,128)(2,1)}, u32[]{:S(2)}, u32[]{:S(2)}) collective-permute-start(bf16[2,4,96,768]{3,2,1,0:T(8,128)(2,1)S(1)} %pad_maximum_fusion.refs_7_), channel_id=1, source_target_pairs={{0,1},{1,0},{2,3},{3,2},{4,5},{5,4},{6,7},{7,6},{8,9},{9,8},{10,11... | collective-permute-start | bytes 3538952 | tf_op jit(solution)/shard_map/ppermute | solution.py:34
  146.2 20.0 %collective-permute-start.27 = (bf16[2,2,4,96,768]{4,3,2,1,0:T(8,128)(2,1)}, bf16[2,2,4,96,768]{4,3,2,1,0:T(8,128)(2,1)S(1)}, u32[]{:S(2)}, u32[]{:S(2)}) collective-permute-start(bf16[2,2,4,96,768]{4,3,2,1,0:T(8,128)(2,1)} %get-tuple-element.300), channel_id=1, source_target_pairs={{0,1},{1,0},{2,3},{3,2},{4,5},{5,4},{6,7},{7,6},{8,9},{9,8},{10,11... | collective-permute-start | bytes 7077896 | tf_op jit(solution)/shard_map/ppermute | solution.py:34
  146.4 19.8 %collective-permute-start.28 = (bf16[2,2,4,96,768]{4,3,2,1,0:T(8,128)(2,1)}, bf16[2,2,4,96,768]{4,3,2,1,0:T(8,128)(2,1)}, u32[]{:S(2)}, u32[]{:S(2)}) collective-permute-start(bf16[2,2,4,96,768]{4,3,2,1,0:T(8,128)(2,1)} %get-tuple-element.301), channel_id=1, source_target_pairs={{0,1},{1,0},{2,3},{3,2},{4,5},{5,4},{6,7},{7,6},{8,9},{9,8},{10,11... | collective-permute-start | bytes 7077896 | tf_op jit(solution)/shard_map/ppermute | solution.py:34
  172.0 29.2 %collective-permute-start.33 = (bf16[2,4,96,768]{3,2,1,0:T(8,128)(2,1)}, bf16[2,4,96,768]{3,2,1,0:T(8,128)(2,1)}, u32[]{:S(2)}, u32[]{:S(2)}) collective-permute-start(bf16[2,4,96,768]{3,2,1,0:T(8,128)(2,1)} %get-tuple-element.455), channel_id=1, source_target_pairs={{0,4},{1,5},{2,6},{3,7},{4,0},{5,1},{6,2},{7,3},{8,12},{9,13},{10,... | collective-permute-start | bytes 3538952 | tf_op jit(solution)/shard_map/ppermute | solution.py:34
  175.0 28.3 %collective-permute-start.32 = (bf16[2,4,96,768]{3,2,1,0:T(8,128)(2,1)}, bf16[2,4,96,768]{3,2,1,0:T(8,128)(2,1)S(1)}, u32[]{:S(2)}, u32[]{:S(2)}) collective-permute-start(bf16[2,4,96,768]{3,2,1,0:T(8,128)(2,1)} %get-tuple-element.457), channel_id=1, source_target_pairs={{0,2},{1,3},{2,0},{3,1},{4,6},{5,7},{6,4},{7,5},{8,10},{9,11},{10,... | collective-permute-start | bytes 3538952 | tf_op jit(solution)/shard_map/ppermute | solution.py:34
  203.3 20.9 %collective-permute-start.34 = (bf16[2,2,4,64,768]{4,3,2,1,0:T(8,128)(2,1)}, bf16[2,2,4,64,768]{4,3,2,1,0:T(8,128)(2,1)}, u32[]{:S(2)}, u32[]{:S(2)}) collective-permute-start(bf16[2,2,4,64,768]{4,3,2,1,0:T(8,128)(2,1)} %get-tuple-element.356), channel_id=1, source_target_pairs={{0,1},{1,0},{2,3},{3,2},{4,5},{5,4},{6,7},{7,6},{8,9},{9,8},{10,11... | collective-permute-start | bytes 4718600 | tf_op jit(solution)/shard_map/ppermute | solution.py:34
  203.3 20.9 %collective-permute-start.35 = (bf16[2,2,4,64,768]{4,3,2,1,0:T(8,128)(2,1)}, bf16[2,2,4,64,768]{4,3,2,1,0:T(8,128)(2,1)}, u32[]{:S(2)}, u32[]{:S(2)}) collective-permute-start(bf16[2,2,4,64,768]{4,3,2,1,0:T(8,128)(2,1)} %get-tuple-element.357), channel_id=1, source_target_pairs={{0,1},{1,0},{2,3},{3,2},{4,5},{5,4},{6,7},{7,6},{8,9},{9,8},{10,11... | collective-permute-start | bytes 4718600 | tf_op jit(solution)/shard_map/ppermute | solution.py:34
  206.7 17.5 %collective-permute-start.37 = (bf16[4,96,768]{2,1,0:T(8,128)(2,1)}, bf16[4,96,768]{2,1,0:T(8,128)(2,1)S(1)}, u32[]{:S(2)}, u32[]{:S(2)}) collective-permute-start(bf16[4,96,768]{2,1,0:T(8,128)(2,1)} %get-tuple-element.461), channel_id=1, source_target_pairs={{0,2},{1,3},{2,0},{3,1},{4,6},{5,7},{6,4},{7,5},{8,10},{9,11},{10,... | collective-permute-start | bytes 1769480 | tf_op jit(solution)/shard_map/ppermute | solution.py:34
  227.6 18.7 %collective-permute-start.38 = (bf16[2,4,64,768]{3,2,1,0:T(8,128)(2,1)}, bf16[2,4,64,768]{3,2,1,0:T(8,128)(2,1)}, u32[]{:S(2)}, u32[]{:S(2)}) collective-permute-start(bf16[2,4,64,768]{3,2,1,0:T(8,128)(2,1)} %fusion.12), channel_id=1, source_target_pairs={{0,2},{1,3},{2,0},{3,1},{4,6},{5,7},{6,4},{7,5},{8,10},{9,11},{10,... | collective-permute-start | bytes 2359304 | tf_op jit(solution)/shard_map/ppermute | solution.py:34
  233.2 20.7 %collective-permute-start.41 = (bf16[2,4,64,768]{3,2,1,0:T(8,128)(2,1)}, bf16[2,4,64,768]{3,2,1,0:T(8,128)(2,1)}, u32[]{:S(2)}, u32[]{:S(2)}) collective-permute-start(bf16[2,4,64,768]{3,2,1,0:T(8,128)(2,1)} %fusion.1), channel_id=1, source_target_pairs={{0,4},{1,5},{2,6},{3,7},{4,0},{5,1},{6,2},{7,3},{8,12},{9,13},{10,... | collective-permute-start | bytes 2359304 | tf_op jit(solution)/shard_map/ppermute | solution.py:34
  235.5 20.7 %collective-permute-start.48 = (bf16[192,768]{1,0:T(8,128)(2,1)}, bf16[192,768]{1,0:T(8,128)(2,1)}, u32[]{:S(2)}, u32[]{:S(2)}) collective-permute-start(bf16[192,768]{1,0:T(8,128)(2,1)} %pad_maximum_fusion.15), channel_id=1, source_target_pairs={{0,24},{1,25},{2,26},{3,27},{4,28},{5,29},{6,30},{7,31},{8,16},{9,... | collective-permute-start | bytes 884744 | tf_op jit(solution)/shard_map/ppermute | solution.py:34
  239.1 23.9 %collective-permute-start.47 = (bf16[192,768]{1,0:T(8,128)(2,1)}, bf16[192,768]{1,0:T(8,128)(2,1)}, u32[]{:S(2)}, u32[]{:S(2)}) collective-permute-start(bf16[192,768]{1,0:T(8,128)(2,1)} %pad_maximum_fusion.14), channel_id=1, source_target_pairs={{0,16},{1,17},{2,18},{3,19},{4,20},{5,21},{6,22},{7,23},{8,24},{9,... | collective-permute-start | bytes 884744 | tf_op jit(solution)/shard_map/ppermute | solution.py:34
  239.9 23.2 %collective-permute-start.46 = (bf16[192,768]{1,0:T(8,128)(2,1)}, bf16[192,768]{1,0:T(8,128)(2,1)}, u32[]{:S(2)}, u32[]{:S(2)}) collective-permute-start(bf16[192,768]{1,0:T(8,128)(2,1)} %pad_maximum_fusion.13), channel_id=1, source_target_pairs={{0,8},{1,9},{2,10},{3,11},{4,12},{5,13},{6,14},{7,15},{8,0},{9,1},... | collective-permute-start | bytes 884744 | tf_op jit(solution)/shard_map/ppermute | solution.py:34
  275.7 25.5 %collective-permute-start.43 = (bf16[128,960]{1,0:T(8,128)(2,1)}, bf16[128,960]{1,0:T(8,128)(2,1)S(1)}, u32[]{:S(2)}, u32[]{:S(2)}) collective-permute-start(bf16[128,960]{1,0:T(8,128)(2,1)} %get-tuple-element.480), channel_id=1, source_target_pairs={{0,1},{1,0},{2,3},{3,2},{4,5},{5,4},{6,7},{7,6},{8,9},{9,8},{10,11... | collective-permute-start | bytes 737288 | tf_op jit(solution)/shard_map/ppermute | solution.py:34
  275.7 25.6 %collective-permute-start.44 = (bf16[128,960]{1,0:T(8,128)(2,1)}, bf16[128,960]{1,0:T(8,128)(2,1)S(1)}, u32[]{:S(2)}, u32[]{:S(2)}) collective-permute-start(bf16[128,960]{1,0:T(8,128)(2,1)} %get-tuple-element.479), channel_id=1, source_target_pairs={{0,2},{1,3},{2,0},{3,1},{4,6},{5,7},{6,4},{7,5},{8,10},{9,11},{10,... | collective-permute-start | bytes 737288 | tf_op jit(solution)/shard_map/ppermute | solution.py:34
  279.4 21.9 %collective-permute-start.45 = (bf16[128,960]{1,0:T(8,128)(2,1)}, bf16[128,960]{1,0:T(8,128)(2,1)}, u32[]{:S(2)}, u32[]{:S(2)}) collective-permute-start(bf16[128,960]{1,0:T(8,128)(2,1)} %get-tuple-element.478), channel_id=1, source_target_pairs={{0,3},{1,2},{2,1},{3,0},{4,7},{5,6},{6,5},{7,4},{8,11},{9,10},{10,... | collective-permute-start | bytes 737288 | tf_op jit(solution)/shard_map/ppermute | solution.py:34
  (86 other events, 685.0 us)
